TPU v7x, 256 devices: a whole 4x4x8 slice. The times are simulated.
256 devices in a mesh: task: 8 (over z_hi, core), dp: 32 (over z_lo, y, x).
Axes of the slice: x: 4, y: 4, z: 8 (z_hi: 4, z_lo: 2; z = z_hi * 2 + z_lo), core: 2. Of those that a mesh axis runs over, the one named last changes fastest.
Arguments:
- inputs: bfloat16 [32768, 4096], P('dp'), may hold values from -6 to 6
- cotangent: bfloat16 [8, 32768, 1024], P('task', 'dp'), may hold values from -0.22097087 to 0.22097087
- task_order: int32 [8], replicated, may hold values from 0 to 7, each once
- conflict_flags: int32 [8, 8], replicated, may hold values 0 or 1
Outputs:
- combined: bfloat16 [4096, 1024], P(None, 'task')
Inputs may be any that keep to these rules, and one draw needn't show every extreme that they name: `task_order`: a permutation of the tasks. `conflict_flags`: diagonal entries are ignored.
All inputs are finite; a program needn't handle non-finite values.
Results may differ from a plain program's by a relative error of at most 0.001.
Values may be sent and summed in bfloat16 or wider, within the bound.
No kernel may reach another device: no remote copies, remote signals or barrier semaphores. Data moves between devices by JAX's collectives and lax.ppermute only.
A program may use at most 128 MiB of HBM per device.

v0:
```python
import jax
import jax.numpy as jnp
from jax import lax
from jax.sharding import Mesh
from jax.sharding import PartitionSpec as P

DP = ("dp_0", "dp_1", "dp_2")
TASK = ("task_0", "task_1")
TASK_DP = ("task_0", "task_1", "dp_0", "dp_1", "dp_2")


def one_axis_at_a_time(value, axes):
    for axis in axes:
        value = lax.psum(value, axis)
    return value


def copy_for_each(value, axis):
    copies = jnp.broadcast_to(value, (lax.axis_size(axis), *value.shape))
    return lax.all_to_all(copies, axis, split_axis=0, concat_axis=0, tiled=True)


def joined_along(pieces, dim):
    pieces = jnp.moveaxis(pieces, 0, dim)
    lengths = pieces.shape
    return pieces.reshape(*lengths[:dim], lengths[dim] * lengths[dim + 1], *lengths[dim + 2 :])


def gather_directly(value, axis, dim):
    pieces = copy_for_each(value, axis)
    return joined_along(pieces, dim)


def project_weights(gram_matrix, task_order, conflict_flags):
    count = gram_matrix.shape[0]
    labels = jnp.arange(count, dtype=jnp.int32)
    coefficients = jnp.eye(count, dtype=jnp.float32)
    for position in range(count):
        target = task_order[position]
        pick_column = (labels == target).astype(jnp.float32)
        column = jnp.dot(gram_matrix, pick_column, precision=lax.Precision.HIGHEST)
        inner_dots = jnp.dot(coefficients, column, precision=lax.Precision.HIGHEST)
        own_square = jnp.sum(pick_column * column)
        active = jnp.dot(
            conflict_flags.astype(jnp.float32), pick_column, precision=lax.Precision.HIGHEST
        ) * (1.0 - pick_column)
        removed = jnp.minimum(inner_dots, 0.0) / own_square * active
        coefficients = coefficients - removed[:, None] * pick_column[None, :]
    return jnp.sum(coefficients, axis=0)


def on_device(inputs, cotangent, task_order, conflict_flags):
    task_cot = cotangent[0]
    shard_grad = lax.psum_scatter(
        lax.dot_general(
            inputs, task_cot, (((0,), (0,)), ((), ())), preferred_element_type=jnp.float32
        ),
        DP,
        scatter_dimension=0,
        tiled=True,
    )
    own_grads = lax.all_to_all(shard_grad[None], TASK, split_axis=2, concat_axis=0, tiled=True)
    gram_part = jnp.einsum("tab,sab->ts", own_grads, own_grads, precision=lax.Precision.HIGHEST)
    gram_matrix = one_axis_at_a_time(gram_part, TASK_DP)
    weights = project_weights(gram_matrix, task_order, conflict_flags)
    own_block = jnp.einsum("t,tab->ab", weights, own_grads, precision=lax.Precision.HIGHEST)
    return gather_directly(own_block.astype(jnp.bfloat16), DP, 0)


def solution(mesh):
    split = Mesh(mesh.devices.reshape(4, 2, 2, 4, 4), ("task_0", "task_1", "dp_0", "dp_1", "dp_2"))
    placed = (P(DP, None), P(TASK, DP, None), P(), P())
    return jax.shard_map(
        on_device, mesh=split, in_specs=placed, out_specs=P(None, TASK), check_vma=False
    )
```

profile of v0, /device:TPU:32, one launch (start us, length us, event | category | flops | bytes accessed | tf_op | source)
XLA Modules:
  0.0 337.4 jit_solution(14176817191690984144)
XLA Ops:
  6.5 1.6 copy-done
  8.1 14.5 %fusion = f32[4096,1024]{1,0:T(8,128)} fusion(bf16[1024,4096]{1,0:T(8,128)(2,1)} %param.4, bf16[1,1024,1024]{2,1,0:T(8,128)(2,1)S(1)} %copy-done), kind=kOutput, calls=%fused_computation | convolution fusion | flops 8589934592 | bytes 27262976 | tf_op jit(solution)/shard_map/dot_general | solution.py:55
  22.7 0.6 copy-done.2
  23.3 0.7 fusion.166
  24.0 0.7 fusion.141
  24.7 1.4 fusion.142
  26.1 1.1 fusion.145
  27.2 1.2 fusion.147
  28.5 0.8 fusion.31
  29.3 0.8 fusion.27
  30.1 0.8 fusion.23
  30.9 199.4 %reduce-scatter.2.cloned.1.call-done = f32[128,1024]{1,0:T(8,128)} async-done(((f32[4096,1024]{1,0:T(8,128)}), f32[128,1024]{1,0:T(8,128)}) %reduce-scatter.2.cloned.1.call-update) | async-done | bytes 524304 | tf_op jit(solution)/shard_map/reduce_scatter | solution.py:54
  230.3 1.9 copy.7
  232.3 7.3 %all-to-all-start = ((f32[1,128,1024]{1,0,2:T(1,128)}), f32[1,128,1024]{1,0,2:T(1,128)S(1)}, u32[]{:S(2)}, u32[]{:S(2)}) async-start(f32[1,128,1024]{1,0,2:T(1,128)} %copy.7), calls=%async_computation.1 | async-start | bytes 1048576 | tf_op jit(solution)/shard_map/all_to_all | solution.py:62
  239.5 0.6 fusion.143
  240.2 0.8 fusion.19
  240.9 0.7 fusion.15
  241.6 0.7 fusion.11
  242.3 0.8 fusion.7
  243.1 13.4 %all-to-all-done = f32[1,128,1024]{1,0,2:T(1,128)S(1)} async-done(((f32[1,128,1024]{1,0,2:T(1,128)}), f32[1,128,1024]{1,0,2:T(1,128)S(1)}, u32[]{:S(2)}, u32[]{:S(2)}) %all-to-all-start) | async-done | bytes 524320 | tf_op jit(solution)/shard_map/all_to_all | solution.py:62
  256.5 0.2 copy.9
  256.8 1.2 convolution_bitcast_fusion
  258.0 10.1 %psum.35 = f32[8,8]{1,0:T(8,128)S(1)} all-reduce(f32[8,8]{1,0:T(8,128)S(1)} %convolution_bitcast_fusion), channel_id=1, replica_groups=mesh['task_0'=4,'task_1'=2,'dp_0'=2,'dp_1'=4,'dp_2'=4] {'task_0'}, use_global_device_ids=true, to_apply=%region_1.0 | all-reduce | flops 64 | bytes 512 | tf_op jit(solution)/shard_map/psum | solution.py:14
  268.1 2.5 psum.36
  270.5 4.9 %psum.37 = f32[8,8]{1,0:T(8,128)S(1)} all-reduce(f32[8,8]{1,0:T(8,128)S(1)} %psum.36), channel_id=1, replica_groups=mesh['task_0'=4,'task_1'=2,'dp_0'=2,'dp_1'=4,'dp_2'=4] {'dp_0'}, use_global_device_ids=true, to_apply=%region_3.0 | all-reduce | flops 64 | bytes 512 | tf_op jit(solution)/shard_map/psum | solution.py:14
  275.4 7.7 %psum.38 = f32[8,8]{1,0:T(8,128)S(1)} all-reduce(f32[8,8]{1,0:T(8,128)S(1)} %psum.37), channel_id=1, replica_groups=mesh['task_0'=4,'task_1'=2,'dp_0'=2,'dp_1'=4,'dp_2'=4] {'dp_1'}, use_global_device_ids=true, to_apply=%region_4.0 | all-reduce | flops 64 | bytes 512 | tf_op jit(solution)/shard_map/psum | solution.py:14
  283.1 10.8 %psum.39 = f32[8,8]{1,0:T(8,128)S(1)} all-reduce(f32[8,8]{1,0:T(8,128)S(1)} %psum.38), channel_id=1, replica_groups=mesh['task_0'=4,'task_1'=2,'dp_0'=2,'dp_1'=4,'dp_2'=4] {'dp_2'}, use_global_device_ids=true, to_apply=%region_5.0 | all-reduce | flops 64 | bytes 512 | tf_op jit(solution)/shard_map/psum | solution.py:14
  293.9 1.3 fusion.140
  295.2 1.5 fusion.139
  296.7 1.3 fusion.137
  298.0 1.3 fusion.135
  299.3 1.5 fusion.133
  300.7 1.4 fusion.131
  302.1 1.4 fusion.129
  303.6 1.4 fusion.127
  305.0 0.8 fusion.33
  305.7 0.7 fusion.3
  306.4 0.9 fusion.6
  307.3 0.8 fusion.10
  308.1 0.8 fusion.14
  308.9 0.8 fusion.18
  309.8 0.8 fusion.22
  310.6 0.8 fusion.26
  311.4 0.8 fusion.30
  312.3 0.6 fusion.34
  312.9 0.2 broadcast_in_dim.5
  313.1 16.5 %all_to_all.23 = bf16[32,128,128]{2,1,0:T(8,128)(2,1)S(1)} all-to-all(bf16[32,128,128]{2,1,0:T(8,128)(2,1)S(1)} %broadcast_in_dim.5), channel_id=1, replica_groups=mesh['task_0'=4,'task_1'=2,'dp_0'=2,'dp_1'=4,'dp_2'=4] {'dp_0','dp_1','d..., dimensions={0} | all-to-all | bytes 2097152 | tf_op jit(solution)/shard_map/all_to_all | solution.py:20
  329.6 1.0 copy.11
  (8 shorter events, 0.1 us)
Async XLA Ops:
  6.5 1.6 copy-start
  6.5 223.8 %reduce-scatter.2.cloned.1.call-start = ((), (), s32[]{:S(2)}) async-start(), calls=%async_computation.3 | async-start | bytes 17301504 | tf_op jit(solution)/shard_map/reduce_scatter | solution.py:54
  22.7 0.7 copy-start.2
  22.7 5.8 %copy-start.1 = (s32[8,8]{1,0:T(8,128)S(1)}, s32[8,8]{1,0:T(8,128)}, u32[]{:S(2)}) copy-start(s32[8,8]{1,0:T(8,128)} %param.7) | copy-start | bytes 772
  232.3 24.3 %all-to-all-start = ((f32[1,128,1024]{1,0,2:T(1,128)}), f32[1,128,1024]{1,0,2:T(1,128)S(1)}, u32[]{:S(2)}, u32[]{:S(2)}) async-start(f32[1,128,1024]{1,0,2:T(1,128)} %copy.7), calls=%async_computation.1 | async-start | bytes 1048576 | tf_op jit(solution)/shard_map/all_to_all | solution.py:62
Sparse Core Ops, SparseCore 0:
  22.8 207.4 reduce-scatter.1
where the time goes:
time: 338 us; the launch traced here: 337 us
  waiting for transfers between devices  213 us (63%)
  blocking collectives  52.4 us (16%)
  matrix products  40 us (12%)
  between operations  13.5 us (4%)
  starting transfers between devices  7.26 us (2%)
  local copies, waits for them, and re-layouts  6.26 us (2%)
  other arithmetic  5.17 us (2%)
    reduce_scatter x1, waiting for transfers between devices, on_device(): lax.psum_scatter(lax.dot_general(inputs, task_cot, (((0,), (0,)), ((), ()...  199 us
    psum x5, blocking collectives, one_axis_at_a_time(): value = lax.psum(value, axis)  35.9 us
    all_to_all x1, blocking collectives, copy_for_each(): return lax.all_to_all(copies, axis, split_axis=0, concat_axis=0, tiled=True)  16.5 us
    dot_general x1, matrix products, on_device(): lax.dot_general(inputs, task_cot, (((0,), (0,)), ((), ())), preferred_ele...  14.5 us
    all_to_all x1, waiting for transfers between devices, on_device(): lax.all_to_all(shard_grad[None], TASK, split_axis=2, concat_axis=0, tiled...  13.4 us
    dot_general x8, matrix products, project_weights(): column = jnp.dot(gram_matrix, pick_column, precision=lax.Precision.HIGHEST)  11.1 us
    all_to_all x1, starting transfers between devices, on_device(): lax.all_to_all(shard_grad[None], TASK, split_axis=2, concat_axis=0, tiled...  7.26 us
  transfers between devices with their start and end apart: 2, of which 2 were waited for; matrix products, arithmetic and copies ran while one was open for 3% of the time, Pallas kernels for 0%

commit v1 on v0

v1 whole, which is shorter than its diff:
```python
import itertools

import jax
import jax.numpy as jnp
import numpy as np
from jax import lax
from jax.experimental import pallas as pl
from jax.experimental.pallas import tpu as pltpu
from jax.sharding import Mesh
from jax.sharding import PartitionSpec as P

AXES = ("zh", "core", "zl", "y", "x")
SIZES = (4, 2, 2, 4, 4)
DP = ("zl", "y", "x")
TASK = ("zh", "core")
F32, BF16, I16, I32 = jnp.float32, jnp.bfloat16, jnp.int16, jnp.int32

PARTNER = {"a": (1, 0, 3, 2), "b": (3, 2, 1, 0)}
BIT = {"a": (0, 1, 1, 0), "b": (0, 0, 1, 1)}
ORDER = {
    (0, 0): ("xa", "ya", "xb", "yb", "z"),
    (0, 1): ("xb", "yb", "xa", "ya", "z"),
    (1, 0): ("ya", "xa", "yb", "xb", "z"),
    (1, 1): ("yb", "xb", "ya", "xa", "z"),
}
FULL = 32000.0
STEPS = 64.0
EXTRA = 16


def coordinates():
    return [dict(zip(AXES, v)) for v in itertools.product(*map(range, SIZES))]


def linear(co):
    index = 0
    for axis, size in zip(AXES, SIZES):
        index = index * size + co[axis]
    return index


def bit_of(co, dim):
    return co["zl"] if dim == "z" else BIT[dim[1]][co[dim[0]]]


def partner(co, dim):
    if dim == "z":
        return {**co, "zl": 1 - co["zl"]}
    return {**co, dim[0]: PARTNER[dim[1]][co[dim[0]]]}


def swap_along(value, dims):
    pairs = [(linear(co), linear(partner(co, dims[co["core"]]))) for co in coordinates()]
    return lax.ppermute(value, AXES, pairs)


def position(co, core, chunk):
    place = 0
    for dim in ORDER[core, chunk]:
        place = 2 * place + bit_of(co, dim)
    return place


def device_table():
    rows = []
    for co in coordinates():
        core = co["core"]
        row = [core, co["zh"]]
        for chunk in range(2):
            bits = [bit_of(co, dim) for dim in ORDER[core, chunk]]
            base = 4 * core + 2 * chunk
            row += [base + 1 - bits[0], base + bits[0]] + bits[1:]
        rows.append(row + [0] * (16 - len(row)))
    return np.asarray(rows, np.int32)


def encode(tile):
    top = jnp.maximum(jnp.max(jnp.abs(tile), axis=0, keepdims=True), 1e-30)
    code = jnp.ceil(jnp.log(top) * STEPS)
    values = jnp.round(tile * (jnp.exp(code * (-1.0 / STEPS)) * FULL))
    return values.astype(I32).astype(I16), code


def scales(codes):
    return jnp.exp(codes.astype(I32).astype(F32) * (1.0 / STEPS)) * (1.0 / FULL)


def floats(values):
    return values.astype(I32).astype(F32)


def params(mib=40):
    return pltpu.CompilerParams(vmem_limit_bytes=mib << 20)


def call(kernel, scalars, grid, inputs, in_specs, out_shape, out_specs, scratch, flops, nbytes, **extra):
    return pl.pallas_call(
        kernel,
        out_shape=out_shape,
        grid_spec=pltpu.PrefetchScalarGridSpec(
            num_scalar_prefetch=1,
            grid=grid,
            in_specs=in_specs,
            out_specs=out_specs,
            scratch_shapes=scratch,
        ),
        compiler_params=params(),
        cost_estimate=pl.CostEstimate(flops=flops, bytes_accessed=nbytes, transcendentals=0),
        **extra,
    )(scalars, *inputs)


def whole(shape):
    return pl.BlockSpec(shape, lambda *_: (0,) * len(shape))


ROWS = 512
TILE = 128
COLS = 256


def dot_rows(transposed, cot):
    return lax.dot_general(transposed, cot, (((1,), (0,)), ((), ())), preferred_element_type=F32)


def send_kernel(s_ref, x_ref, own_ref, other_ref, out_ref, turned, codes):
    step = pl.program_id(0)

    @pl.when(step == 0)
    def _():
        turned[...] = x_ref[...].T
        codes[...] = jnp.zeros_like(codes)

    column = pl.ds(pl.multiple_of(lax.rem(step, 4) * COLS, COLS), COLS)

    def one(task, cot_ref):
        product = dot_rows(turned[...], cot_ref[...])
        for tile in range(ROWS // TILE):
            values, code = encode(product[tile * TILE : (tile + 1) * TILE])
            out_ref[pl.ds(task * ROWS + tile * TILE, TILE), column] = values
            codes[pl.ds(task * (ROWS // TILE) + tile, 1), column] = code

    @pl.when(step < 4)
    def _():
        one(0, own_ref)

    @pl.when(step >= 4)
    def _():
        one(1, other_ref)

    @pl.when(step == 7)
    def _():
        out_ref[2 * ROWS :, :] = codes[...].astype(I32).astype(I16)


def cot_specs(tokens):
    return [
        pl.BlockSpec((tokens, COLS), lambda n, s: (0, jnp.minimum(n, 3))),
        pl.BlockSpec((tokens, COLS), lambda n, s: (0, jnp.maximum(n - 4, 0))),
    ]


def send_term(table, slot, inputs, own, other):
    tokens, width = own.shape
    return call(
        send_kernel,
        table,
        (8,),
        (inputs, own, other),
        [pl.BlockSpec((tokens, ROWS), lambda n, s: (0, s[slot]))] + cot_specs(tokens),
        jax.ShapeDtypeStruct((2 * ROWS + EXTRA, width), I16),
        whole((2 * ROWS + EXTRA, width)),
        [pltpu.VMEM((ROWS, tokens), BF16), pltpu.VMEM((EXTRA, width), F32)],
        4 * ROWS * tokens * width,
        7 << 20,
    )


def keep_kernel(s_ref, x_ref, own_ref, other_ref, out_ref, turned):
    step = pl.program_id(0)

    @pl.when(step == 0)
    def _():
        turned[...] = x_ref[...].T

    @pl.when(step < 4)
    def _():
        out_ref[0] = dot_rows(turned[...], own_ref[...])

    @pl.when(step >= 4)
    def _():
        out_ref[0] = dot_rows(turned[...], other_ref[...])


def keep_term(table, slot, inputs, own, other):
    tokens, width = own.shape
    return call(
        keep_kernel,
        table,
        (8,),
        (inputs, own, other),
        [pl.BlockSpec((tokens, ROWS), lambda n, s: (0, s[slot]))] + cot_specs(tokens),
        jax.ShapeDtypeStruct((2, ROWS, width), F32),
        pl.BlockSpec((1, ROWS, COLS), lambda n, s: (n // 4, 0, lax.rem(n, 4))),
        [pltpu.VMEM((ROWS, tokens), BF16)],
        4 * ROWS * tokens * width,
        9 << 20,
    )


def level(table, slot, kept, arrived):
    _, rows, width = kept.shape
    half = rows // 2
    tile = min(TILE, half)
    per = half // tile
    code_rows = min(TILE, rows)

    def kernel(s_ref, keep_ref, give_ref, keep_in, give_in, codes_ref, sum_ref, out_ref, scale, codes):
        task, j = pl.program_id(0), pl.program_id(1)
        bit = s_ref[slot]

        @pl.when((task == 0) & (j == 0))
        def _():
            scale[...] = scales(codes_ref[...])
            codes[...] = jnp.zeros_like(codes)

        def row_of(side):
            return (task * rows + side * half + j * tile) // code_rows

        sum_ref[0] = keep_ref[0] + floats(keep_in[...]) * scale[pl.ds(row_of(bit), 1), :]
        give = give_ref[0] + floats(give_in[...]) * scale[pl.ds(row_of(1 - bit), 1), :]
        values, code = encode(give)
        at = task * per + j
        out_ref[pl.ds(pl.multiple_of(at * tile, tile), tile), :] = values
        codes[pl.ds(at, 1), :] = code

        @pl.when((task == 1) & (j == per - 1))
        def _():
            out_ref[2 * half :, :] = codes[...].astype(I32).astype(I16)

    return call(
        kernel,
        table,
        (2, per),
        (kept, kept, arrived, arrived, arrived),
        [
            pl.BlockSpec((1, tile, width), lambda t, j, s: (t, s[slot] * per + j, 0)),
            pl.BlockSpec((1, tile, width), lambda t, j, s: (t, (1 - s[slot]) * per + j, 0)),
            pl.BlockSpec((tile, width), lambda t, j, s: ((2 * t + s[slot]) * per + j, 0)),
            pl.BlockSpec((tile, width), lambda t, j, s: ((2 * t + 1 - s[slot]) * per + j, 0)),
            pl.BlockSpec((EXTRA, width), lambda t, j, s: (2 * rows // EXTRA, 0)),
        ],
        (jax.ShapeDtypeStruct((2, half, width), F32), jax.ShapeDtypeStruct((2 * half + EXTRA, width), I16)),
        (pl.BlockSpec((1, tile, width), lambda t, j, s: (t, j, 0)), whole((2 * half + EXTRA, width))),
        [pltpu.VMEM((EXTRA, width), F32), pltpu.VMEM((EXTRA, width), F32)],
        16 * rows * width,
        2 * rows * width * 9,
    )


def join_level(table, slot, kept, arrived):
    _, rows, width = kept[0].shape
    half = rows // 2

    def kernel(s_ref, keep_a, keep_b, in_a, in_b, sum_ref, out_ref):
        bit = s_ref[slot]
        out_codes = []
        for chunk, (keep, arr) in enumerate(((keep_a, in_a), (keep_b, in_b))):
            scale = scales(arr[2 * rows :, :])
            for task in range(2):

                def part(side):
                    at = pl.multiple_of(side * half, half)
                    values = floats(arr[pl.ds(pl.multiple_of(task * rows + side * half, half), half), :])
                    return keep[task, pl.ds(at, half), :] + values * scale[task : task + 1]

                sum_ref[chunk, task] = part(bit)
                values, code = encode(part(1 - bit))
                n = 2 * chunk + task
                out_ref[n * half : (n + 1) * half, :] = values
                out_codes.append(code)
        out_codes.append(jnp.zeros((EXTRA - 4, width), F32))
        out_ref[4 * half :, :] = jnp.concatenate(out_codes, axis=0).astype(I32).astype(I16)

    shapes = ((2, rows, width), (2, rows, width), (2 * rows + EXTRA, width), (2 * rows + EXTRA, width))
    return call(
        kernel,
        table,
        (1,),
        (*kept, *arrived),
        [whole(s) for s in shapes],
        (jax.ShapeDtypeStruct((2, 2, half, width), F32), jax.ShapeDtypeStruct((4 * half + EXTRA, width), I16)),
        (whole((2, 2, half, width)), whole((4 * half + EXTRA, width))),
        [],
        32 * rows * width,
        4 * rows * width * 9,
    )


def columns_kernel(s_ref, keep_ref, in_ref, own_ref, out1, out2, out3, total):
    zh = s_ref[1]
    rows = keep_ref.shape[2]
    scale = scales(in_ref[4 * rows :, :])
    for n in range(4):
        total[n * rows : (n + 1) * rows, :] = keep_ref[n // 2, n % 2] + floats(
            in_ref[n * rows : (n + 1) * rows, :]
        ) * scale[n : n + 1]
    wide = own_ref.shape[1]

    def block(k):
        return total[:, pl.ds(pl.multiple_of(lax.rem(zh + k, 4) * wide, wide), wide)]

    own_ref[...] = block(0)
    for k, out in ((1, out1), (2, out2), (3, out3)):
        value = block(k)
        codes = []
        for n in range(4):
            values, code = encode(value[n * rows : (n + 1) * rows])
            out[n * rows : (n + 1) * rows, :] = values
            codes.append(code)
        codes.append(jnp.zeros((EXTRA - 4, wide), F32))
        out[4 * rows :, :] = jnp.concatenate(codes, axis=0).astype(I32).astype(I16)


def columns(table, kept, arrived):
    rows, width = kept.shape[2:]
    wide = width // 4
    coded = (4 * rows + EXTRA, wide)
    return call(
        columns_kernel,
        table,
        (1,),
        (kept, arrived),
        [whole(kept.shape), whole(arrived.shape)],
        (jax.ShapeDtypeStruct((4 * rows, wide), F32),) + (jax.ShapeDtypeStruct(coded, I16),) * 3,
        (whole((4 * rows, wide)),) + (whole(coded),) * 3,
        [pltpu.VMEM((4 * rows, width), F32)],
        16 * rows * width,
        8 * rows * width * 4,
    )


def lanes(shape, dim):
    return lax.broadcasted_iota(I32, shape, dim)


def gram_kernel(s_ref, own_ref, in1, in2, in3, grads_ref, gram_ref):
    core, zh = s_ref[0], s_ref[1]
    rows = own_ref.shape[0] // 4

    def place(k, tiles):
        pair = lax.rem(zh + 4 - k, 4)
        for n in range(4):
            chunk, task = n // 2, n % 2
            mine = 2 * pair + (task + core - 2 * task * core)
            grads_ref[mine, chunk * rows : (chunk + 1) * rows, :] = tiles(n)

    place(0, lambda n: own_ref[n * rows : (n + 1) * rows, :])
    for k, ref in ((1, in1), (2, in2), (3, in3)):
        scale = scales(ref[4 * rows :, :])
        place(k, lambda n: floats(ref[n * rows : (n + 1) * rows, :]) * scale[n : n + 1])

    grads = [grads_ref[t] for t in range(8)]
    lane, sub = lanes((8, 128), 1), lanes((8, 128), 0)
    matrix = jnp.zeros((8, 128), F32)
    for s in range(8):
        for t in range(s, 8):
            product = grads[s] * grads[t]
            folded = product[:, :128] + product[:, 128:]
            total = jnp.sum(jnp.sum(folded, axis=0, keepdims=True), axis=1, keepdims=True)
            here = ((sub == s) & (lane == t)) | ((sub == t) & (lane == s))
            matrix = jnp.where(here, total, matrix)
    line = jnp.zeros((8, 128), F32)
    for s in range(8):
        row = jnp.where(sub == s, matrix, 0.0)
        line = line + (row if s == 0 else pltpu.roll(row, 8 * s, 1))
    flat = jnp.sum(line, axis=0, keepdims=True)
    gram_ref[...] = jnp.broadcast_to(flat, gram_ref.shape)


def gram(table, own, arrived):
    rows, wide = own.shape
    coded = arrived[0].shape
    return call(
        gram_kernel,
        table,
        (1,),
        (own, *arrived),
        [whole(own.shape)] + [whole(coded)] * 3,
        (jax.ShapeDtypeStruct((8, rows // 2, wide), F32), jax.ShapeDtypeStruct((256, 128), F32)),
        (whole((8, rows // 2, wide)), whole((256, 128))),
        [],
        80 * rows * wide,
        16 * rows * wide,
    )


def combine_kernel(s_ref, order_ref, flags_ref, gram_ref, grads_ref, mine_ref, give_ref):
    core = s_ref[0]
    lane, sub = lanes((8, 128), 1), lanes((8, 128), 0)
    flat = jnp.broadcast_to(jnp.sum(gram_ref[...], axis=0, keepdims=True), (8, 128))
    matrix = jnp.zeros((8, 128), F32)
    for s in range(8):
        row = flat if s == 0 else pltpu.roll(flat, 128 - 8 * s, 1)
        matrix = jnp.where((sub == s) & (lane < 8), row, matrix)
    flags = flags_ref[...].astype(F32)
    small = lanes((8, 8), 1)
    coefficients = jnp.where(lane == sub, 1.0, 0.0)
    for k in range(8):
        target = order_ref[k]
        row = jnp.sum(jnp.where(sub == target, matrix, 0.0), axis=0, keepdims=True)
        dots = jnp.sum(coefficients * row, axis=1, keepdims=True)
        square = jnp.sum(jnp.where(lane[:1] == target, row, 0.0), axis=1, keepdims=True)
        active = jnp.sum(jnp.where(small == target, flags, 0.0), axis=1, keepdims=True)
        active = jnp.where(sub[:, :1] == target, 0.0, active)
        removed = jnp.minimum(dots, 0.0) / square * active
        coefficients = coefficients - jnp.where(lane == target, removed, 0.0)
    weights = jnp.sum(coefficients, axis=0, keepdims=True)
    total = None
    for t in range(8):
        weight = jnp.sum(jnp.where(lane[:1] == t, weights, 0.0), axis=1, keepdims=True)
        term = weight * grads_ref[t]
        total = term if total is None else total + term
    left, right = total[:, :128].astype(BF16), total[:, 128:].astype(BF16)

    @pl.when(core == 0)
    def _():
        mine_ref[...] = left
        give_ref[...] = right

    @pl.when(core == 1)
    def _():
        mine_ref[...] = right
        give_ref[...] = left


def combine(table, order, flags, grams, grads):
    rows = grads.shape[1]
    part = jax.ShapeDtypeStruct((rows, 128), BF16)
    return call(
        combine_kernel,
        table,
        (1,),
        (order, flags, grams, grads),
        [pl.BlockSpec(memory_space=pltpu.SMEM), whole((8, 8)), whole((256, 128)), whole(grads.shape)],
        (part, part),
        (whole((rows, 128)),) * 2,
        [],
        20 * rows * 256,
        40 * rows * 256,
    )


def place_kernel(in_ref, out_ref):
    rows = in_ref.shape[1] // 4
    for index, (zl, y, x) in enumerate(itertools.product(range(2), range(4), range(4))):
        co = {"zl": zl, "y": y, "x": x}
        for n in range(4):
            at = (n * 32 + position(co, n // 2, n % 2)) * rows
            out_ref[at : at + rows, :] = in_ref[index, n * rows : (n + 1) * rows, :]


def place(gathered):
    count, rows, cols = gathered.shape
    return pl.pallas_call(
        place_kernel,
        out_shape=jax.ShapeDtypeStruct((count * rows, cols), BF16),
        compiler_params=params(),
        cost_estimate=pl.CostEstimate(flops=0, bytes_accessed=4 * count * rows * cols, transcendentals=0),
    )(gathered)


def on_device(inputs, cotangent, task_order, conflict_flags):
    table = jnp.asarray(device_table())[lax.axis_index(AXES)]
    core = lax.axis_index("core")
    own = cotangent[0]
    other = lax.ppermute(own, "core", [(0, 1), (1, 0)])

    dims = [[(ORDER[0, chunk][n], ORDER[1, chunk][n]) for n in range(5)] for chunk in range(2)]
    slots = [2, 8]
    arrived, kept = [], []
    for chunk in range(2):
        coded = send_term(table, slots[chunk], inputs, own, other)
        arrived.append(swap_along(coded, dims[chunk][0]))
    for chunk in range(2):
        kept.append(keep_term(table, slots[chunk] + 1, inputs, own, other))
    for n in range(1, 4):
        for chunk in range(2):
            kept[chunk], coded = level(table, slots[chunk] + 1 + n, kept[chunk], arrived[chunk])
            arrived[chunk] = swap_along(coded, dims[chunk][n])
    summed, coded = join_level(table, slots[0] + 5, kept, arrived)
    own_cols, *coded = columns(table, summed, swap_along(coded, ("z", "z")))
    turned = [
        lax.ppermute(value, "zh", [(i, (i + k) % 4) for i in range(4)]) for k, value in zip((1, 2, 3), coded)
    ]
    grads, grams = gram(table, own_cols, turned)
    grams = lax.all_to_all(grams, AXES, split_axis=0, concat_axis=0, tiled=True)
    mine, give = combine(table, task_order, conflict_flags, grams, grads)
    taken = lax.ppermute(give, "core", [(0, 1), (1, 0)])
    first = jnp.where(core == 0, mine, taken)
    second = jnp.where(core == 0, taken, mine)
    block = jnp.concatenate([first, second], axis=0)
    copies = jnp.broadcast_to(block, (32, *block.shape))
    gathered = lax.all_to_all(copies, DP, split_axis=0, concat_axis=0, tiled=True)
    return place(gathered)


def solution(mesh):
    split = Mesh(mesh.devices.reshape(SIZES), AXES)
    placed = (P(DP, None), P(TASK, DP, None), P(), P())
    return jax.shard_map(
        on_device, mesh=split, in_specs=placed, out_specs=P(None, TASK), check_vma=False
    )
```

time: 338 us -> 166 us (0.49)
  waiting for transfers between devices: 213 us -> 45.7 us
  Pallas kernels: 0 us -> 42.9 us
  matrix products: 40 us -> 0 us
  starting transfers between devices: 7.26 us -> 26.1 us
  between operations: 13.5 us -> 0.16 us
  blocking collectives: 52.4 us -> 45.1 us
  other arithmetic: 5.17 us -> 0.01 us
    reduce_scatter x1 -> x0, waiting for transfers between devices: 199 us -> none  [on_device(): lax.psum_scatter(lax.dot_general(inputs, task_cot, (((0,), (0,)), ((), ()...]
    ppermute x0 -> x14, waiting for transfers between devices: none -> 45.7 us  [the longest x9 38.9 us: swap_along(): return lax.ppermute(value, AXES, pairs)]
    pallas_call x0 -> x15, Pallas kernels: none -> 42.9 us  [the longest x14 41.9 us: call(): pl.pallas_call(kernel, out_shape=out_shape, grid_spec=pltpu.PrefetchScala...]
    dot_general x26 -> x0, matrix products: 39.4 us -> none  [the longest x1 14.5 us: on_device(): lax.dot_general(inputs, task_cot, (((0,), (0,)), ((), ())), preferred_ele...]
    psum x5 -> x0, blocking collectives: 35.9 us -> none  [one_axis_at_a_time(): value = lax.psum(value, axis)]
    all_to_all x1 -> x2, blocking collectives: 16.5 us -> 45.1 us  [the longest x1 23.8 us: on_device(): grams = lax.all_to_all(grams, AXES, split_axis=0, concat_axis=0, tiled=True)]
    ppermute x0 -> x14, starting transfers between devices: none -> 26.1 us  [the longest x9 13.7 us: swap_along(): return lax.ppermute(value, AXES, pairs)]
    all_to_all x1 -> x0, waiting for transfers between devices: 13.4 us -> none  [on_device(): lax.all_to_all(shard_grad[None], TASK, split_axis=2, concat_axis=0, tiled...]
  transfers between devices with their start and end apart: 2 -> 14, of which waited for: 2 -> 12; matrix products, arithmetic and copies ran while one was open for 3% -> 0% of each run, Pallas kernels for 0% -> 18%
where the time goes in v1:
time: 166 us
  waiting for transfers between devices  45.7 us (28%)
  blocking collectives  45.1 us (27%)
  Pallas kernels  42.9 us (26%)
  starting transfers between devices  26.1 us (16%)
  local copies, waits for them, and re-layouts  5.48 us (3%)
    pallas_call x14, Pallas kernels, call(): pl.pallas_call(kernel, out_shape=out_shape, grid_spec=pltpu.PrefetchScala...  41.9 us
    ppermute x9, waiting for transfers between devices, swap_along(): return lax.ppermute(value, AXES, pairs)  38.9 us
    all_to_all x1, blocking collectives, on_device(): grams = lax.all_to_all(grams, AXES, split_axis=0, concat_axis=0, tiled=True)  23.8 us
    all_to_all x1, blocking collectives, on_device(): lax.all_to_all(copies, DP, split_axis=0, concat_axis=0, tiled=True)  21.3 us
    ppermute x9, starting transfers between devices, swap_along(): return lax.ppermute(value, AXES, pairs)  13.7 us
    ppermute x3, starting transfers between devices, on_device(): lax.ppermute(value, 'zh', [(i, (i + k) % 4) for i in range(4)])  12.3 us
    unnamed x10, local copies, waits for them, and re-layouts  4.56 us
    ppermute x1, waiting for transfers between devices, on_device(): other = lax.ppermute(own, 'core', [(0, 1), (1, 0)])  3.68 us
  transfers between devices with their start and end apart: 14, of which 12 were waited for; matrix products, arithmetic and copies ran while one was open for 0% of the time, Pallas kernels for 18%

profile of v1, /device:TPU:32, one launch (start us, length us, event | category | flops | bytes accessed | tf_op | source)
XLA Modules:
  0.0 165.5 jit_solution(10785538140664465412)
XLA Ops:
  0.0 0.7 dynamic-slice_bitcast_fusion.s_ref
  0.7 3.7 %collective-permute-done.other_ref = bf16[1024,1024]{1,0:T(8,128)(2,1)S(1)} collective-permute-done((bf16[1024,1024]{1,0:T(8,128)(2,1)}, bf16[1024,1024]{1,0:T(8,128)(2,1)S(1)}, u32[]{:S(2)}, u32[]{:S(2)}) %collective-permute-start) | collective-permute-done | bytes 2097184 | tf_op jit(solution)/shard_map/ppermute | solution.py:477
  4.4 1.6 copy-done
  6.0 8.2 %shard_map.61 = s16[1040,1024]{1,0:T(8,128)(2,1)} custom-call(s32[16]{0:T(128)S(1)} %dynamic-slice_bitcast_fusion.s_ref, bf16[1024,4096]{1,0:T(8,128)(2,1)} %x_ref.7, bf16[1024,1024]{1,0:T(8,128)(2,1)S(1)} %bitcast.8, bf16[1024,1024]{1,0:T(8,128)(2,1)S(1)} %collective-permute-done.other_ref), custom_call_target="tpu_custom_call" | custom-call | flops 2147483648 | bytes 7340032 | tf_op jit(solution)/shard_map/pallas_call | solution.py:97
  14.2 2.8 %collective-permute-start.4 = (s16[1040,1024]{1,0:T(8,128)(2,1)}, s16[1040,1024]{1,0:T(8,128)(2,1)S(1)}, u32[]{:S(2)}, u32[]{:S(2)}) collective-permute-start(s16[1040,1024]{1,0:T(8,128)(2,1)} %shard_map.61), channel_id=1, source_target_pairs={{0,3},{1,2},{2,1},{3,0},{4,7},{5,6},{6,5},{7,4},{8,11},{9,10},{10,... | collective-permute-start | bytes 6389768 | tf_op jit(solution)/shard_map/ppermute | solution.py:54
  16.9 6.9 %shard_map.56 = s16[1040,1024]{1,0:T(8,128)(2,1)S(1)} custom-call(s32[16]{0:T(128)S(1)} %dynamic-slice_bitcast_fusion.s_ref, bf16[1024,4096]{1,0:T(8,128)(2,1)} %x_ref.7, bf16[1024,1024]{1,0:T(8,128)(2,1)S(1)} %bitcast.9, bf16[1024,1024]{1,0:T(8,128)(2,1)S(1)} %collective-permute-done.other_ref), custom_call_target="tpu_custom_call" | custom-call | flops 2147483648 | bytes 7340032 | tf_op jit(solution)/shard_map/pallas_call | solution.py:97
  23.8 0.3 collective-permute-start.1
  24.1 7.0 %shard_map.60.keep_ref.give_ref = f32[2,512,1024]{2,1,0:T(8,128)S(1)} custom-call(s32[16]{0:T(128)S(1)} %dynamic-slice_bitcast_fusion.s_ref, bf16[1024,4096]{1,0:T(8,128)(2,1)} %x_ref.7, bf16[1024,1024]{1,0:T(8,128)(2,1)S(1)} %bitcast.10, bf16[1024,1024]{1,0:T(8,128)(2,1)S(1)} %collective-permute-done.other_ref), custom_call_target="tpu_custom_call" | custom-call | flops 2147483648 | bytes 9437184 | tf_op jit(solution)/shard_map/pallas_call | solution.py:97
  31.1 7.0 %shard_map.55.keep_ref.give_ref = f32[2,512,1024]{2,1,0:T(8,128)S(1)} custom-call(s32[16]{0:T(128)S(1)} %dynamic-slice_bitcast_fusion.s_ref, bf16[1024,4096]{1,0:T(8,128)(2,1)} %x_ref.7, bf16[1024,1024]{1,0:T(8,128)(2,1)S(1)} %bitcast.11, bf16[1024,1024]{1,0:T(8,128)(2,1)S(1)} %collective-permute-done.other_ref), custom_call_target="tpu_custom_call" | custom-call | flops 2147483648 | bytes 9437184 | tf_op jit(solution)/shard_map/pallas_call | solution.py:97
  38.1 3.9 %collective-permute-done.4.keep_in.give_in.codes_ref = s16[1040,1024]{1,0:T(8,128)(2,1)S(1)} collective-permute-done((s16[1040,1024]{1,0:T(8,128)(2,1)}, s16[1040,1024]{1,0:T(8,128)(2,1)S(1)}, u32[]{:S(2)}, u32[]{:S(2)}) %collective-permute-start.4) | collective-permute-done | bytes 2129952 | tf_op jit(solution)/shard_map/ppermute | solution.py:54
  42.0 1.4 copy-done.1
  43.3 1.6 copy-done.2
  44.9 2.0 %shard_map.62 = (f32[2,256,1024]{2,1,0:T(8,128)S(1)}, s16[528,1024]{1,0:T(8,128)(2,1)S(1)}) custom-call(s32[16]{0:T(128)S(1)} %dynamic-slice_bitcast_fusion.s_ref, f32[2,512,1024]{2,1,0:T(8,128)S(1)} %shard_map.60.keep_ref.give_ref, f32[2,512,1024]{2,1,0:T(8,128)S(1)} %shard_map.60.keep_ref.give_ref, s16[1040,1024]{1,0:T(8,128)(2,1)S(1)} %copy-done.2, ...), custom_call_target="tpu_custom_call" | custom-call | flops 8388608 | bytes 9437184 | tf_op jit(solution)/shard_map/pallas_call | solution.py:97
  46.9 3.1 %collective-permute-start.5 = (s16[528,1024]{1,0:T(8,128)(2,1)S(1)}, s16[528,1024]{1,0:T(8,128)(2,1)S(1)}, u32[]{:S(2)}, u32[]{:S(2)}) collective-permute-start(s16[528,1024]{1,0:T(8,128)(2,1)S(1)} %get-tuple-element.33), channel_id=1, source_target_pairs={{0,12},{1,13},{2,14},{3,15},{4,8},{5,9},{6,10},{7,11},{8,4},{9,5},... | collective-permute-start | bytes 3244040 | tf_op jit(solution)/shard_map/ppermute | solution.py:54
  50.0 0.3 collective-permute-done.1.keep_in.give_in.codes_ref
  50.3 2.0 %shard_map.57 = (f32[2,256,1024]{2,1,0:T(8,128)S(1)}, s16[528,1024]{1,0:T(8,128)(2,1)S(1)}) custom-call(s32[16]{0:T(128)S(1)} %dynamic-slice_bitcast_fusion.s_ref, f32[2,512,1024]{2,1,0:T(8,128)S(1)} %shard_map.55.keep_ref.give_ref, f32[2,512,1024]{2,1,0:T(8,128)S(1)} %shard_map.55.keep_ref.give_ref, ...), custom_call_target="tpu_custom_call" | custom-call | flops 8388608 | bytes 9437184 | tf_op jit(solution)/shard_map/pallas_call | solution.py:97
  52.2 1.7 %collective-permute-start.2 = (s16[528,1024]{1,0:T(8,128)(2,1)S(1)}, s16[528,1024]{1,0:T(8,128)(2,1)S(1)}, u32[]{:S(2)}, u32[]{:S(2)}) collective-permute-start(s16[528,1024]{1,0:T(8,128)(2,1)S(1)} %get-tuple-element.28), channel_id=1, source_target_pairs={{0,4},{1,5},{2,6},{3,7},{4,0},{5,1},{6,2},{7,3},{8,12},{9,13},{10,... | collective-permute-start | bytes 3244040 | tf_op jit(solution)/shard_map/ppermute | solution.py:54
  53.9 9.4 %collective-permute-done.5.keep_in.give_in.codes_ref = s16[528,1024]{1,0:T(8,128)(2,1)S(1)} collective-permute-done((s16[528,1024]{1,0:T(8,128)(2,1)S(1)}, s16[528,1024]{1,0:T(8,128)(2,1)S(1)}, u32[]{:S(2)}, u32[]{:S(2)}) %collective-permute-start.5) | collective-permute-done | bytes 1081376 | tf_op jit(solution)/shard_map/ppermute | solution.py:54
  63.4 1.2 shard_map.63
  64.6 0.4 collective-permute-start.6
  65.0 4.5 %collective-permute-done.2.keep_in.give_in.codes_ref = s16[528,1024]{1,0:T(8,128)(2,1)S(1)} collective-permute-done((s16[528,1024]{1,0:T(8,128)(2,1)S(1)}, s16[528,1024]{1,0:T(8,128)(2,1)S(1)}, u32[]{:S(2)}, u32[]{:S(2)}) %collective-permute-start.2) | collective-permute-done | bytes 1081376 | tf_op jit(solution)/shard_map/ppermute | solution.py:54
  69.5 1.2 shard_map.58
  70.8 1.9 %collective-permute-start.3 = (s16[272,1024]{1,0:T(8,128)(2,1)S(1)}, s16[272,1024]{1,0:T(8,128)(2,1)S(1)}, u32[]{:S(2)}, u32[]{:S(2)}) collective-permute-start(s16[272,1024]{1,0:T(8,128)(2,1)S(1)} %get-tuple-element.30), channel_id=1, source_target_pairs={{0,3},{1,2},{2,1},{3,0},{4,7},{5,6},{6,5},{7,4},{8,11},{9,10},{10,... | collective-permute-start | bytes 1671176 | tf_op jit(solution)/shard_map/ppermute | solution.py:54
  72.7 1.5 collective-permute-done.6.keep_in.give_in.codes_ref
  74.2 0.9 shard_map.64
  75.2 0.5 collective-permute-start.8
  75.6 6.0 %collective-permute-done.3.keep_in.give_in.codes_ref = s16[272,1024]{1,0:T(8,128)(2,1)S(1)} collective-permute-done((s16[272,1024]{1,0:T(8,128)(2,1)S(1)}, s16[272,1024]{1,0:T(8,128)(2,1)S(1)}, u32[]{:S(2)}, u32[]{:S(2)}) %collective-permute-start.3) | collective-permute-done | bytes 557088 | tf_op jit(solution)/shard_map/ppermute | solution.py:54
  81.6 0.9 shard_map.59
  82.5 0.0 copy-start.3
  82.5 2.8 %collective-permute-start.7 = (s16[144,1024]{1,0:T(8,128)(2,1)S(1)}, s16[144,1024]{1,0:T(8,128)(2,1)S(1)}, u32[]{:S(2)}, u32[]{:S(2)}) collective-permute-start(s16[144,1024]{1,0:T(8,128)(2,1)S(1)} %get-tuple-element.37), channel_id=1, source_target_pairs={{0,12},{1,13},{2,14},{3,15},{4,8},{5,9},{6,10},{7,11},{8,4},{9,5},... | collective-permute-start | bytes 884744 | tf_op jit(solution)/shard_map/ppermute | solution.py:54
  85.3 5.2 %collective-permute-done.7.in_a = s16[144,1024]{1,0:T(8,128)(2,1)S(1)} collective-permute-done((s16[144,1024]{1,0:T(8,128)(2,1)S(1)}, s16[144,1024]{1,0:T(8,128)(2,1)S(1)}, u32[]{:S(2)}, u32[]{:S(2)}) %collective-permute-start.7) | collective-permute-done | bytes 294944 | tf_op jit(solution)/shard_map/ppermute | solution.py:54
  90.6 0.8 shard_map.65
  91.4 0.3 collective-permute-start.9
  91.7 8.0 %collective-permute-done.9.in_ref = s16[144,1024]{1,0:T(8,128)(2,1)S(1)} collective-permute-done((s16[144,1024]{1,0:T(8,128)(2,1)S(1)}, s16[144,1024]{1,0:T(8,128)(2,1)S(1)}, u32[]{:S(2)}, u32[]{:S(2)}) %collective-permute-start.9) | collective-permute-done | bytes 294944 | tf_op jit(solution)/shard_map/ppermute | solution.py:54
  99.7 0.8 shard_map.66
  100.5 4.2 %collective-permute-start.10 = (s16[144,256]{1,0:T(8,128)(2,1)S(1)}, s16[144,256]{1,0:T(8,128)(2,1)S(1)}, u32[]{:S(2)}, u32[]{:S(2)}) collective-permute-start(s16[144,256]{1,0:T(8,128)(2,1)S(1)} %get-tuple-element.42), channel_id=1, source_target_pairs={{0,64},{64,128},{128,192},{192,0},{1,65},{65,129},{129,193},{193,1... | collective-permute-start | bytes 221192 | tf_op jit(solution)/shard_map/ppermute | solution.py:494
  104.8 4.1 %collective-permute-start.11 = (s16[144,256]{1,0:T(8,128)(2,1)S(1)}, s16[144,256]{1,0:T(8,128)(2,1)S(1)}, u32[]{:S(2)}, u32[]{:S(2)}) collective-permute-start(s16[144,256]{1,0:T(8,128)(2,1)S(1)} %get-tuple-element.43), channel_id=1, source_target_pairs={{0,128},{64,192},{128,0},{192,64},{1,129},{65,193},{129,1},{193,65... | collective-permute-start | bytes 221192 | tf_op jit(solution)/shard_map/ppermute | solution.py:494
  108.9 4.0 %collective-permute-start.12 = (s16[144,256]{1,0:T(8,128)(2,1)S(1)}, s16[144,256]{1,0:T(8,128)(2,1)S(1)}, u32[]{:S(2)}, u32[]{:S(2)}) collective-permute-start(s16[144,256]{1,0:T(8,128)(2,1)S(1)} %get-tuple-element.44), channel_id=1, source_target_pairs={{0,192},{64,0},{128,64},{192,128},{1,193},{65,1},{129,65},{193,129... | collective-permute-start | bytes 221192 | tf_op jit(solution)/shard_map/ppermute | solution.py:494
  112.9 0.3 collective-permute-done.11.in2
  113.1 1.7 %collective-permute-done.12.in3 = s16[144,256]{1,0:T(8,128)(2,1)S(1)} collective-permute-done((s16[144,256]{1,0:T(8,128)(2,1)S(1)}, s16[144,256]{1,0:T(8,128)(2,1)S(1)}, u32[]{:S(2)}, u32[]{:S(2)}) %collective-permute-start.12) | collective-permute-done | bytes 73760 | tf_op jit(solution)/shard_map/ppermute | solution.py:494
  114.9 1.0 shard_map.67
  115.8 23.8 %all_to_all.16 = f32[256,1,128]{2,1,0:T(1,128)S(1)} all-to-all(f32[256,1,128]{2,1,0:T(1,128)S(1)} %bitcast.13), channel_id=1, replica_groups=mesh['zh'=4,'core'=2,'zl'=2,'y'=4,'x'=4] {'zh','core','zl','y','x'}, dimensions={0} | all-to-all | bytes 262144 | tf_op jit(solution)/shard_map/all_to_all | solution.py:497
  139.6 2.0 %shard_map.68 = (bf16[64,128]{1,0:T(8,128)(2,1)S(1)}, bf16[64,128]{1,0:T(8,128)(2,1)S(1)}) custom-call(s32[16]{0:T(128)S(1)} %dynamic-slice_bitcast_fusion.s_ref, s32[8]{0:T(128)S(1)} %copy-done.4, s32[8,8]{1,0:T(8,128)S(1)} %copy-done.3, f32[256,128]{1,0:T(8,128)S(1)} %bitcast.12, f32[8,64,256]{2,1,0:T(8,128)S(1)} %get-tuple-element.46.grads_ref), custom_call_target="tpu_custom_call" | custom-call | flops 327680 | bytes 655360 | tf_op jit(solution)/shard_map/pallas_call | solution.py:97
  141.6 0.1 collective-permute-start.13
  141.7 1.2 collective-permute-done.13
  142.9 0.2 broadcast_in_dim.3
  143.1 21.3 %all_to_all.17.in_ref = bf16[32,128,128]{2,1,0:T(8,128)(2,1)S(1)} all-to-all(bf16[32,128,128]{2,1,0:T(8,128)(2,1)S(1)} %broadcast_in_dim.3), channel_id=1, replica_groups=mesh['zh'=4,'core'=2,'zl'=2,'y'=4,'x'=4] {'zl','y','x'}, dimensions={0} | all-to-all | bytes 2097152 | tf_op jit(solution)/shard_map/all_to_all | solution.py:504
  164.5 1.0 shard_map.69
  (11 shorter events, 0.0 us)
Async XLA Ops:
  0.0 4.4 %collective-permute-start = (bf16[1024,1024]{1,0:T(8,128)(2,1)}, bf16[1024,1024]{1,0:T(8,128)(2,1)S(1)}, u32[]{:S(2)}, u32[]{:S(2)}) collective-permute-start(bf16[1024,1024]{1,0:T(8,128)(2,1)} %bitcast.7), channel_id=1, source_target_pairs={{0,32},{32,0},{1,33},{33,1},{2,34},{34,2},{3,35},{35,3},{4,36},{36... | collective-permute-start | bytes 6291464 | tf_op jit(solution)/shard_map/ppermute | solution.py:477
  4.4 1.6 copy-start
  14.2 27.8 %collective-permute-start.4 = (s16[1040,1024]{1,0:T(8,128)(2,1)}, s16[1040,1024]{1,0:T(8,128)(2,1)S(1)}, u32[]{:S(2)}, u32[]{:S(2)}) collective-permute-start(s16[1040,1024]{1,0:T(8,128)(2,1)} %shard_map.61), channel_id=1, source_target_pairs={{0,3},{1,2},{2,1},{3,0},{4,7},{5,6},{6,5},{7,4},{8,11},{9,10},{10,... | collective-permute-start | bytes 6389768 | tf_op jit(solution)/shard_map/ppermute | solution.py:54
  23.8 26.5 %collective-permute-start.1 = (s16[1040,1024]{1,0:T(8,128)(2,1)S(1)}, s16[1040,1024]{1,0:T(8,128)(2,1)S(1)}, u32[]{:S(2)}, u32[]{:S(2)}) collective-permute-start(s16[1040,1024]{1,0:T(8,128)(2,1)S(1)} %shard_map.56), channel_id=1, source_target_pairs={{0,1},{1,0},{2,3},{3,2},{4,5},{5,4},{6,7},{7,6},{8,9},{9,8},{10,11... | collective-permute-start | bytes 6389768 | tf_op jit(solution)/shard_map/ppermute | solution.py:54
  42.0 1.4 copy-start.1
  43.3 1.6 copy-start.2
  46.9 16.4 %collective-permute-start.5 = (s16[528,1024]{1,0:T(8,128)(2,1)S(1)}, s16[528,1024]{1,0:T(8,128)(2,1)S(1)}, u32[]{:S(2)}, u32[]{:S(2)}) collective-permute-start(s16[528,1024]{1,0:T(8,128)(2,1)S(1)} %get-tuple-element.33), channel_id=1, source_target_pairs={{0,12},{1,13},{2,14},{3,15},{4,8},{5,9},{6,10},{7,11},{8,4},{9,5},... | collective-permute-start | bytes 3244040 | tf_op jit(solution)/shard_map/ppermute | solution.py:54
  52.2 17.3 %collective-permute-start.2 = (s16[528,1024]{1,0:T(8,128)(2,1)S(1)}, s16[528,1024]{1,0:T(8,128)(2,1)S(1)}, u32[]{:S(2)}, u32[]{:S(2)}) collective-permute-start(s16[528,1024]{1,0:T(8,128)(2,1)S(1)} %get-tuple-element.28), channel_id=1, source_target_pairs={{0,4},{1,5},{2,6},{3,7},{4,0},{5,1},{6,2},{7,3},{8,12},{9,13},{10,... | collective-permute-start | bytes 3244040 | tf_op jit(solution)/shard_map/ppermute | solution.py:54
  64.6 9.6 %collective-permute-start.6 = (s16[272,1024]{1,0:T(8,128)(2,1)S(1)}, s16[272,1024]{1,0:T(8,128)(2,1)S(1)}, u32[]{:S(2)}, u32[]{:S(2)}) collective-permute-start(s16[272,1024]{1,0:T(8,128)(2,1)S(1)} %get-tuple-element.35), channel_id=1, source_target_pairs={{0,1},{1,0},{2,3},{3,2},{4,5},{5,4},{6,7},{7,6},{8,9},{9,8},{10,11... | collective-permute-start | bytes 1671176 | tf_op jit(solution)/shard_map/ppermute | solution.py:54
  70.8 10.8 %collective-permute-start.3 = (s16[272,1024]{1,0:T(8,128)(2,1)S(1)}, s16[272,1024]{1,0:T(8,128)(2,1)S(1)}, u32[]{:S(2)}, u32[]{:S(2)}) collective-permute-start(s16[272,1024]{1,0:T(8,128)(2,1)S(1)} %get-tuple-element.30), channel_id=1, source_target_pairs={{0,3},{1,2},{2,1},{3,0},{4,7},{5,6},{6,5},{7,4},{8,11},{9,10},{10,... | collective-permute-start | bytes 1671176 | tf_op jit(solution)/shard_map/ppermute | solution.py:54
  75.2 10.2 %collective-permute-start.8 = (s16[144,1024]{1,0:T(8,128)(2,1)S(1)}, s16[144,1024]{1,0:T(8,128)(2,1)S(1)}, u32[]{:S(2)}, u32[]{:S(2)}) collective-permute-start(s16[144,1024]{1,0:T(8,128)(2,1)S(1)} %get-tuple-element.38), channel_id=1, source_target_pairs={{0,4},{1,5},{2,6},{3,7},{4,0},{5,1},{6,2},{7,3},{8,12},{9,13},{10,... | collective-permute-start | bytes 884744 | tf_op jit(solution)/shard_map/ppermute | solution.py:54
  82.5 57.1 %copy-start.3 = (s32[8,8]{1,0:T(8,128)S(1)}, s32[8,8]{1,0:T(8,128)}, u32[]{:S(2)}) copy-start(s32[8,8]{1,0:T(8,128)} %flags_ref.1) | copy-start | bytes 772
  82.5 57.1 %copy-start.4 = (s32[8]{0:T(128)S(1)}, s32[8]{0:T(128)}, u32[]{:S(2)}) copy-start(s32[8]{0:T(128)} %order_ref.1) | copy-start | bytes 100
  82.5 8.0 %collective-permute-start.7 = (s16[144,1024]{1,0:T(8,128)(2,1)S(1)}, s16[144,1024]{1,0:T(8,128)(2,1)S(1)}, u32[]{:S(2)}, u32[]{:S(2)}) collective-permute-start(s16[144,1024]{1,0:T(8,128)(2,1)S(1)} %get-tuple-element.37), channel_id=1, source_target_pairs={{0,12},{1,13},{2,14},{3,15},{4,8},{5,9},{6,10},{7,11},{8,4},{9,5},... | collective-permute-start | bytes 884744 | tf_op jit(solution)/shard_map/ppermute | solution.py:54
  91.4 8.3 %collective-permute-start.9 = (s16[144,1024]{1,0:T(8,128)(2,1)S(1)}, s16[144,1024]{1,0:T(8,128)(2,1)S(1)}, u32[]{:S(2)}, u32[]{:S(2)}) collective-permute-start(s16[144,1024]{1,0:T(8,128)(2,1)S(1)} %get-tuple-element.40), channel_id=1, source_target_pairs={{0,16},{1,17},{2,18},{3,19},{4,20},{5,21},{6,22},{7,23},{8,24},{9,... | collective-permute-start | bytes 884744 | tf_op jit(solution)/shard_map/ppermute | solution.py:54
  100.5 12.3 %collective-permute-start.10 = (s16[144,256]{1,0:T(8,128)(2,1)S(1)}, s16[144,256]{1,0:T(8,128)(2,1)S(1)}, u32[]{:S(2)}, u32[]{:S(2)}) collective-permute-start(s16[144,256]{1,0:T(8,128)(2,1)S(1)} %get-tuple-element.42), channel_id=1, source_target_pairs={{0,64},{64,128},{128,192},{192,0},{1,65},{65,129},{129,193},{193,1... | collective-permute-start | bytes 221192 | tf_op jit(solution)/shard_map/ppermute | solution.py:494
  104.8 8.4 %collective-permute-start.11 = (s16[144,256]{1,0:T(8,128)(2,1)S(1)}, s16[144,256]{1,0:T(8,128)(2,1)S(1)}, u32[]{:S(2)}, u32[]{:S(2)}) collective-permute-start(s16[144,256]{1,0:T(8,128)(2,1)S(1)} %get-tuple-element.43), channel_id=1, source_target_pairs={{0,128},{64,192},{128,0},{192,64},{1,129},{65,193},{129,1},{193,65... | collective-permute-start | bytes 221192 | tf_op jit(solution)/shard_map/ppermute | solution.py:494
  108.9 6.0 %collective-permute-start.12 = (s16[144,256]{1,0:T(8,128)(2,1)S(1)}, s16[144,256]{1,0:T(8,128)(2,1)S(1)}, u32[]{:S(2)}, u32[]{:S(2)}) collective-permute-start(s16[144,256]{1,0:T(8,128)(2,1)S(1)} %get-tuple-element.44), channel_id=1, source_target_pairs={{0,192},{64,0},{128,64},{192,128},{1,193},{65,1},{129,65},{193,129... | collective-permute-start | bytes 221192 | tf_op jit(solution)/shard_map/ppermute | solution.py:494
  141.6 1.3 collective-permute-start.13

commit v2 on v1

v2 whole, which is shorter than its diff:
```python
import itertools

import jax
import jax.numpy as jnp
import numpy as np
from jax import lax
from jax.experimental import pallas as pl
from jax.experimental.pallas import tpu as pltpu
from jax.sharding import Mesh
from jax.sharding import PartitionSpec as P

AXES = ("zh", "core", "zl", "y", "x")
SIZES = (4, 2, 2, 4, 4)
DP = ("zl", "y", "x")
TASK = ("zh", "core")
F32, BF16, I16, I32 = jnp.float32, jnp.bfloat16, jnp.int16, jnp.int32

PARTNER = {"a": (1, 0, 3, 2), "b": (3, 2, 1, 0)}
BIT = {"a": (0, 1, 1, 0), "b": (0, 0, 1, 1)}
ORDER = {
    (0, 0): ("xa", "yb", "xb", "ya", "z"),
    (0, 1): ("yb", "xa", "ya", "xb", "z"),
    (1, 0): ("ya", "xb", "xa", "yb", "z"),
    (1, 1): ("xb", "ya", "yb", "xa", "z"),
}
FULL = 32000.0
STEPS = 64.0
EXTRA = 16


def coordinates():
    return [dict(zip(AXES, v)) for v in itertools.product(*map(range, SIZES))]


def linear(co):
    index = 0
    for axis, size in zip(AXES, SIZES):
        index = index * size + co[axis]
    return index


def bit_of(co, dim):
    return co["zl"] if dim == "z" else BIT[dim[1]][co[dim[0]]]


def partner(co, dim):
    if dim == "z":
        return {**co, "zl": 1 - co["zl"]}
    return {**co, dim[0]: PARTNER[dim[1]][co[dim[0]]]}


def swap_along(value, dims):
    pairs = [(linear(co), linear(partner(co, dims[co["core"]]))) for co in coordinates()]
    return lax.ppermute(value, AXES, pairs)


def position(co, core, chunk):
    place = 0
    for dim in ORDER[core, chunk]:
        place = 2 * place + bit_of(co, dim)
    return place


def device_table():
    rows = []
    for co in coordinates():
        core = co["core"]
        row = [core, co["zh"]]
        for chunk in range(2):
            bits = [bit_of(co, dim) for dim in ORDER[core, chunk]]
            row += bits + [0]
        rows.append(row + [0] * (16 - len(row)))
    return np.asarray(rows, np.int32)


def encode(tile):
    top = jnp.maximum(jnp.max(jnp.abs(tile), axis=0, keepdims=True), 1e-30)
    code = jnp.ceil(jnp.log(top) * STEPS)
    values = jnp.round(tile * (jnp.exp(code * (-1.0 / STEPS)) * FULL))
    return values.astype(I32).astype(I16), code


def scales(codes):
    return jnp.exp(codes.astype(I32).astype(F32) * (1.0 / STEPS)) * (1.0 / FULL)


def floats(values):
    return values.astype(I32).astype(F32)


def params(mib=14):
    return pltpu.CompilerParams(vmem_limit_bytes=mib << 20)


def call(kernel, scalars, grid, inputs, in_specs, out_shape, out_specs, scratch, flops, nbytes, **extra):
    return pl.pallas_call(
        kernel,
        out_shape=out_shape,
        grid_spec=pltpu.PrefetchScalarGridSpec(
            num_scalar_prefetch=1,
            grid=grid,
            in_specs=in_specs,
            out_specs=out_specs,
            scratch_shapes=scratch,
        ),
        compiler_params=params(),
        cost_estimate=pl.CostEstimate(flops=flops, bytes_accessed=nbytes, transcendentals=0),
        **extra,
    )(scalars, *inputs)


def whole(shape):
    return pl.BlockSpec(shape, lambda *_: (0,) * len(shape))


ROWS = 512
TILE = 128


def encode_kernel(s_ref, term_ref, out_ref, codes):
    tile = pl.program_id(0)
    values, code = encode(term_ref[...])
    out_ref[pl.ds(pl.multiple_of(tile * TILE, TILE), TILE), :] = values
    codes[pl.ds(tile, 1), :] = code

    @pl.when(tile == ROWS // TILE - 1)
    def _():
        out_ref[ROWS:, :] = codes[...].astype(I32).astype(I16)


def encode_term(table, slot, term):
    rows, width = ROWS, term.shape[1]
    per = rows // TILE
    return call(
        encode_kernel,
        table,
        (per,),
        (term,),
        [pl.BlockSpec((TILE, width), lambda n, s: ((1 - s[slot]) * per + n, 0))],
        jax.ShapeDtypeStruct((rows + EXTRA, width), I16),
        whole((rows + EXTRA, width)),
        [pltpu.VMEM((EXTRA, width), F32)],
        8 * rows * width,
        6 * rows * width,
    )


def term_of(inputs, start, cot):
    part = lax.dynamic_slice(inputs, (0, start), (inputs.shape[0], 2 * ROWS))
    return lax.dot_general(part, cot, (((0,), (0,)), ((), ())), preferred_element_type=F32)


def after(value, *others):
    return lax.optimization_barrier((value, *others))[0]


def level(table, slot, kept, arrived, first=None):
    tasks, rows, width = kept.shape
    rows = rows if first is None else rows // 2
    half = rows // 2
    tile = min(TILE, half)
    per = half // tile
    code_rows = min(TILE, rows)

    def skip(s):
        return 0 if first is None else s[first] * 2 * per

    def kernel(s_ref, keep_ref, give_ref, keep_in, give_in, codes_ref, sum_ref, out_ref, scale, codes):
        task, j = pl.program_id(0), pl.program_id(1)
        bit = s_ref[slot]

        @pl.when((task == 0) & (j == 0))
        def _():
            scale[...] = scales(codes_ref[...])
            codes[...] = jnp.zeros_like(codes)

        def row_of(side):
            return (task * rows + side * half + j * tile) // code_rows

        give = give_ref[0] + floats(give_in[...]) * scale[pl.ds(row_of(1 - bit), 1), :]
        values, code = encode(give)
        at = task * per + j
        out_ref[pl.ds(pl.multiple_of(at * tile, tile), tile), :] = values
        codes[pl.ds(at, 1), :] = code
        sum_ref[0] = keep_ref[0] + floats(keep_in[...]) * scale[pl.ds(row_of(bit), 1), :]

        @pl.when((task == tasks - 1) & (j == per - 1))
        def _():
            out_ref[tasks * half :, :] = codes[...].astype(I32).astype(I16)

    return call(
        kernel,
        table,
        (tasks, per),
        (kept, kept, arrived, arrived, arrived),
        [
            pl.BlockSpec((1, tile, width), lambda t, j, s: (t, skip(s) + s[slot] * per + j, 0)),
            pl.BlockSpec((1, tile, width), lambda t, j, s: (t, skip(s) + (1 - s[slot]) * per + j, 0)),
            pl.BlockSpec((tile, width), lambda t, j, s: ((2 * t + s[slot]) * per + j, 0)),
            pl.BlockSpec((tile, width), lambda t, j, s: ((2 * t + 1 - s[slot]) * per + j, 0)),
            pl.BlockSpec((EXTRA, width), lambda t, j, s: (tasks * rows // EXTRA, 0)),
        ],
        (
            jax.ShapeDtypeStruct((tasks, half, width), F32),
            jax.ShapeDtypeStruct((tasks * half + EXTRA, width), I16),
        ),
        (pl.BlockSpec((1, tile, width), lambda t, j, s: (t, j, 0)), whole((tasks * half + EXTRA, width))),
        [pltpu.VMEM((EXTRA, width), F32), pltpu.VMEM((EXTRA, width), F32)],
        8 * tasks * rows * width,
        tasks * rows * width * 9,
    )


def join_tasks(table, slot, kept, arrived):
    _, rows, width = kept[0].shape
    half = rows // 2

    def kernel(s_ref, keep_a, keep_b, in_a, in_b, sum_ref, out_ref, scale):
        bit = s_ref[slot]
        out_codes = []
        for task, (keep, arr) in enumerate(((keep_a, in_a), (keep_b, in_b))):
            scale[...] = scales(arr[rows:, :])

            def part(side):
                at = pl.ds(pl.multiple_of(side * half, half), half)
                return keep[0, at, :] + floats(arr[at, :]) * scale[pl.ds(side * half // TILE, 1), :]

            values, code = encode(part(1 - bit))
            out_ref[task * half : (task + 1) * half, :] = values
            out_codes.append(code)
            sum_ref[task] = part(bit)
        out_codes.append(jnp.zeros((EXTRA - 2, width), F32))
        out_ref[2 * half :, :] = jnp.concatenate(out_codes, axis=0).astype(I32).astype(I16)

    shapes = ((1, rows, width), (1, rows, width), (rows + EXTRA, width), (rows + EXTRA, width))
    return call(
        kernel,
        table,
        (1,),
        (*kept, *arrived),
        [whole(s) for s in shapes],
        (jax.ShapeDtypeStruct((2, half, width), F32), jax.ShapeDtypeStruct((2 * half + EXTRA, width), I16)),
        (whole((2, half, width)), whole((2 * half + EXTRA, width))),
        [pltpu.VMEM((EXTRA, width), F32)],
        16 * rows * width,
        2 * rows * width * 9,
    )


def line_blocks(kept, arrived):
    _, rows, width = kept[0].shape
    half, wide = rows // 2, width // 4

    def kernel(keep_a, keep_b, in_a, in_b, out_ref, total):
        for chunk, (keep, arr) in enumerate(((keep_a, in_a), (keep_b, in_b))):
            scale = scales(arr[2 * rows :, :])
            for task in range(2):
                values = floats(arr[task * rows : (task + 1) * rows, :])
                total[2 * chunk + task] = keep[task] + values * scale[task : task + 1]
        for side in range(2):
            out_codes = []
            for n in range(4):
                values, code = encode(total[n, side * half : (side + 1) * half, :])
                for zh in range(4):
                    out_ref[2 * zh + side, n * half : (n + 1) * half, :] = values[:, zh * wide : (zh + 1) * wide]
                out_codes.append(code)
            out_codes.append(jnp.zeros((EXTRA - 4, width), F32))
            codes = jnp.concatenate(out_codes, axis=0).astype(I32).astype(I16)
            for zh in range(4):
                out_ref[2 * zh + side, 4 * half :, :] = codes[:, zh * wide : (zh + 1) * wide]

    return pl.pallas_call(
        kernel,
        out_shape=jax.ShapeDtypeStruct((8, 4 * half + EXTRA, wide), I16),
        scratch_shapes=[pltpu.VMEM((4, rows, width), F32)],
        compiler_params=params(),
        cost_estimate=pl.CostEstimate(flops=32 * rows * width, bytes_accessed=36 * rows * width, transcendentals=0),
    )(*kept, *arrived)


def lanes(shape, dim):
    return lax.broadcasted_iota(I32, shape, dim)


def gram_kernel(s_ref, in_ref, grads_ref, gram_ref):
    core = s_ref[0]
    rows = (in_ref.shape[1] - EXTRA) // 4
    for zh in range(4):
        near, far = scales(in_ref[2 * zh, 4 * rows :, :]), scales(in_ref[2 * zh + 1, 4 * rows :, :])
        for n in range(4):
            chunk, task = n // 2, n % 2
            at = slice(n * rows, (n + 1) * rows)
            value = floats(in_ref[2 * zh, at, :]) * near[n : n + 1]
            value = value + floats(in_ref[2 * zh + 1, at, :]) * far[n : n + 1]
            mine = 2 * zh + (task + core - 2 * task * core)
            grads_ref[mine, chunk * rows : (chunk + 1) * rows, :] = value

    grads = [grads_ref[t] for t in range(8)]
    lane, sub = lanes((8, 128), 1), lanes((8, 128), 0)
    matrix = jnp.zeros((8, 128), F32)
    for s in range(8):
        for t in range(s, 8):
            product = grads[s] * grads[t]
            folded = product[:, :128] + product[:, 128:]
            total = jnp.sum(jnp.sum(folded, axis=0, keepdims=True), axis=1, keepdims=True)
            here = ((sub == s) & (lane == t)) | ((sub == t) & (lane == s))
            matrix = jnp.where(here, total, matrix)
    line = jnp.zeros((8, 128), F32)
    for s in range(8):
        row = jnp.where(sub == s, matrix, 0.0)
        line = line + (row if s == 0 else pltpu.roll(row, 8 * s, 1))
    flat = jnp.sum(line, axis=0, keepdims=True)
    gram_ref[...] = jnp.broadcast_to(flat, gram_ref.shape)


def gram(table, arrived):
    _, rows, wide = arrived.shape
    rows = (rows - EXTRA) // 2
    return call(
        gram_kernel,
        table,
        (1,),
        (arrived,),
        [whole(arrived.shape)],
        (jax.ShapeDtypeStruct((8, rows, wide), F32), jax.ShapeDtypeStruct((256, 128), F32)),
        (whole((8, rows, wide)), whole((256, 128))),
        [],
        160 * rows * wide,
        32 * rows * wide,
    )


def combine_kernel(s_ref, order_ref, flags_ref, gram_ref, grads_ref, mine_ref, give_ref):
    core = s_ref[0]
    lane, sub = lanes((8, 128), 1), lanes((8, 128), 0)
    flat = jnp.broadcast_to(jnp.sum(gram_ref[...], axis=0, keepdims=True), (8, 128))
    matrix = jnp.zeros((8, 128), F32)
    for s in range(8):
        row = flat if s == 0 else pltpu.roll(flat, 128 - 8 * s, 1)
        matrix = jnp.where((sub == s) & (lane < 8), row, matrix)
    flags = flags_ref[...].astype(F32)
    small = lanes((8, 8), 1)
    coefficients = jnp.where(lane == sub, 1.0, 0.0)
    for k in range(8):
        target = order_ref[k]
        row = jnp.sum(jnp.where(sub == target, matrix, 0.0), axis=0, keepdims=True)
        dots = jnp.sum(coefficients * row, axis=1, keepdims=True)
        square = jnp.sum(jnp.where(lane[:1] == target, row, 0.0), axis=1, keepdims=True)
        active = jnp.sum(jnp.where(small == target, flags, 0.0), axis=1, keepdims=True)
        active = jnp.where(sub[:, :1] == target, 0.0, active)
        removed = jnp.minimum(dots, 0.0) / square * active
        coefficients = coefficients - jnp.where(lane == target, removed, 0.0)
    weights = jnp.sum(coefficients, axis=0, keepdims=True)
    total = None
    for t in range(8):
        weight = jnp.sum(jnp.where(lane[:1] == t, weights, 0.0), axis=1, keepdims=True)
        term = weight * grads_ref[t]
        total = term if total is None else total + term
    left, right = total[:, :128].astype(BF16), total[:, 128:].astype(BF16)

    @pl.when(core == 0)
    def _():
        mine_ref[...] = left
        give_ref[...] = right

    @pl.when(core == 1)
    def _():
        mine_ref[...] = right
        give_ref[...] = left


def combine(table, order, flags, grams, grads):
    rows = grads.shape[1]
    part = jax.ShapeDtypeStruct((rows, 128), BF16)
    return call(
        combine_kernel,
        table,
        (1,),
        (order, flags, grams, grads),
        [pl.BlockSpec(memory_space=pltpu.SMEM), whole((8, 8)), whole((256, 128)), whole(grads.shape)],
        (part, part),
        (whole((rows, 128)),) * 2,
        [],
        20 * rows * 256,
        40 * rows * 256,
    )


def place_kernel(in_ref, out_ref):
    rows = in_ref.shape[1] // 4
    for index, (zl, y, x) in enumerate(itertools.product(range(2), range(4), range(4))):
        co = {"zl": zl, "y": y, "x": x}
        for n in range(4):
            at = (n * 32 + position(co, n // 2, n % 2)) * rows
            out_ref[at : at + rows, :] = in_ref[index, n * rows : (n + 1) * rows, :]


def place(gathered):
    count, rows, cols = gathered.shape
    return pl.pallas_call(
        place_kernel,
        out_shape=jax.ShapeDtypeStruct((count * rows, cols), BF16),
        compiler_params=params(),
        cost_estimate=pl.CostEstimate(flops=0, bytes_accessed=4 * count * rows * cols, transcendentals=0),
    )(gathered)


def on_device(inputs, cotangent, task_order, conflict_flags):
    table = jnp.asarray(device_table())[lax.axis_index(AXES)]
    core = lax.axis_index("core")
    own = cotangent[0]
    other = lax.ppermute(own, "core", [(0, 1), (1, 0)])

    dims = [[(ORDER[0, chunk][n], ORDER[1, chunk][n]) for n in range(5)] for chunk in range(2)]
    slots = [2, 8]
    keys = [(task, chunk) for task in range(2) for chunk in range(2)]
    cots = (own, other)
    arrived, kept = {}, {}
    terms = {}
    for task, chunk in keys:
        start = (2 * core + chunk) * 2 * ROWS
        cot = cots[task] if not terms else after(cots[task], coded)
        terms[task, chunk] = term_of(inputs, start, cot)
        coded = encode_term(table, slots[chunk], terms[task, chunk])
        arrived[task, chunk] = swap_along(coded, dims[chunk][0])
    for at in keys:
        chunk = at[1]
        kept[at], coded = level(table, slots[chunk] + 1, terms[at][None], arrived[at], slots[chunk])
        arrived[at] = swap_along(coded, dims[chunk][1])
    joined, taken = [], []
    for chunk in range(2):
        pair = [(task, chunk) for task in range(2)]
        summed, coded = join_tasks(
            table, slots[chunk] + 2, [kept[at] for at in pair], [arrived[at] for at in pair]
        )
        joined.append(summed)
        taken.append(swap_along(coded, dims[chunk][2]))
    for chunk in range(2):
        joined[chunk], coded = level(table, slots[chunk] + 3, joined[chunk], taken[chunk])
        taken[chunk] = swap_along(coded, dims[chunk][3])
    blocks = line_blocks(joined, taken)
    blocks = lax.all_to_all(blocks, ("zh", "zl"), split_axis=0, concat_axis=0, tiled=True)
    grads, grams = gram(table, blocks)
    grams = lax.all_to_all(grams, AXES, split_axis=0, concat_axis=0, tiled=True)
    mine, give = combine(table, task_order, conflict_flags, grams, grads)
    taken = lax.ppermute(give, "core", [(0, 1), (1, 0)])
    first = jnp.where(core == 0, mine, taken)
    second = jnp.where(core == 0, taken, mine)
    block = jnp.concatenate([first, second], axis=0)
    copies = jnp.broadcast_to(block, (32, *block.shape))
    gathered = lax.all_to_all(copies, DP, split_axis=0, concat_axis=0, tiled=True)
    return place(gathered)


def solution(mesh):
    split = Mesh(mesh.devices.reshape(SIZES), AXES)
    placed = (P(DP, None), P(TASK, DP, None), P(), P())
    return jax.shard_map(
        on_device, mesh=split, in_specs=placed, out_specs=P(None, TASK), check_vma=False
    )
```

time: 166 us -> 149 us (0.90)
  Pallas kernels: 42.9 us -> 17.9 us
  matrix products: 0 us -> 18.7 us
  blocking collectives: 45.1 us -> 60.9 us
  waiting for transfers between devices: 45.7 us -> 34.2 us
  starting transfers between devices: 26.1 us -> 14.8 us
  local copies, waits for them, and re-layouts: 5.48 us -> 2.45 us
    pallas_call x14, Pallas kernels: 41.9 us -> 16.4 us  [call(): pl.pallas_call(kernel, out_shape=out_shape, grid_spec=pltpu.PrefetchScala...]
    all_to_all x0 -> x1, blocking collectives: none -> 20.9 us  [on_device(): lax.all_to_all(blocks, ('zh', 'zl'), split_axis=0, concat_axis=0, tiled=T...]
    dot_general x0 -> x4, matrix products: none -> 18.7 us  [term_of(): lax.dot_general(part, cot, (((0,), (0,)), ((), ())), preferred_element_ty...]
    ppermute x3 -> x0, starting transfers between devices: 12.3 us -> none  [on_device(): lax.ppermute(value, 'zh', [(i, (i + k) % 4) for i in range(4)])]
    ppermute x9 -> x12, waiting for transfers between devices: 38.9 us -> 33 us  [swap_along(): return lax.ppermute(value, AXES, pairs)]
    all_to_all x1, blocking collectives: 23.8 us -> 18.7 us  [on_device(): grams = lax.all_to_all(grams, AXES, split_axis=0, concat_axis=0, tiled=True)]
    ppermute x1, waiting for transfers between devices: 3.68 us -> 0.01 us  [on_device(): other = lax.ppermute(own, 'core', [(0, 1), (1, 0)])]
    unnamed x10 -> x8, local copies, waits for them, and re-layouts: 4.56 us -> 1.53 us
  transfers between devices with their start and end apart: 14 -> 14, of which waited for: 12 -> 9; matrix products, arithmetic and copies ran while one was open for 0% -> 13% of each run, Pallas kernels for 18% -> 9%
where the time goes in v2:
time: 149 us
  blocking collectives  60.9 us (41%)
  waiting for transfers between devices  34.2 us (23%)
  matrix products  18.7 us (13%)
  Pallas kernels  17.9 us (12%)
  starting transfers between devices  14.8 us (10%)
  local copies, waits for them, and re-layouts  2.45 us (2%)
    ppermute x12, waiting for transfers between devices, swap_along(): return lax.ppermute(value, AXES, pairs)  33 us
    all_to_all x1, blocking collectives, on_device(): lax.all_to_all(copies, DP, split_axis=0, concat_axis=0, tiled=True)  21.3 us
    all_to_all x1, blocking collectives, on_device(): lax.all_to_all(blocks, ('zh', 'zl'), split_axis=0, concat_axis=0, tiled=T...  20.9 us
    all_to_all x1, blocking collectives, on_device(): grams = lax.all_to_all(grams, AXES, split_axis=0, concat_axis=0, tiled=True)  18.7 us
    dot_general x4, matrix products, term_of(): lax.dot_general(part, cot, (((0,), (0,)), ((), ())), preferred_element_ty...  18.7 us
    pallas_call x14, Pallas kernels, call(): pl.pallas_call(kernel, out_shape=out_shape, grid_spec=pltpu.PrefetchScala...  16.4 us
    ppermute x12, starting transfers between devices, swap_along(): return lax.ppermute(value, AXES, pairs)  14.7 us
  transfers between devices with their start and end apart: 14, of which 9 were waited for; matrix products, arithmetic and copies ran while one was open for 13% of the time, Pallas kernels for 9%

profile of v2, /device:TPU:32, one launch (start us, length us, event | category | flops | bytes accessed | tf_op | source)
XLA Modules:
  0.0 149.0 jit_solution(15645524519516533270)
XLA Ops:
  0.0 0.7 fusion.12.s_ref
  0.7 4.7 %fusion.6.term_ref = f32[1024,1024]{1,0:T(8,128)S(1)} fusion(bf16[1024,4096]{1,0:T(8,128)(2,1)} %param.5, s32[]{:T(128)S(6)} %select_n.25, bf16[1,1024,1024]{2,1,0:T(8,128)(2,1)} %param.6), kind=kOutput, calls=%fused_computation.6 | convolution fusion | flops 2147483648 | bytes 8388612 | tf_op jit(solution)/shard_map/dot_general | solution.py:150
  5.4 1.0 shard_map.55
  6.4 0.9 copy-done
  7.3 1.5 %collective-permute-start = (s16[528,1024]{1,0:T(8,128)(2,1)S(1)}, s16[528,1024]{1,0:T(8,128)(2,1)S(1)}, u32[]{:S(2)}, u32[]{:S(2)}) collective-permute-start(s16[528,1024]{1,0:T(8,128)(2,1)S(1)} %shard_map.55), channel_id=1, source_target_pairs={{0,1},{1,0},{2,3},{3,2},{4,5},{5,4},{6,7},{7,6},{8,9},{9,8},{10,11... | collective-permute-start | bytes 3244040 | tf_op jit(solution)/shard_map/ppermute | solution.py:54
  8.8 4.7 %fusion.2.term_ref = f32[1024,1024]{1,0:T(8,128)S(1)} fusion(bf16[1024,1024]{1,0:T(8,128)(2,1)} %bitcast.27, bf16[1024,4096]{1,0:T(8,128)(2,1)} %param.5, s32[]{:T(128)S(6)} %select_n.26), kind=kOutput, calls=%fused_computation.2 | convolution fusion | flops 2147483648 | bytes 8388612 | tf_op jit(solution)/shard_map/dot_general | solution.py:150
  13.5 1.0 shard_map.57
  14.5 3.1 %collective-permute-start.6 = (s16[528,1024]{1,0:T(8,128)(2,1)S(1)}, s16[528,1024]{1,0:T(8,128)(2,1)S(1)}, u32[]{:S(2)}, u32[]{:S(2)}) collective-permute-start(s16[528,1024]{1,0:T(8,128)(2,1)S(1)} %shard_map.57), channel_id=1, source_target_pairs={{0,12},{1,13},{2,14},{3,15},{4,8},{5,9},{6,10},{7,11},{8,4},{9,5},... | collective-permute-start | bytes 3244040 | tf_op jit(solution)/shard_map/ppermute | solution.py:54
  17.6 4.7 %fusion.4.term_ref = f32[1024,1024]{1,0:T(8,128)S(1)} fusion(bf16[1024,1024]{1,0:T(8,128)(2,1)} %collective-permute-done.1, bf16[1024,4096]{1,0:T(8,128)(2,1)} %param.5, s32[]{:T(128)S(6)} %select_n.25), kind=kOutput, calls=%fused_computation.4 | convolution fusion | flops 2147483648 | bytes 8388612 | tf_op jit(solution)/shard_map/dot_general | solution.py:150
  22.3 1.0 shard_map.58
  23.4 0.6 collective-permute-start.2
  24.0 4.7 %fusion.term_ref = f32[1024,1024]{1,0:T(8,128)S(1)} fusion(bf16[1024,1024]{1,0:T(8,128)(2,1)} %collective-permute-done.1, bf16[1024,4096]{1,0:T(8,128)(2,1)} %param.5, s32[]{:T(128)S(6)} %select_n.26), kind=kOutput, calls=%fused_computation | convolution fusion | flops 2147483648 | bytes 8388612 | tf_op jit(solution)/shard_map/dot_general | solution.py:150
  28.7 1.0 shard_map.63
  29.7 0.5 collective-permute-start.7
  30.2 0.6 copy-done.1
  30.8 1.2 shard_map.56
  32.1 2.5 %collective-permute-start.3 = (s16[272,1024]{1,0:T(8,128)(2,1)S(1)}, s16[272,1024]{1,0:T(8,128)(2,1)S(1)}, u32[]{:S(2)}, u32[]{:S(2)}) collective-permute-start(s16[272,1024]{1,0:T(8,128)(2,1)S(1)} %get-tuple-element.32), channel_id=1, source_target_pairs={{0,12},{1,13},{2,14},{3,15},{4,8},{5,9},{6,10},{7,11},{8,4},{9,5},... | collective-permute-start | bytes 1671176 | tf_op jit(solution)/shard_map/ppermute | solution.py:54
  34.6 1.2 shard_map.62
  35.8 2.8 %collective-permute-done.2.keep_in.give_in.codes_ref = s16[528,1024]{1,0:T(8,128)(2,1)S(1)} collective-permute-done((s16[528,1024]{1,0:T(8,128)(2,1)S(1)}, s16[528,1024]{1,0:T(8,128)(2,1)S(1)}, u32[]{:S(2)}, u32[]{:S(2)}) %collective-permute-start.2) | collective-permute-done | bytes 1081376 | tf_op jit(solution)/shard_map/ppermute | solution.py:54
  38.6 1.2 shard_map.59
  39.8 0.3 collective-permute-start.4
  40.1 0.5 collective-permute-start.8
  40.7 5.7 %collective-permute-done.7.keep_in.give_in.codes_ref = s16[528,1024]{1,0:T(8,128)(2,1)S(1)} collective-permute-done((s16[528,1024]{1,0:T(8,128)(2,1)S(1)}, s16[528,1024]{1,0:T(8,128)(2,1)S(1)}, u32[]{:S(2)}, u32[]{:S(2)}) %collective-permute-start.7) | collective-permute-done | bytes 1081376 | tf_op jit(solution)/shard_map/ppermute | solution.py:54
  46.4 1.2 shard_map.64
  47.6 1.6 %collective-permute-start.9 = (s16[272,1024]{1,0:T(8,128)(2,1)S(1)}, s16[272,1024]{1,0:T(8,128)(2,1)S(1)}, u32[]{:S(2)}, u32[]{:S(2)}) collective-permute-start(s16[272,1024]{1,0:T(8,128)(2,1)S(1)} %get-tuple-element.41), channel_id=1, source_target_pairs={{0,1},{1,0},{2,3},{3,2},{4,5},{5,4},{6,7},{7,6},{8,9},{9,8},{10,11... | collective-permute-start | bytes 1671176 | tf_op jit(solution)/shard_map/ppermute | solution.py:54
  49.2 3.1 %collective-permute-done.3.in_a = s16[272,1024]{1,0:T(8,128)(2,1)S(1)} collective-permute-done((s16[272,1024]{1,0:T(8,128)(2,1)S(1)}, s16[272,1024]{1,0:T(8,128)(2,1)S(1)}, u32[]{:S(2)}, u32[]{:S(2)}) %collective-permute-start.3) | collective-permute-done | bytes 557088 | tf_op jit(solution)/shard_map/ppermute | solution.py:54
  52.3 6.0 %collective-permute-done.4.in_b = s16[272,1024]{1,0:T(8,128)(2,1)S(1)} collective-permute-done((s16[272,1024]{1,0:T(8,128)(2,1)S(1)}, s16[272,1024]{1,0:T(8,128)(2,1)S(1)}, u32[]{:S(2)}, u32[]{:S(2)}) %collective-permute-start.4) | collective-permute-done | bytes 557088 | tf_op jit(solution)/shard_map/ppermute | solution.py:54
  58.3 1.2 shard_map.60
  59.5 2.8 %collective-permute-start.5 = (s16[272,1024]{1,0:T(8,128)(2,1)S(1)}, s16[272,1024]{1,0:T(8,128)(2,1)S(1)}, u32[]{:S(2)}, u32[]{:S(2)}) collective-permute-start(s16[272,1024]{1,0:T(8,128)(2,1)S(1)} %get-tuple-element.35), channel_id=1, source_target_pairs={{0,3},{1,2},{2,1},{3,0},{4,7},{5,6},{6,5},{7,4},{8,11},{9,10},{10,... | collective-permute-start | bytes 1671176 | tf_op jit(solution)/shard_map/ppermute | solution.py:54
  62.3 1.2 shard_map.65
  63.5 0.1 collective-permute-start.10
  63.6 6.7 %collective-permute-done.5.keep_in.give_in.codes_ref = s16[272,1024]{1,0:T(8,128)(2,1)S(1)} collective-permute-done((s16[272,1024]{1,0:T(8,128)(2,1)S(1)}, s16[272,1024]{1,0:T(8,128)(2,1)S(1)}, u32[]{:S(2)}, u32[]{:S(2)}) %collective-permute-start.5) | collective-permute-done | bytes 557088 | tf_op jit(solution)/shard_map/ppermute | solution.py:54
  70.3 0.9 shard_map.61
  71.3 0.1 collective-permute-start.11
  71.4 1.8 %collective-permute-done.10.keep_in.give_in.codes_ref = s16[272,1024]{1,0:T(8,128)(2,1)S(1)} collective-permute-done((s16[272,1024]{1,0:T(8,128)(2,1)S(1)}, s16[272,1024]{1,0:T(8,128)(2,1)S(1)}, u32[]{:S(2)}, u32[]{:S(2)}) %collective-permute-start.10) | collective-permute-done | bytes 557088 | tf_op jit(solution)/shard_map/ppermute | solution.py:54
  73.2 0.9 shard_map.66
  74.1 1.1 collective-permute-start.12
  75.2 2.9 %collective-permute-done.11.in_a = s16[144,1024]{1,0:T(8,128)(2,1)S(1)} collective-permute-done((s16[144,1024]{1,0:T(8,128)(2,1)S(1)}, s16[144,1024]{1,0:T(8,128)(2,1)S(1)}, u32[]{:S(2)}, u32[]{:S(2)}) %collective-permute-start.11) | collective-permute-done | bytes 294944 | tf_op jit(solution)/shard_map/ppermute | solution.py:54
  78.1 4.1 %collective-permute-done.12.in_b = s16[144,1024]{1,0:T(8,128)(2,1)S(1)} collective-permute-done((s16[144,1024]{1,0:T(8,128)(2,1)S(1)}, s16[144,1024]{1,0:T(8,128)(2,1)S(1)}, u32[]{:S(2)}, u32[]{:S(2)}) %collective-permute-start.12) | collective-permute-done | bytes 294944 | tf_op jit(solution)/shard_map/ppermute | solution.py:54
  82.1 0.4 shard_map.67
  82.6 20.9 %all_to_all.21.in_ref = s16[8,144,256]{2,1,0:T(8,128)(2,1)S(1)} all-to-all(s16[8,144,256]{2,1,0:T(8,128)(2,1)S(1)} %shard_map.67), channel_id=1, replica_groups=mesh['zh'=4,'core'=2,'zl'=2,'y'=4,'x'=4] {'zh','zl'}, dimensions={0} | all-to-all | bytes 1179648 | tf_op jit(solution)/shard_map/all_to_all | solution.py:442
  103.4 1.0 shard_map.68
  104.5 18.7 %all_to_all.22 = f32[256,1,128]{2,1,0:T(1,128)S(1)} all-to-all(f32[256,1,128]{2,1,0:T(1,128)S(1)} %bitcast.25), channel_id=1, replica_groups=mesh['zh'=4,'core'=2,'zl'=2,'y'=4,'x'=4] {'zh','core','zl','y','x'}, dimensions={0} | all-to-all | bytes 262144 | tf_op jit(solution)/shard_map/all_to_all | solution.py:444
  123.2 2.0 %shard_map.69 = (bf16[64,128]{1,0:T(8,128)(2,1)S(1)}, bf16[64,128]{1,0:T(8,128)(2,1)S(1)}) custom-call(s32[16]{0:T(128)S(1)} %fusion.12.s_ref, s32[8]{0:T(128)S(1)} %copy-done.3, s32[8,8]{1,0:T(8,128)S(1)} %copy-done.2, f32[256,128]{1,0:T(8,128)S(1)} %bitcast.24, f32[8,64,256]{2,1,0:T(8,128)S(1)} %get-tuple-element.48.grads_ref), custom_call_target="tpu_custom_call" | custom-call | flops 327680 | bytes 655360 | tf_op jit(solution)/shard_map/pallas_call | solution.py:96
  125.2 1.2 collective-permute-done.13
  126.4 0.2 broadcast_in_dim.19
  126.7 21.3 %all_to_all.23.in_ref = bf16[32,128,128]{2,1,0:T(8,128)(2,1)S(1)} all-to-all(bf16[32,128,128]{2,1,0:T(8,128)(2,1)S(1)} %broadcast_in_dim.19), channel_id=1, replica_groups=mesh['zh'=4,'core'=2,'zl'=2,'y'=4,'x'=4] {'zl','y','x'}, dimensions={0} | all-to-all | bytes 2097152 | tf_op jit(solution)/shard_map/all_to_all | solution.py:451
  148.0 1.0 shard_map.70
  (15 shorter events, 0.1 us)
Async XLA Ops:
  0.0 17.6 %collective-permute-start.1 = (bf16[1024,1024]{1,0:T(8,128)(2,1)}, bf16[1024,1024]{1,0:T(8,128)(2,1)}, u32[]{:S(2)}, u32[]{:S(2)}) collective-permute-start(bf16[1024,1024]{1,0:T(8,128)(2,1)} %bitcast.26), channel_id=1, source_target_pairs={{0,32},{32,0},{1,33},{33,1},{2,34},{34,2},{3,35},{35,3},{4,36},{36... | collective-permute-start | bytes 6291464 | tf_op jit(solution)/shard_map/ppermute | solution.py:412
  5.4 1.9 %copy-start = (f32[1024,1024]{1,0:T(8,128)}, f32[1024,1024]{1,0:T(8,128)S(1)}, u32[]{:S(2)}) copy-start(f32[1024,1024]{1,0:T(8,128)S(1)} %fusion.6.term_ref) | copy-start | bytes 12582916
  7.3 22.9 %collective-permute-start = (s16[528,1024]{1,0:T(8,128)(2,1)S(1)}, s16[528,1024]{1,0:T(8,128)(2,1)S(1)}, u32[]{:S(2)}, u32[]{:S(2)}) collective-permute-start(s16[528,1024]{1,0:T(8,128)(2,1)S(1)} %shard_map.55), channel_id=1, source_target_pairs={{0,1},{1,0},{2,3},{3,2},{4,5},{5,4},{6,7},{7,6},{8,9},{9,8},{10,11... | collective-permute-start | bytes 3244040 | tf_op jit(solution)/shard_map/ppermute | solution.py:54
  14.5 20.0 %collective-permute-start.6 = (s16[528,1024]{1,0:T(8,128)(2,1)S(1)}, s16[528,1024]{1,0:T(8,128)(2,1)S(1)}, u32[]{:S(2)}, u32[]{:S(2)}) collective-permute-start(s16[528,1024]{1,0:T(8,128)(2,1)S(1)} %shard_map.57), channel_id=1, source_target_pairs={{0,12},{1,13},{2,14},{3,15},{4,8},{5,9},{6,10},{7,11},{8,4},{9,5},... | collective-permute-start | bytes 3244040 | tf_op jit(solution)/shard_map/ppermute | solution.py:54
  23.4 15.2 %collective-permute-start.2 = (s16[528,1024]{1,0:T(8,128)(2,1)S(1)}, s16[528,1024]{1,0:T(8,128)(2,1)S(1)}, u32[]{:S(2)}, u32[]{:S(2)}) collective-permute-start(s16[528,1024]{1,0:T(8,128)(2,1)S(1)} %shard_map.58), channel_id=1, source_target_pairs={{0,1},{1,0},{2,3},{3,2},{4,5},{5,4},{6,7},{7,6},{8,9},{9,8},{10,11... | collective-permute-start | bytes 3244040 | tf_op jit(solution)/shard_map/ppermute | solution.py:54
  28.7 2.2 %copy-start.1 = (f32[1024,1024]{1,0:T(8,128)S(1)}, f32[1024,1024]{1,0:T(8,128)}, u32[]{:S(2)}) copy-start(f32[1024,1024]{1,0:T(8,128)} %copy-done) | copy-start | bytes 12582916
  29.7 16.6 %collective-permute-start.7 = (s16[528,1024]{1,0:T(8,128)(2,1)S(1)}, s16[528,1024]{1,0:T(8,128)(2,1)S(1)}, u32[]{:S(2)}, u32[]{:S(2)}) collective-permute-start(s16[528,1024]{1,0:T(8,128)(2,1)S(1)} %shard_map.63), channel_id=1, source_target_pairs={{0,12},{1,13},{2,14},{3,15},{4,8},{5,9},{6,10},{7,11},{8,4},{9,5},... | collective-permute-start | bytes 3244040 | tf_op jit(solution)/shard_map/ppermute | solution.py:54
  32.1 20.2 %collective-permute-start.3 = (s16[272,1024]{1,0:T(8,128)(2,1)S(1)}, s16[272,1024]{1,0:T(8,128)(2,1)S(1)}, u32[]{:S(2)}, u32[]{:S(2)}) collective-permute-start(s16[272,1024]{1,0:T(8,128)(2,1)S(1)} %get-tuple-element.32), channel_id=1, source_target_pairs={{0,12},{1,13},{2,14},{3,15},{4,8},{5,9},{6,10},{7,11},{8,4},{9,5},... | collective-permute-start | bytes 1671176 | tf_op jit(solution)/shard_map/ppermute | solution.py:54
  39.8 18.5 %collective-permute-start.4 = (s16[272,1024]{1,0:T(8,128)(2,1)S(1)}, s16[272,1024]{1,0:T(8,128)(2,1)S(1)}, u32[]{:S(2)}, u32[]{:S(2)}) collective-permute-start(s16[272,1024]{1,0:T(8,128)(2,1)S(1)} %get-tuple-element.33), channel_id=1, source_target_pairs={{0,12},{1,13},{2,14},{3,15},{4,8},{5,9},{6,10},{7,11},{8,4},{9,5},... | collective-permute-start | bytes 1671176 | tf_op jit(solution)/shard_map/ppermute | solution.py:54
  40.1 22.2 %collective-permute-start.8 = (s16[272,1024]{1,0:T(8,128)(2,1)S(1)}, s16[272,1024]{1,0:T(8,128)(2,1)S(1)}, u32[]{:S(2)}, u32[]{:S(2)}) collective-permute-start(s16[272,1024]{1,0:T(8,128)(2,1)S(1)} %get-tuple-element.40), channel_id=1, source_target_pairs={{0,1},{1,0},{2,3},{3,2},{4,5},{5,4},{6,7},{7,6},{8,9},{9,8},{10,11... | collective-permute-start | bytes 1671176 | tf_op jit(solution)/shard_map/ppermute | solution.py:54
  47.6 14.7 %collective-permute-start.9 = (s16[272,1024]{1,0:T(8,128)(2,1)S(1)}, s16[272,1024]{1,0:T(8,128)(2,1)S(1)}, u32[]{:S(2)}, u32[]{:S(2)}) collective-permute-start(s16[272,1024]{1,0:T(8,128)(2,1)S(1)} %get-tuple-element.41), channel_id=1, source_target_pairs={{0,1},{1,0},{2,3},{3,2},{4,5},{5,4},{6,7},{7,6},{8,9},{9,8},{10,11... | collective-permute-start | bytes 1671176 | tf_op jit(solution)/shard_map/ppermute | solution.py:54
  59.5 10.8 %collective-permute-start.5 = (s16[272,1024]{1,0:T(8,128)(2,1)S(1)}, s16[272,1024]{1,0:T(8,128)(2,1)S(1)}, u32[]{:S(2)}, u32[]{:S(2)}) collective-permute-start(s16[272,1024]{1,0:T(8,128)(2,1)S(1)} %get-tuple-element.35), channel_id=1, source_target_pairs={{0,3},{1,2},{2,1},{3,0},{4,7},{5,6},{6,5},{7,4},{8,11},{9,10},{10,... | collective-permute-start | bytes 1671176 | tf_op jit(solution)/shard_map/ppermute | solution.py:54
  63.5 9.6 %collective-permute-start.10 = (s16[272,1024]{1,0:T(8,128)(2,1)S(1)}, s16[272,1024]{1,0:T(8,128)(2,1)S(1)}, u32[]{:S(2)}, u32[]{:S(2)}) collective-permute-start(s16[272,1024]{1,0:T(8,128)(2,1)S(1)} %get-tuple-element.43), channel_id=1, source_target_pairs={{0,4},{1,5},{2,6},{3,7},{4,0},{5,1},{6,2},{7,3},{8,12},{9,13},{10,... | collective-permute-start | bytes 1671176 | tf_op jit(solution)/shard_map/ppermute | solution.py:54
  71.3 6.8 %collective-permute-start.11 = (s16[144,1024]{1,0:T(8,128)(2,1)S(1)}, s16[144,1024]{1,0:T(8,128)(2,1)S(1)}, u32[]{:S(2)}, u32[]{:S(2)}) collective-permute-start(s16[144,1024]{1,0:T(8,128)(2,1)S(1)} %get-tuple-element.45), channel_id=1, source_target_pairs={{0,4},{1,5},{2,6},{3,7},{4,0},{5,1},{6,2},{7,3},{8,12},{9,13},{10,... | collective-permute-start | bytes 884744 | tf_op jit(solution)/shard_map/ppermute | solution.py:54
  74.1 8.0 %collective-permute-start.12 = (s16[144,1024]{1,0:T(8,128)(2,1)S(1)}, s16[144,1024]{1,0:T(8,128)(2,1)S(1)}, u32[]{:S(2)}, u32[]{:S(2)}) collective-permute-start(s16[144,1024]{1,0:T(8,128)(2,1)S(1)} %get-tuple-element.46), channel_id=1, source_target_pairs={{0,3},{1,2},{2,1},{3,0},{4,7},{5,6},{6,5},{7,4},{8,11},{9,10},{10,... | collective-permute-start | bytes 884744 | tf_op jit(solution)/shard_map/ppermute | solution.py:54
  82.1 41.0 %copy-start.2 = (s32[8,8]{1,0:T(8,128)S(1)}, s32[8,8]{1,0:T(8,128)}, u32[]{:S(2)}) copy-start(s32[8,8]{1,0:T(8,128)} %flags_ref.1) | copy-start | bytes 772
  82.1 41.0 %copy-start.3 = (s32[8]{0:T(128)S(1)}, s32[8]{0:T(128)}, u32[]{:S(2)}) copy-start(s32[8]{0:T(128)} %order_ref.1) | copy-start | bytes 100
  125.1 1.3 collective-permute-start.13

commit v3 on v2

--- a/solution.py
+++ b/solution.py
@@ -427,18 +427,20 @@
         chunk = at[1]
         kept[at], coded = level(table, slots[chunk] + 1, terms[at][None], arrived[at], slots[chunk])
         arrived[at] = swap_along(coded, dims[chunk][1])
-    joined, taken = [], []
-    for chunk in range(2):
+    joined, taken = {}, {}
+    for chunk in (1, 0):
         pair = [(task, chunk) for task in range(2)]
-        summed, coded = join_tasks(
-            table, slots[chunk] + 2, [kept[at] for at in pair], [arrived[at] for at in pair]
-        )
-        joined.append(summed)
-        taken.append(swap_along(coded, dims[chunk][2]))
-    for chunk in range(2):
+        sums = [kept[at] for at in pair]
+        if chunk == 0:
+            sums[0] = after(sums[0], coded)
+        joined[chunk], coded = join_tasks(table, slots[chunk] + 2, sums, [arrived[at] for at in pair])
+        taken[chunk] = swap_along(coded, dims[chunk][2])
+    for chunk in (1, 0):
+        if chunk == 0:
+            joined[chunk] = after(joined[chunk], coded)
         joined[chunk], coded = level(table, slots[chunk] + 3, joined[chunk], taken[chunk])
         taken[chunk] = swap_along(coded, dims[chunk][3])
-    blocks = line_blocks(joined, taken)
+    blocks = line_blocks([joined[0], joined[1]], [taken[0], taken[1]])
     blocks = lax.all_to_all(blocks, ("zh", "zl"), split_axis=0, concat_axis=0, tiled=True)
     grads, grams = gram(table, blocks)
     grams = lax.all_to_all(grams, AXES, split_axis=0, concat_axis=0, tiled=True)

time: 149 us -> 161 us (1.081)
  starting transfers between devices: 14.8 us -> 19.9 us
  waiting for transfers between devices: 34.2 us -> 38.4 us
  blocking collectives: 60.9 us -> 63.5 us
    ppermute x12, starting transfers between devices: 14.7 us -> 19.8 us  [swap_along(): return lax.ppermute(value, AXES, pairs)]
    ppermute x12, waiting for transfers between devices: 33 us -> 37.3 us  [swap_along(): return lax.ppermute(value, AXES, pairs)]
    all_to_all x1, blocking collectives: 20.9 us -> 22.6 us  [on_device(): lax.all_to_all(blocks, ('zh', 'zl'), split_axis=0, concat_axis=0, tiled=T...]
  transfers between devices with their start and end apart: 14 -> 14, of which waited for: 9 -> 9; matrix products, arithmetic and copies ran while one was open for 13% -> 12% of each run, Pallas kernels for 9% -> 8%
where the time goes in v3:
time: 161 us
  blocking collectives  63.5 us (39%)
  waiting for transfers between devices  38.4 us (24%)
  starting transfers between devices  19.9 us (12%)
  matrix products  18 us (11%)
  Pallas kernels  17.9 us (11%)
  local copies, waits for them, and re-layouts  2.89 us (2%)
    ppermute x12, waiting for transfers between devices, swap_along(): return lax.ppermute(value, AXES, pairs)  37.3 us
    all_to_all x1, blocking collectives, on_device(): lax.all_to_all(blocks, ('zh', 'zl'), split_axis=0, concat_axis=0, tiled=T...  22.6 us
    all_to_all x1, blocking collectives, on_device(): lax.all_to_all(copies, DP, split_axis=0, concat_axis=0, tiled=True)  21.3 us
    ppermute x12, starting transfers between devices, swap_along(): return lax.ppermute(value, AXES, pairs)  19.8 us
    all_to_all x1, blocking collectives, on_device(): grams = lax.all_to_all(grams, AXES, split_axis=0, concat_axis=0, tiled=True)  19.6 us
    dot_general x4, matrix products, term_of(): lax.dot_general(part, cot, (((0,), (0,)), ((), ())), preferred_element_ty...  18 us
    pallas_call x14, Pallas kernels, call(): pl.pallas_call(kernel, out_shape=out_shape, grid_spec=pltpu.PrefetchScala...  16.4 us
  transfers between devices with their start and end apart: 14, of which 9 were waited for; matrix products, arithmetic and copies ran while one was open for 12% of the time, Pallas kernels for 8%

profile of v3, /device:TPU:32, one launch (start us, length us, event | category | flops | bytes accessed | tf_op | source)
XLA Modules:
  0.0 160.8 jit_solution(13847358327179473481)
XLA Ops:
  0.0 0.7 fusion.12.s_ref
  0.7 4.7 %fusion.6.term_ref = f32[1024,1024]{1,0:T(8,128)S(1)} fusion(bf16[1024,4096]{1,0:T(8,128)(2,1)} %param.5, s32[]{:T(128)S(6)} %select_n.25, bf16[1,1024,1024]{2,1,0:T(8,128)(2,1)} %param.6), kind=kOutput, calls=%fused_computation.6 | convolution fusion | flops 2147483648 | bytes 8388612 | tf_op jit(solution)/shard_map/dot_general | solution.py:150
  5.4 1.1 shard_map.55
  6.4 1.9 %copy-done = f32[1024,1024]{1,0:T(8,128)} copy-done((f32[1024,1024]{1,0:T(8,128)}, f32[1024,1024]{1,0:T(8,128)S(1)}, u32[]{:S(2)}) %copy-start) | copy-done | bytes 4194328
  8.4 4.0 %fusion.2.term_ref = f32[1024,1024]{1,0:T(8,128)S(1)} fusion(bf16[1024,1024]{1,0:T(8,128)(2,1)S(1)} %bitcast.27, bf16[1024,4096]{1,0:T(8,128)(2,1)} %param.5, s32[]{:T(128)S(6)} %select_n.26), kind=kOutput, calls=%fused_computation.2 | convolution fusion | flops 2147483648 | bytes 8388612 | tf_op jit(solution)/shard_map/dot_general | solution.py:150
  12.4 1.0 shard_map.57
  13.5 3.1 %collective-permute-start.1 = (s16[528,1024]{1,0:T(8,128)(2,1)S(1)}, s16[528,1024]{1,0:T(8,128)(2,1)S(1)}, u32[]{:S(2)}, u32[]{:S(2)}) collective-permute-start(s16[528,1024]{1,0:T(8,128)(2,1)S(1)} %shard_map.57), channel_id=1, source_target_pairs={{0,12},{1,13},{2,14},{3,15},{4,8},{5,9},{6,10},{7,11},{8,4},{9,5},... | collective-permute-start | bytes 3244040 | tf_op jit(solution)/shard_map/ppermute | solution.py:54
  16.6 4.7 %fusion.4.term_ref = f32[1024,1024]{1,0:T(8,128)S(1)} fusion(bf16[1024,1024]{1,0:T(8,128)(2,1)} %collective-permute-done.2, bf16[1024,4096]{1,0:T(8,128)(2,1)} %param.5, s32[]{:T(128)S(6)} %select_n.25), kind=kOutput, calls=%fused_computation.4 | convolution fusion | flops 2147483648 | bytes 8388612 | tf_op jit(solution)/shard_map/dot_general | solution.py:150
  21.3 1.0 shard_map.59
  22.3 4.7 %fusion.term_ref = f32[1024,1024]{1,0:T(8,128)S(1)} fusion(bf16[1024,1024]{1,0:T(8,128)(2,1)} %collective-permute-done.2, bf16[1024,4096]{1,0:T(8,128)(2,1)} %param.5, s32[]{:T(128)S(6)} %select_n.26), kind=kOutput, calls=%fused_computation | convolution fusion | flops 2147483648 | bytes 8388612 | tf_op jit(solution)/shard_map/dot_general | solution.py:150
  27.0 1.0 shard_map.60
  28.0 0.3 collective-permute-start.3
  28.3 1.5 collective-permute-start
  29.8 0.5 collective-permute-start.6
  30.4 1.2 shard_map.58
  31.6 1.6 collective-permute-start.4
  33.2 11.3 %collective-permute-done.3.keep_in.give_in.codes_ref = s16[528,1024]{1,0:T(8,128)(2,1)S(1)} collective-permute-done((s16[528,1024]{1,0:T(8,128)(2,1)S(1)}, s16[528,1024]{1,0:T(8,128)(2,1)S(1)}, u32[]{:S(2)}, u32[]{:S(2)}) %collective-permute-start.3) | collective-permute-done | bytes 1081376 | tf_op jit(solution)/shard_map/ppermute | solution.py:54
  44.5 1.2 shard_map.61
  45.7 1.6 collective-permute-start.5
  47.3 1.2 shard_map.56
  48.6 0.3 collective-permute-start.7
  48.9 6.2 %collective-permute-done.6.keep_in.give_in.codes_ref = s16[528,1024]{1,0:T(8,128)(2,1)S(1)} collective-permute-done((s16[528,1024]{1,0:T(8,128)(2,1)S(1)}, s16[528,1024]{1,0:T(8,128)(2,1)S(1)}, u32[]{:S(2)}, u32[]{:S(2)}) %collective-permute-start.6) | collective-permute-done | bytes 1081376 | tf_op jit(solution)/shard_map/ppermute | solution.py:54
  55.1 1.3 shard_map.63
  56.3 3.1 %collective-permute-start.8 = (s16[272,1024]{1,0:T(8,128)(2,1)S(1)}, s16[272,1024]{1,0:T(8,128)(2,1)S(1)}, u32[]{:S(2)}, u32[]{:S(2)}) collective-permute-start(s16[272,1024]{1,0:T(8,128)(2,1)S(1)} %get-tuple-element.42), channel_id=1, source_target_pairs={{0,12},{1,13},{2,14},{3,15},{4,8},{5,9},{6,10},{7,11},{8,4},{9,5},... | collective-permute-start | bytes 1671176 | tf_op jit(solution)/shard_map/ppermute | solution.py:54
  59.4 1.6 collective-permute-done.4.in_a
  61.1 6.0 %collective-permute-done.5.in_b = s16[272,1024]{1,0:T(8,128)(2,1)S(1)} collective-permute-done((s16[272,1024]{1,0:T(8,128)(2,1)S(1)}, s16[272,1024]{1,0:T(8,128)(2,1)S(1)}, u32[]{:S(2)}, u32[]{:S(2)}) %collective-permute-start.5) | collective-permute-done | bytes 557088 | tf_op jit(solution)/shard_map/ppermute | solution.py:54
  67.0 1.2 shard_map.62
  68.2 0.5 collective-permute-start.9
  68.7 1.2 shard_map.64
  69.8 2.8 %collective-permute-start.10 = (s16[272,1024]{1,0:T(8,128)(2,1)S(1)}, s16[272,1024]{1,0:T(8,128)(2,1)S(1)}, u32[]{:S(2)}, u32[]{:S(2)}) collective-permute-start(s16[272,1024]{1,0:T(8,128)(2,1)S(1)} %get-tuple-element.47), channel_id=1, source_target_pairs={{0,3},{1,2},{2,1},{3,0},{4,7},{5,6},{6,5},{7,4},{8,11},{9,10},{10,... | collective-permute-start | bytes 1671176 | tf_op jit(solution)/shard_map/ppermute | solution.py:54
  72.7 5.1 %collective-permute-done.9.keep_in.give_in.codes_ref = s16[272,1024]{1,0:T(8,128)(2,1)S(1)} collective-permute-done((s16[272,1024]{1,0:T(8,128)(2,1)S(1)}, s16[272,1024]{1,0:T(8,128)(2,1)S(1)}, u32[]{:S(2)}, u32[]{:S(2)}) %collective-permute-start.9) | collective-permute-done | bytes 557088 | tf_op jit(solution)/shard_map/ppermute | solution.py:54
  77.8 0.9 shard_map.65
  78.8 1.9 %collective-permute-done.10.keep_in.give_in.codes_ref = s16[272,1024]{1,0:T(8,128)(2,1)S(1)} collective-permute-done((s16[272,1024]{1,0:T(8,128)(2,1)S(1)}, s16[272,1024]{1,0:T(8,128)(2,1)S(1)}, u32[]{:S(2)}, u32[]{:S(2)}) %collective-permute-start.10) | collective-permute-done | bytes 557088 | tf_op jit(solution)/shard_map/ppermute | solution.py:54
  80.7 0.9 shard_map.66
  81.6 1.7 %collective-permute-start.11 = (s16[144,1024]{1,0:T(8,128)(2,1)S(1)}, s16[144,1024]{1,0:T(8,128)(2,1)S(1)}, u32[]{:S(2)}, u32[]{:S(2)}) collective-permute-start(s16[144,1024]{1,0:T(8,128)(2,1)S(1)} %get-tuple-element.50), channel_id=1, source_target_pairs={{0,4},{1,5},{2,6},{3,7},{4,0},{5,1},{6,2},{7,3},{8,12},{9,13},{10,... | collective-permute-start | bytes 884744 | tf_op jit(solution)/shard_map/ppermute | solution.py:54
  83.4 2.8 %collective-permute-start.12 = (s16[144,1024]{1,0:T(8,128)(2,1)S(1)}, s16[144,1024]{1,0:T(8,128)(2,1)S(1)}, u32[]{:S(2)}, u32[]{:S(2)}) collective-permute-start(s16[144,1024]{1,0:T(8,128)(2,1)S(1)} %get-tuple-element.45), channel_id=1, source_target_pairs={{0,3},{1,2},{2,1},{3,0},{4,7},{5,6},{6,5},{7,4},{8,11},{9,10},{10,... | collective-permute-start | bytes 884744 | tf_op jit(solution)/shard_map/ppermute | solution.py:54
  86.1 2.3 %collective-permute-done.11.in_a = s16[144,1024]{1,0:T(8,128)(2,1)S(1)} collective-permute-done((s16[144,1024]{1,0:T(8,128)(2,1)S(1)}, s16[144,1024]{1,0:T(8,128)(2,1)S(1)}, u32[]{:S(2)}, u32[]{:S(2)}) %collective-permute-start.11) | collective-permute-done | bytes 294944 | tf_op jit(solution)/shard_map/ppermute | solution.py:54
  88.4 2.9 %collective-permute-done.12.in_b = s16[144,1024]{1,0:T(8,128)(2,1)S(1)} collective-permute-done((s16[144,1024]{1,0:T(8,128)(2,1)S(1)}, s16[144,1024]{1,0:T(8,128)(2,1)S(1)}, u32[]{:S(2)}, u32[]{:S(2)}) %collective-permute-start.12) | collective-permute-done | bytes 294944 | tf_op jit(solution)/shard_map/ppermute | solution.py:54
  91.3 0.4 shard_map.67
  91.7 22.6 %all_to_all.21.in_ref = s16[8,144,256]{2,1,0:T(8,128)(2,1)S(1)} all-to-all(s16[8,144,256]{2,1,0:T(8,128)(2,1)S(1)} %shard_map.67), channel_id=1, replica_groups=mesh['zh'=4,'core'=2,'zl'=2,'y'=4,'x'=4] {'zh','zl'}, dimensions={0} | all-to-all | bytes 1179648 | tf_op jit(solution)/shard_map/all_to_all | solution.py:444
  114.3 1.0 shard_map.68
  115.3 19.6 %all_to_all.22 = f32[256,1,128]{2,1,0:T(1,128)S(1)} all-to-all(f32[256,1,128]{2,1,0:T(1,128)S(1)} %bitcast.25), channel_id=1, replica_groups=mesh['zh'=4,'core'=2,'zl'=2,'y'=4,'x'=4] {'zh','core','zl','y','x'}, dimensions={0} | all-to-all | bytes 262144 | tf_op jit(solution)/shard_map/all_to_all | solution.py:446
  134.9 2.0 %shard_map.69 = (bf16[64,128]{1,0:T(8,128)(2,1)S(1)}, bf16[64,128]{1,0:T(8,128)(2,1)S(1)}) custom-call(s32[16]{0:T(128)S(1)} %fusion.12.s_ref, s32[8]{0:T(128)S(1)} %copy-done.3, s32[8,8]{1,0:T(8,128)S(1)} %copy-done.2, f32[256,128]{1,0:T(8,128)S(1)} %bitcast.24, f32[8,64,256]{2,1,0:T(8,128)S(1)} %get-tuple-element.52.grads_ref), custom_call_target="tpu_custom_call" | custom-call | flops 327680 | bytes 655360 | tf_op jit(solution)/shard_map/pallas_call | solution.py:96
  136.9 0.1 collective-permute-start.13
  137.0 1.2 collective-permute-done.13
  138.2 0.2 broadcast_in_dim.19
  138.4 21.3 %all_to_all.23.in_ref = bf16[32,128,128]{2,1,0:T(8,128)(2,1)S(1)} all-to-all(bf16[32,128,128]{2,1,0:T(8,128)(2,1)S(1)} %broadcast_in_dim.19), channel_id=1, replica_groups=mesh['zh'=4,'core'=2,'zl'=2,'y'=4,'x'=4] {'zl','y','x'}, dimensions={0} | all-to-all | bytes 2097152 | tf_op jit(solution)/shard_map/all_to_all | solution.py:453
  159.8 1.0 shard_map.70
  (17 shorter events, 0.0 us)
Async XLA Ops:
  0.0 16.6 %collective-permute-start.2 = (bf16[1024,1024]{1,0:T(8,128)(2,1)}, bf16[1024,1024]{1,0:T(8,128)(2,1)}, u32[]{:S(2)}, u32[]{:S(2)}) collective-permute-start(bf16[1024,1024]{1,0:T(8,128)(2,1)} %bitcast.26), channel_id=1, source_target_pairs={{0,32},{32,0},{1,33},{33,1},{2,34},{34,2},{3,35},{35,3},{4,36},{36... | collective-permute-start | bytes 6291464 | tf_op jit(solution)/shard_map/ppermute | solution.py:412
  5.4 3.0 %copy-start.4 = (bf16[1,1024,1024]{2,1,0:T(8,128)(2,1)S(1)}, bf16[1,1024,1024]{2,1,0:T(8,128)(2,1)}, u32[]{:S(2)}) copy-start(bf16[1,1024,1024]{2,1,0:T(8,128)(2,1)} %param.6) | copy-start | bytes 6291460
  6.4 2.0 %copy-start = (f32[1024,1024]{1,0:T(8,128)}, f32[1024,1024]{1,0:T(8,128)S(1)}, u32[]{:S(2)}) copy-start(f32[1024,1024]{1,0:T(8,128)S(1)} %fusion.6.term_ref) | copy-start | bytes 12582916
  13.5 16.9 %collective-permute-start.1 = (s16[528,1024]{1,0:T(8,128)(2,1)S(1)}, s16[528,1024]{1,0:T(8,128)(2,1)S(1)}, u32[]{:S(2)}, u32[]{:S(2)}) collective-permute-start(s16[528,1024]{1,0:T(8,128)(2,1)S(1)} %shard_map.57), channel_id=1, source_target_pairs={{0,12},{1,13},{2,14},{3,15},{4,8},{5,9},{6,10},{7,11},{8,4},{9,5},... | collective-permute-start | bytes 3244040 | tf_op jit(solution)/shard_map/ppermute | solution.py:54
  28.0 16.4 %collective-permute-start.3 = (s16[528,1024]{1,0:T(8,128)(2,1)S(1)}, s16[528,1024]{1,0:T(8,128)(2,1)S(1)}, u32[]{:S(2)}, u32[]{:S(2)}) collective-permute-start(s16[528,1024]{1,0:T(8,128)(2,1)S(1)} %shard_map.60), channel_id=1, source_target_pairs={{0,12},{1,13},{2,14},{3,15},{4,8},{5,9},{6,10},{7,11},{8,4},{9,5},... | collective-permute-start | bytes 3244040 | tf_op jit(solution)/shard_map/ppermute | solution.py:54
  28.3 19.0 %collective-permute-start = (s16[528,1024]{1,0:T(8,128)(2,1)S(1)}, s16[528,1024]{1,0:T(8,128)(2,1)S(1)}, u32[]{:S(2)}, u32[]{:S(2)}) collective-permute-start(s16[528,1024]{1,0:T(8,128)(2,1)S(1)} %shard_map.55), channel_id=1, source_target_pairs={{0,1},{1,0},{2,3},{3,2},{4,5},{5,4},{6,7},{7,6},{8,9},{9,8},{10,11... | collective-permute-start | bytes 3244040 | tf_op jit(solution)/shard_map/ppermute | solution.py:54
  29.8 25.2 %collective-permute-start.6 = (s16[528,1024]{1,0:T(8,128)(2,1)S(1)}, s16[528,1024]{1,0:T(8,128)(2,1)S(1)}, u32[]{:S(2)}, u32[]{:S(2)}) collective-permute-start(s16[528,1024]{1,0:T(8,128)(2,1)S(1)} %shard_map.59), channel_id=1, source_target_pairs={{0,1},{1,0},{2,3},{3,2},{4,5},{5,4},{6,7},{7,6},{8,9},{9,8},{10,11... | collective-permute-start | bytes 3244040 | tf_op jit(solution)/shard_map/ppermute | solution.py:54
  31.6 29.4 %collective-permute-start.4 = (s16[272,1024]{1,0:T(8,128)(2,1)S(1)}, s16[272,1024]{1,0:T(8,128)(2,1)S(1)}, u32[]{:S(2)}, u32[]{:S(2)}) collective-permute-start(s16[272,1024]{1,0:T(8,128)(2,1)S(1)} %get-tuple-element.36), channel_id=1, source_target_pairs={{0,1},{1,0},{2,3},{3,2},{4,5},{5,4},{6,7},{7,6},{8,9},{9,8},{10,11... | collective-permute-start | bytes 1671176 | tf_op jit(solution)/shard_map/ppermute | solution.py:54
  44.5 2.8 %copy-start.1 = (f32[1024,1024]{1,0:T(8,128)S(1)}, f32[1024,1024]{1,0:T(8,128)}, u32[]{:S(2)}) copy-start(f32[1024,1024]{1,0:T(8,128)} %copy-done) | copy-start | bytes 12582916
  45.7 21.3 %collective-permute-start.5 = (s16[272,1024]{1,0:T(8,128)(2,1)S(1)}, s16[272,1024]{1,0:T(8,128)(2,1)S(1)}, u32[]{:S(2)}, u32[]{:S(2)}) collective-permute-start(s16[272,1024]{1,0:T(8,128)(2,1)S(1)} %get-tuple-element.37), channel_id=1, source_target_pairs={{0,1},{1,0},{2,3},{3,2},{4,5},{5,4},{6,7},{7,6},{8,9},{9,8},{10,11... | collective-permute-start | bytes 1671176 | tf_op jit(solution)/shard_map/ppermute | solution.py:54
  48.6 20.1 %collective-permute-start.7 = (s16[272,1024]{1,0:T(8,128)(2,1)S(1)}, s16[272,1024]{1,0:T(8,128)(2,1)S(1)}, u32[]{:S(2)}, u32[]{:S(2)}) collective-permute-start(s16[272,1024]{1,0:T(8,128)(2,1)S(1)} %get-tuple-element.41), channel_id=1, source_target_pairs={{0,12},{1,13},{2,14},{3,15},{4,8},{5,9},{6,10},{7,11},{8,4},{9,5},... | collective-permute-start | bytes 1671176 | tf_op jit(solution)/shard_map/ppermute | solution.py:54
  56.3 12.3 %collective-permute-start.8 = (s16[272,1024]{1,0:T(8,128)(2,1)S(1)}, s16[272,1024]{1,0:T(8,128)(2,1)S(1)}, u32[]{:S(2)}, u32[]{:S(2)}) collective-permute-start(s16[272,1024]{1,0:T(8,128)(2,1)S(1)} %get-tuple-element.42), channel_id=1, source_target_pairs={{0,12},{1,13},{2,14},{3,15},{4,8},{5,9},{6,10},{7,11},{8,4},{9,5},... | collective-permute-start | bytes 1671176 | tf_op jit(solution)/shard_map/ppermute | solution.py:54
  68.2 9.6 %collective-permute-start.9 = (s16[272,1024]{1,0:T(8,128)(2,1)S(1)}, s16[272,1024]{1,0:T(8,128)(2,1)S(1)}, u32[]{:S(2)}, u32[]{:S(2)}) collective-permute-start(s16[272,1024]{1,0:T(8,128)(2,1)S(1)} %get-tuple-element.38), channel_id=1, source_target_pairs={{0,4},{1,5},{2,6},{3,7},{4,0},{5,1},{6,2},{7,3},{8,12},{9,13},{10,... | collective-permute-start | bytes 1671176 | tf_op jit(solution)/shard_map/ppermute | solution.py:54
  69.8 10.8 %collective-permute-start.10 = (s16[272,1024]{1,0:T(8,128)(2,1)S(1)}, s16[272,1024]{1,0:T(8,128)(2,1)S(1)}, u32[]{:S(2)}, u32[]{:S(2)}) collective-permute-start(s16[272,1024]{1,0:T(8,128)(2,1)S(1)} %get-tuple-element.47), channel_id=1, source_target_pairs={{0,3},{1,2},{2,1},{3,0},{4,7},{5,6},{6,5},{7,4},{8,11},{9,10},{10,... | collective-permute-start | bytes 1671176 | tf_op jit(solution)/shard_map/ppermute | solution.py:54
  81.6 6.8 %collective-permute-start.11 = (s16[144,1024]{1,0:T(8,128)(2,1)S(1)}, s16[144,1024]{1,0:T(8,128)(2,1)S(1)}, u32[]{:S(2)}, u32[]{:S(2)}) collective-permute-start(s16[144,1024]{1,0:T(8,128)(2,1)S(1)} %get-tuple-element.50), channel_id=1, source_target_pairs={{0,4},{1,5},{2,6},{3,7},{4,0},{5,1},{6,2},{7,3},{8,12},{9,13},{10,... | collective-permute-start | bytes 884744 | tf_op jit(solution)/shard_map/ppermute | solution.py:54
  83.4 7.9 %collective-permute-start.12 = (s16[144,1024]{1,0:T(8,128)(2,1)S(1)}, s16[144,1024]{1,0:T(8,128)(2,1)S(1)}, u32[]{:S(2)}, u32[]{:S(2)}) collective-permute-start(s16[144,1024]{1,0:T(8,128)(2,1)S(1)} %get-tuple-element.45), channel_id=1, source_target_pairs={{0,3},{1,2},{2,1},{3,0},{4,7},{5,6},{6,5},{7,4},{8,11},{9,10},{10,... | collective-permute-start | bytes 884744 | tf_op jit(solution)/shard_map/ppermute | solution.py:54
  91.3 43.6 %copy-start.2 = (s32[8,8]{1,0:T(8,128)S(1)}, s32[8,8]{1,0:T(8,128)}, u32[]{:S(2)}) copy-start(s32[8,8]{1,0:T(8,128)} %flags_ref.1) | copy-start | bytes 772
  91.3 43.6 %copy-start.3 = (s32[8]{0:T(128)S(1)}, s32[8]{0:T(128)}, u32[]{:S(2)}) copy-start(s32[8]{0:T(128)} %order_ref.1) | copy-start | bytes 100
  136.9 1.3 collective-permute-start.13

commit v4 on v2

--- a/solution.py
+++ b/solution.py
@@ -18,10 +18,10 @@
 PARTNER = {"a": (1, 0, 3, 2), "b": (3, 2, 1, 0)}
 BIT = {"a": (0, 1, 1, 0), "b": (0, 0, 1, 1)}
 ORDER = {
-    (0, 0): ("xa", "yb", "xb", "ya", "z"),
-    (0, 1): ("yb", "xa", "ya", "xb", "z"),
-    (1, 0): ("ya", "xb", "xa", "yb", "z"),
-    (1, 1): ("xb", "ya", "yb", "xa", "z"),
+    (0, 0): ("xa", "ya", "xb", "yb", "z"),
+    (0, 1): ("yb", "xb", "ya", "xa", "z"),
+    (1, 0): ("ya", "xa", "yb", "xb", "z"),
+    (1, 1): ("xb", "yb", "xa", "ya", "z"),
 }
 FULL = 32000.0
 STEPS = 64.0
@@ -430,12 +430,15 @@
     joined, taken = [], []
     for chunk in range(2):
         pair = [(task, chunk) for task in range(2)]
-        summed, coded = join_tasks(
-            table, slots[chunk] + 2, [kept[at] for at in pair], [arrived[at] for at in pair]
-        )
+        sums = [kept[at] for at in pair]
+        if chunk:
+            sums[0] = after(sums[0], coded)
+        summed, coded = join_tasks(table, slots[chunk] + 2, sums, [arrived[at] for at in pair])
         joined.append(summed)
         taken.append(swap_along(coded, dims[chunk][2]))
     for chunk in range(2):
+        if chunk:
+            joined[chunk] = after(joined[chunk], coded)
         joined[chunk], coded = level(table, slots[chunk] + 3, joined[chunk], taken[chunk])
         taken[chunk] = swap_along(coded, dims[chunk][3])
     blocks = line_blocks(joined, taken)

time: 149 us -> 151 us (1.013)
  starting transfers between devices: 14.8 us -> 17.6 us
  waiting for transfers between devices: 34.2 us -> 32.5 us
    ppermute x12, starting transfers between devices: 14.7 us -> 17.5 us  [swap_along(): return lax.ppermute(value, AXES, pairs)]
    ppermute x12, waiting for transfers between devices: 33 us -> 31.3 us  [swap_along(): return lax.ppermute(value, AXES, pairs)]
  transfers between devices with their start and end apart: 14 -> 14, of which waited for: 9 -> 7; matrix products, arithmetic and copies ran while one was open for 13% -> 13% of each run, Pallas kernels for 9% -> 9%
where the time goes in v4:
time: 151 us
  blocking collectives  61.6 us (41%)
  waiting for transfers between devices  32.5 us (22%)
  matrix products  18.7 us (12%)
  Pallas kernels  17.9 us (12%)
  starting transfers between devices  17.6 us (12%)
  local copies, waits for them, and re-layouts  2.45 us (2%)
    ppermute x12, waiting for transfers between devices, swap_along(): return lax.ppermute(value, AXES, pairs)  31.3 us
    all_to_all x1, blocking collectives, on_device(): lax.all_to_all(copies, DP, split_axis=0, concat_axis=0, tiled=True)  21.3 us
    all_to_all x1, blocking collectives, on_device(): lax.all_to_all(blocks, ('zh', 'zl'), split_axis=0, concat_axis=0, tiled=T...  20.9 us
    all_to_all x1, blocking collectives, on_device(): grams = lax.all_to_all(grams, AXES, split_axis=0, concat_axis=0, tiled=True)  19.4 us
    dot_general x4, matrix products, term_of(): lax.dot_general(part, cot, (((0,), (0,)), ((), ())), preferred_element_ty...  18.7 us
    ppermute x12, starting transfers between devices, swap_along(): return lax.ppermute(value, AXES, pairs)  17.5 us
    pallas_call x14, Pallas kernels, call(): pl.pallas_call(kernel, out_shape=out_shape, grid_spec=pltpu.PrefetchScala...  16.4 us
  transfers between devices with their start and end apart: 14, of which 7 were waited for; matrix products, arithmetic and copies ran while one was open for 13% of the time, Pallas kernels for 9%

profile of v4, /device:TPU:32, one launch (start us, length us, event | category | flops | bytes accessed | tf_op | source)
XLA Modules:
  0.0 150.9 jit_solution(14704921867985136898)
XLA Ops:
  0.0 0.7 fusion.12.s_ref
  0.7 4.7 %fusion.6.term_ref = f32[1024,1024]{1,0:T(8,128)S(1)} fusion(bf16[1024,4096]{1,0:T(8,128)(2,1)} %param.5, s32[]{:T(128)S(6)} %select_n.25, bf16[1,1024,1024]{2,1,0:T(8,128)(2,1)} %param.6), kind=kOutput, calls=%fused_computation.6 | convolution fusion | flops 2147483648 | bytes 8388612 | tf_op jit(solution)/shard_map/dot_general | solution.py:150
  5.4 1.0 shard_map.55
  6.4 0.9 copy-done
  7.3 1.5 collective-permute-start
  8.8 4.7 %fusion.2.term_ref = f32[1024,1024]{1,0:T(8,128)S(1)} fusion(bf16[1024,1024]{1,0:T(8,128)(2,1)} %bitcast.27, bf16[1024,4096]{1,0:T(8,128)(2,1)} %param.5, s32[]{:T(128)S(6)} %select_n.26), kind=kOutput, calls=%fused_computation.2 | convolution fusion | flops 2147483648 | bytes 8388612 | tf_op jit(solution)/shard_map/dot_general | solution.py:150
  13.5 1.0 shard_map.57
  14.5 3.1 %collective-permute-start.6 = (s16[528,1024]{1,0:T(8,128)(2,1)S(1)}, s16[528,1024]{1,0:T(8,128)(2,1)S(1)}, u32[]{:S(2)}, u32[]{:S(2)}) collective-permute-start(s16[528,1024]{1,0:T(8,128)(2,1)S(1)} %shard_map.57), channel_id=1, source_target_pairs={{0,12},{1,13},{2,14},{3,15},{4,8},{5,9},{6,10},{7,11},{8,4},{9,5},... | collective-permute-start | bytes 3244040 | tf_op jit(solution)/shard_map/ppermute | solution.py:54
  17.6 0.0 collective-permute-done.1
  17.6 4.7 %fusion.4.term_ref = f32[1024,1024]{1,0:T(8,128)S(1)} fusion(bf16[1024,1024]{1,0:T(8,128)(2,1)} %collective-permute-done.1, bf16[1024,4096]{1,0:T(8,128)(2,1)} %param.5, s32[]{:T(128)S(6)} %select_n.25), kind=kOutput, calls=%fused_computation.4 | convolution fusion | flops 2147483648 | bytes 8388612 | tf_op jit(solution)/shard_map/dot_general | solution.py:150
  22.3 1.0 shard_map.58
  23.4 0.6 collective-permute-start.2
  24.0 4.7 %fusion.term_ref = f32[1024,1024]{1,0:T(8,128)S(1)} fusion(bf16[1024,1024]{1,0:T(8,128)(2,1)} %collective-permute-done.1, bf16[1024,4096]{1,0:T(8,128)(2,1)} %param.5, s32[]{:T(128)S(6)} %select_n.26), kind=kOutput, calls=%fused_computation | convolution fusion | flops 2147483648 | bytes 8388612 | tf_op jit(solution)/shard_map/dot_general | solution.py:150
  28.7 1.0 shard_map.63
  29.7 0.5 collective-permute-start.7
  30.2 0.6 copy-done.1
  30.8 1.2 shard_map.56
  32.1 0.2 collective-permute-start.3
  32.3 10.6 %collective-permute-done.2.keep_in.give_in.codes_ref = s16[528,1024]{1,0:T(8,128)(2,1)S(1)} collective-permute-done((s16[528,1024]{1,0:T(8,128)(2,1)S(1)}, s16[528,1024]{1,0:T(8,128)(2,1)S(1)}, u32[]{:S(2)}, u32[]{:S(2)}) %collective-permute-start.2) | collective-permute-done | bytes 1081376 | tf_op jit(solution)/shard_map/ppermute | solution.py:54
  42.9 1.2 shard_map.59
  44.2 0.1 collective-permute-start.4
  44.3 1.2 shard_map.62
  45.5 2.2 %collective-permute-start.8 = (s16[272,1024]{1,0:T(8,128)(2,1)S(1)}, s16[272,1024]{1,0:T(8,128)(2,1)S(1)}, u32[]{:S(2)}, u32[]{:S(2)}) collective-permute-start(s16[272,1024]{1,0:T(8,128)(2,1)S(1)} %get-tuple-element.43), channel_id=1, source_target_pairs={{0,3},{1,2},{2,1},{3,0},{4,7},{5,6},{6,5},{7,4},{8,11},{9,10},{10,... | collective-permute-start | bytes 1671176 | tf_op jit(solution)/shard_map/ppermute | solution.py:54
  47.7 1.2 shard_map.64
  49.0 5.5 %collective-permute-start.9 = (s16[272,1024]{1,0:T(8,128)(2,1)S(1)}, s16[272,1024]{1,0:T(8,128)(2,1)S(1)}, u32[]{:S(2)}, u32[]{:S(2)}) collective-permute-start(s16[272,1024]{1,0:T(8,128)(2,1)S(1)} %get-tuple-element.44), channel_id=1, source_target_pairs={{0,3},{1,2},{2,1},{3,0},{4,7},{5,6},{6,5},{7,4},{8,11},{9,10},{10,... | collective-permute-start | bytes 1671176 | tf_op jit(solution)/shard_map/ppermute | solution.py:54
  54.4 1.2 shard_map.60
  55.6 1.5 %collective-permute-start.5 = (s16[272,1024]{1,0:T(8,128)(2,1)S(1)}, s16[272,1024]{1,0:T(8,128)(2,1)S(1)}, u32[]{:S(2)}, u32[]{:S(2)}) collective-permute-start(s16[272,1024]{1,0:T(8,128)(2,1)S(1)} %get-tuple-element.37), channel_id=1, source_target_pairs={{0,3},{1,2},{2,1},{3,0},{4,7},{5,6},{6,5},{7,4},{8,11},{9,10},{10,... | collective-permute-start | bytes 1671176 | tf_op jit(solution)/shard_map/ppermute | solution.py:54
  57.2 5.2 %collective-permute-done.9.in_b = s16[272,1024]{1,0:T(8,128)(2,1)S(1)} collective-permute-done((s16[272,1024]{1,0:T(8,128)(2,1)S(1)}, s16[272,1024]{1,0:T(8,128)(2,1)S(1)}, u32[]{:S(2)}, u32[]{:S(2)}) %collective-permute-start.9) | collective-permute-done | bytes 557088 | tf_op jit(solution)/shard_map/ppermute | solution.py:54
  62.3 1.2 shard_map.65
  63.5 2.1 %collective-permute-start.10 = (s16[272,1024]{1,0:T(8,128)(2,1)S(1)}, s16[272,1024]{1,0:T(8,128)(2,1)S(1)}, u32[]{:S(2)}, u32[]{:S(2)}) collective-permute-start(s16[272,1024]{1,0:T(8,128)(2,1)S(1)} %get-tuple-element.48), channel_id=1, source_target_pairs={{0,4},{1,5},{2,6},{3,7},{4,0},{5,1},{6,2},{7,3},{8,12},{9,13},{10,... | collective-permute-start | bytes 1671176 | tf_op jit(solution)/shard_map/ppermute | solution.py:54
  65.6 2.7 %collective-permute-done.5.keep_in.give_in.codes_ref = s16[272,1024]{1,0:T(8,128)(2,1)S(1)} collective-permute-done((s16[272,1024]{1,0:T(8,128)(2,1)S(1)}, s16[272,1024]{1,0:T(8,128)(2,1)S(1)}, u32[]{:S(2)}, u32[]{:S(2)}) %collective-permute-start.5) | collective-permute-done | bytes 557088 | tf_op jit(solution)/shard_map/ppermute | solution.py:54
  68.3 0.9 shard_map.61
  69.2 0.1 collective-permute-start.11
  69.3 6.1 %collective-permute-done.10.keep_in.give_in.codes_ref = s16[272,1024]{1,0:T(8,128)(2,1)S(1)} collective-permute-done((s16[272,1024]{1,0:T(8,128)(2,1)S(1)}, s16[272,1024]{1,0:T(8,128)(2,1)S(1)}, u32[]{:S(2)}, u32[]{:S(2)}) %collective-permute-start.10) | collective-permute-done | bytes 557088 | tf_op jit(solution)/shard_map/ppermute | solution.py:54
  75.5 0.9 shard_map.66
  76.4 0.1 collective-permute-start.12
  76.5 0.7 collective-permute-done.11.in_a
  77.3 6.0 %collective-permute-done.12.in_b = s16[144,1024]{1,0:T(8,128)(2,1)S(1)} collective-permute-done((s16[144,1024]{1,0:T(8,128)(2,1)S(1)}, s16[144,1024]{1,0:T(8,128)(2,1)S(1)}, u32[]{:S(2)}, u32[]{:S(2)}) %collective-permute-start.12) | collective-permute-done | bytes 294944 | tf_op jit(solution)/shard_map/ppermute | solution.py:54
  83.2 0.4 shard_map.67
  83.7 20.9 %all_to_all.21.in_ref = s16[8,144,256]{2,1,0:T(8,128)(2,1)S(1)} all-to-all(s16[8,144,256]{2,1,0:T(8,128)(2,1)S(1)} %shard_map.67), channel_id=1, replica_groups=mesh['zh'=4,'core'=2,'zl'=2,'y'=4,'x'=4] {'zh','zl'}, dimensions={0} | all-to-all | bytes 1179648 | tf_op jit(solution)/shard_map/all_to_all | solution.py:445
  104.6 1.0 shard_map.68
  105.6 19.4 %all_to_all.22 = f32[256,1,128]{2,1,0:T(1,128)S(1)} all-to-all(f32[256,1,128]{2,1,0:T(1,128)S(1)} %bitcast.25), channel_id=1, replica_groups=mesh['zh'=4,'core'=2,'zl'=2,'y'=4,'x'=4] {'zh','core','zl','y','x'}, dimensions={0} | all-to-all | bytes 262144 | tf_op jit(solution)/shard_map/all_to_all | solution.py:447
  125.0 2.0 %shard_map.69 = (bf16[64,128]{1,0:T(8,128)(2,1)S(1)}, bf16[64,128]{1,0:T(8,128)(2,1)S(1)}) custom-call(s32[16]{0:T(128)S(1)} %fusion.12.s_ref, s32[8]{0:T(128)S(1)} %copy-done.3, s32[8,8]{1,0:T(8,128)S(1)} %copy-done.2, f32[256,128]{1,0:T(8,128)S(1)} %bitcast.24, f32[8,64,256]{2,1,0:T(8,128)S(1)} %get-tuple-element.52.grads_ref), custom_call_target="tpu_custom_call" | custom-call | flops 327680 | bytes 655360 | tf_op jit(solution)/shard_map/pallas_call | solution.py:96
  127.0 0.1 collective-permute-start.13
  127.1 1.2 collective-permute-done.13
  128.3 0.2 broadcast_in_dim.19
  128.5 21.3 %all_to_all.23.in_ref = bf16[32,128,128]{2,1,0:T(8,128)(2,1)S(1)} all-to-all(bf16[32,128,128]{2,1,0:T(8,128)(2,1)S(1)} %broadcast_in_dim.19), channel_id=1, replica_groups=mesh['zh'=4,'core'=2,'zl'=2,'y'=4,'x'=4] {'zl','y','x'}, dimensions={0} | all-to-all | bytes 2097152 | tf_op jit(solution)/shard_map/all_to_all | solution.py:454
  149.8 1.0 shard_map.70
  (15 shorter events, 0.0 us)
Async XLA Ops:
  0.0 17.6 %collective-permute-start.1 = (bf16[1024,1024]{1,0:T(8,128)(2,1)}, bf16[1024,1024]{1,0:T(8,128)(2,1)}, u32[]{:S(2)}, u32[]{:S(2)}) collective-permute-start(bf16[1024,1024]{1,0:T(8,128)(2,1)} %bitcast.26), channel_id=1, source_target_pairs={{0,32},{32,0},{1,33},{33,1},{2,34},{34,2},{3,35},{35,3},{4,36},{36... | collective-permute-start | bytes 6291464 | tf_op jit(solution)/shard_map/ppermute | solution.py:412
  5.4 1.9 %copy-start = (f32[1024,1024]{1,0:T(8,128)}, f32[1024,1024]{1,0:T(8,128)S(1)}, u32[]{:S(2)}) copy-start(f32[1024,1024]{1,0:T(8,128)S(1)} %fusion.6.term_ref) | copy-start | bytes 12582916
  7.3 22.9 %collective-permute-start = (s16[528,1024]{1,0:T(8,128)(2,1)S(1)}, s16[528,1024]{1,0:T(8,128)(2,1)S(1)}, u32[]{:S(2)}, u32[]{:S(2)}) collective-permute-start(s16[528,1024]{1,0:T(8,128)(2,1)S(1)} %shard_map.55), channel_id=1, source_target_pairs={{0,1},{1,0},{2,3},{3,2},{4,5},{5,4},{6,7},{7,6},{8,9},{9,8},{10,11... | collective-permute-start | bytes 3244040 | tf_op jit(solution)/shard_map/ppermute | solution.py:54
  14.5 29.7 %collective-permute-start.6 = (s16[528,1024]{1,0:T(8,128)(2,1)S(1)}, s16[528,1024]{1,0:T(8,128)(2,1)S(1)}, u32[]{:S(2)}, u32[]{:S(2)}) collective-permute-start(s16[528,1024]{1,0:T(8,128)(2,1)S(1)} %shard_map.57), channel_id=1, source_target_pairs={{0,12},{1,13},{2,14},{3,15},{4,8},{5,9},{6,10},{7,11},{8,4},{9,5},... | collective-permute-start | bytes 3244040 | tf_op jit(solution)/shard_map/ppermute | solution.py:54
  23.4 19.6 %collective-permute-start.2 = (s16[528,1024]{1,0:T(8,128)(2,1)S(1)}, s16[528,1024]{1,0:T(8,128)(2,1)S(1)}, u32[]{:S(2)}, u32[]{:S(2)}) collective-permute-start(s16[528,1024]{1,0:T(8,128)(2,1)S(1)} %shard_map.58), channel_id=1, source_target_pairs={{0,1},{1,0},{2,3},{3,2},{4,5},{5,4},{6,7},{7,6},{8,9},{9,8},{10,11... | collective-permute-start | bytes 3244040 | tf_op jit(solution)/shard_map/ppermute | solution.py:54
  28.7 2.2 %copy-start.1 = (f32[1024,1024]{1,0:T(8,128)S(1)}, f32[1024,1024]{1,0:T(8,128)}, u32[]{:S(2)}) copy-start(f32[1024,1024]{1,0:T(8,128)} %copy-done) | copy-start | bytes 12582916
  29.7 18.0 %collective-permute-start.7 = (s16[528,1024]{1,0:T(8,128)(2,1)S(1)}, s16[528,1024]{1,0:T(8,128)(2,1)S(1)}, u32[]{:S(2)}, u32[]{:S(2)}) collective-permute-start(s16[528,1024]{1,0:T(8,128)(2,1)S(1)} %shard_map.63), channel_id=1, source_target_pairs={{0,12},{1,13},{2,14},{3,15},{4,8},{5,9},{6,10},{7,11},{8,4},{9,5},... | collective-permute-start | bytes 3244040 | tf_op jit(solution)/shard_map/ppermute | solution.py:54
  32.1 22.3 %collective-permute-start.3 = (s16[272,1024]{1,0:T(8,128)(2,1)S(1)}, s16[272,1024]{1,0:T(8,128)(2,1)S(1)}, u32[]{:S(2)}, u32[]{:S(2)}) collective-permute-start(s16[272,1024]{1,0:T(8,128)(2,1)S(1)} %get-tuple-element.34), channel_id=1, source_target_pairs={{0,4},{1,5},{2,6},{3,7},{4,0},{5,1},{6,2},{7,3},{8,12},{9,13},{10,... | collective-permute-start | bytes 1671176 | tf_op jit(solution)/shard_map/ppermute | solution.py:54
  44.2 10.3 %collective-permute-start.4 = (s16[272,1024]{1,0:T(8,128)(2,1)S(1)}, s16[272,1024]{1,0:T(8,128)(2,1)S(1)}, u32[]{:S(2)}, u32[]{:S(2)}) collective-permute-start(s16[272,1024]{1,0:T(8,128)(2,1)S(1)} %get-tuple-element.35), channel_id=1, source_target_pairs={{0,4},{1,5},{2,6},{3,7},{4,0},{5,1},{6,2},{7,3},{8,12},{9,13},{10,... | collective-permute-start | bytes 1671176 | tf_op jit(solution)/shard_map/ppermute | solution.py:54
  45.5 11.6 %collective-permute-start.8 = (s16[272,1024]{1,0:T(8,128)(2,1)S(1)}, s16[272,1024]{1,0:T(8,128)(2,1)S(1)}, u32[]{:S(2)}, u32[]{:S(2)}) collective-permute-start(s16[272,1024]{1,0:T(8,128)(2,1)S(1)} %get-tuple-element.43), channel_id=1, source_target_pairs={{0,3},{1,2},{2,1},{3,0},{4,7},{5,6},{6,5},{7,4},{8,11},{9,10},{10,... | collective-permute-start | bytes 1671176 | tf_op jit(solution)/shard_map/ppermute | solution.py:54
  49.0 13.4 %collective-permute-start.9 = (s16[272,1024]{1,0:T(8,128)(2,1)S(1)}, s16[272,1024]{1,0:T(8,128)(2,1)S(1)}, u32[]{:S(2)}, u32[]{:S(2)}) collective-permute-start(s16[272,1024]{1,0:T(8,128)(2,1)S(1)} %get-tuple-element.44), channel_id=1, source_target_pairs={{0,3},{1,2},{2,1},{3,0},{4,7},{5,6},{6,5},{7,4},{8,11},{9,10},{10,... | collective-permute-start | bytes 1671176 | tf_op jit(solution)/shard_map/ppermute | solution.py:54
  55.6 12.7 %collective-permute-start.5 = (s16[272,1024]{1,0:T(8,128)(2,1)S(1)}, s16[272,1024]{1,0:T(8,128)(2,1)S(1)}, u32[]{:S(2)}, u32[]{:S(2)}) collective-permute-start(s16[272,1024]{1,0:T(8,128)(2,1)S(1)} %get-tuple-element.37), channel_id=1, source_target_pairs={{0,3},{1,2},{2,1},{3,0},{4,7},{5,6},{6,5},{7,4},{8,11},{9,10},{10,... | collective-permute-start | bytes 1671176 | tf_op jit(solution)/shard_map/ppermute | solution.py:54
  63.5 11.9 %collective-permute-start.10 = (s16[272,1024]{1,0:T(8,128)(2,1)S(1)}, s16[272,1024]{1,0:T(8,128)(2,1)S(1)}, u32[]{:S(2)}, u32[]{:S(2)}) collective-permute-start(s16[272,1024]{1,0:T(8,128)(2,1)S(1)} %get-tuple-element.48), channel_id=1, source_target_pairs={{0,4},{1,5},{2,6},{3,7},{4,0},{5,1},{6,2},{7,3},{8,12},{9,13},{10,... | collective-permute-start | bytes 1671176 | tf_op jit(solution)/shard_map/ppermute | solution.py:54
  69.2 8.0 %collective-permute-start.11 = (s16[144,1024]{1,0:T(8,128)(2,1)S(1)}, s16[144,1024]{1,0:T(8,128)(2,1)S(1)}, u32[]{:S(2)}, u32[]{:S(2)}) collective-permute-start(s16[144,1024]{1,0:T(8,128)(2,1)S(1)} %get-tuple-element.46), channel_id=1, source_target_pairs={{0,12},{1,13},{2,14},{3,15},{4,8},{5,9},{6,10},{7,11},{8,4},{9,5},... | collective-permute-start | bytes 884744 | tf_op jit(solution)/shard_map/ppermute | solution.py:54
  76.4 6.8 %collective-permute-start.12 = (s16[144,1024]{1,0:T(8,128)(2,1)S(1)}, s16[144,1024]{1,0:T(8,128)(2,1)S(1)}, u32[]{:S(2)}, u32[]{:S(2)}) collective-permute-start(s16[144,1024]{1,0:T(8,128)(2,1)S(1)} %get-tuple-element.50), channel_id=1, source_target_pairs={{0,1},{1,0},{2,3},{3,2},{4,5},{5,4},{6,7},{7,6},{8,9},{9,8},{10,11... | collective-permute-start | bytes 884744 | tf_op jit(solution)/shard_map/ppermute | solution.py:54
  83.2 41.8 %copy-start.2 = (s32[8,8]{1,0:T(8,128)S(1)}, s32[8,8]{1,0:T(8,128)}, u32[]{:S(2)}) copy-start(s32[8,8]{1,0:T(8,128)} %flags_ref.1) | copy-start | bytes 772
  83.2 41.8 %copy-start.3 = (s32[8]{0:T(128)S(1)}, s32[8]{0:T(128)}, u32[]{:S(2)}) copy-start(s32[8]{0:T(128)} %order_ref.1) | copy-start | bytes 100
  127.0 1.3 collective-permute-start.13

commit v5 on v4

--- a/solution.py
+++ b/solution.py
@@ -18,10 +18,10 @@
 PARTNER = {"a": (1, 0, 3, 2), "b": (3, 2, 1, 0)}
 BIT = {"a": (0, 1, 1, 0), "b": (0, 0, 1, 1)}
 ORDER = {
-    (0, 0): ("xa", "ya", "xb", "yb", "z"),
-    (0, 1): ("yb", "xb", "ya", "xa", "z"),
-    (1, 0): ("ya", "xa", "yb", "xb", "z"),
-    (1, 1): ("xb", "yb", "xa", "ya", "z"),
+    (0, 0): ("xa", "yb", "xb", "ya", "z"),
+    (0, 1): ("yb", "xa", "ya", "xb", "z"),
+    (1, 0): ("ya", "xb", "xa", "yb", "z"),
+    (1, 1): ("xb", "ya", "yb", "xa", "z"),
 }
 FULL = 32000.0
 STEPS = 64.0
@@ -340,21 +340,21 @@
         matrix = jnp.where((sub == s) & (lane < 8), row, matrix)
     flags = flags_ref[...].astype(F32)
     small = lanes((8, 8), 1)
-    coefficients = jnp.where(lane == sub, 1.0, 0.0)
+    turned = jnp.where(lane == sub, 1.0, 0.0)
     for k in range(8):
         target = order_ref[k]
-        row = jnp.sum(jnp.where(sub == target, matrix, 0.0), axis=0, keepdims=True)
-        dots = jnp.sum(coefficients * row, axis=1, keepdims=True)
-        square = jnp.sum(jnp.where(lane[:1] == target, row, 0.0), axis=1, keepdims=True)
+        column = jnp.sum(jnp.where(lane == target, matrix, 0.0), axis=1, keepdims=True)
+        square = jnp.sum(jnp.where(sub[:, :1] == target, column, 0.0), axis=0, keepdims=True)
         active = jnp.sum(jnp.where(small == target, flags, 0.0), axis=1, keepdims=True)
         active = jnp.where(sub[:, :1] == target, 0.0, active)
+        active = jnp.sum(jnp.where(lane == sub, active, 0.0), axis=0, keepdims=True)
+        dots = jnp.sum(turned * column, axis=0, keepdims=True)
         removed = jnp.minimum(dots, 0.0) / square * active
-        coefficients = coefficients - jnp.where(lane == target, removed, 0.0)
-    weights = jnp.sum(coefficients, axis=0, keepdims=True)
+        turned = turned - jnp.where(sub == target, removed, 0.0)
+    weights = jnp.sum(jnp.where(lane < 8, turned, 0.0), axis=1, keepdims=True)
     total = None
     for t in range(8):
-        weight = jnp.sum(jnp.where(lane[:1] == t, weights, 0.0), axis=1, keepdims=True)
-        term = weight * grads_ref[t]
+        term = weights[t : t + 1] * grads_ref[t]
         total = term if total is None else total + term
     left, right = total[:, :128].astype(BF16), total[:, 128:].astype(BF16)
 
@@ -388,17 +388,22 @@
 
 def place_kernel(in_ref, out_ref):
     rows = in_ref.shape[1] // 4
-    for index, (zl, y, x) in enumerate(itertools.product(range(2), range(4), range(4))):
-        co = {"zl": zl, "y": y, "x": x}
-        for n in range(4):
-            at = (n * 32 + position(co, n // 2, n % 2)) * rows
-            out_ref[at : at + rows, :] = in_ref[index, n * rows : (n + 1) * rows, :]
+    for n in range(4):
+
+        @pl.when(pl.program_id(0) == n)
+        def _():
+            for index, (zl, y, x) in enumerate(itertools.product(range(2), range(4), range(4))):
+                at = position({"zl": zl, "y": y, "x": x}, n // 2, n % 2) * rows
+                out_ref[at : at + rows, :] = in_ref[index, n * rows : (n + 1) * rows, :]
 
 
 def place(gathered):
     count, rows, cols = gathered.shape
     return pl.pallas_call(
         place_kernel,
+        grid=(4,),
+        in_specs=[whole(gathered.shape)],
+        out_specs=pl.BlockSpec((count * rows // 4, cols), lambda n: (n, 0)),
         out_shape=jax.ShapeDtypeStruct((count * rows, cols), BF16),
         compiler_params=params(),
         cost_estimate=pl.CostEstimate(flops=0, bytes_accessed=4 * count * rows * cols, transcendentals=0),

time: 151 us -> 149 us (0.987)
  starting transfers between devices: 17.6 us -> 14.9 us
  waiting for transfers between devices: 32.5 us -> 34.1 us
    ppermute x12, starting transfers between devices: 17.5 us -> 14.8 us  [swap_along(): return lax.ppermute(value, AXES, pairs)]
    ppermute x12, waiting for transfers between devices: 31.3 us -> 32.9 us  [swap_along(): return lax.ppermute(value, AXES, pairs)]
  transfers between devices with their start and end apart: 14 -> 14, of which waited for: 7 -> 9; matrix products, arithmetic and copies ran while one was open for 13% -> 13% of each run, Pallas kernels for 9% -> 9%
where the time goes in v5:
time: 149 us
  blocking collectives  60.9 us (41%)
  waiting for transfers between devices  34.1 us (23%)
  matrix products  18.7 us (13%)
  Pallas kernels  17.9 us (12%)
  starting transfers between devices  14.9 us (10%)
  local copies, waits for them, and re-layouts  2.45 us (2%)
    ppermute x12, waiting for transfers between devices, swap_along(): return lax.ppermute(value, AXES, pairs)  32.9 us
    all_to_all x1, blocking collectives, on_device(): lax.all_to_all(copies, DP, split_axis=0, concat_axis=0, tiled=True)  21.3 us
    all_to_all x1, blocking collectives, on_device(): lax.all_to_all(blocks, ('zh', 'zl'), split_axis=0, concat_axis=0, tiled=T...  20.9 us
    all_to_all x1, blocking collectives, on_device(): grams = lax.all_to_all(grams, AXES, split_axis=0, concat_axis=0, tiled=True)  18.7 us
    dot_general x4, matrix products, term_of(): lax.dot_general(part, cot, (((0,), (0,)), ((), ())), preferred_element_ty...  18.7 us
    pallas_call x14, Pallas kernels, call(): pl.pallas_call(kernel, out_shape=out_shape, grid_spec=pltpu.PrefetchScala...  15.9 us
    ppermute x12, starting transfers between devices, swap_along(): return lax.ppermute(value, AXES, pairs)  14.8 us
  transfers between devices with their start and end apart: 14, of which 9 were waited for; matrix products, arithmetic and copies ran while one was open for 13% of the time, Pallas kernels for 9%

profile of v5, /device:TPU:32, one launch (start us, length us, event | category | flops | bytes accessed | tf_op | source)
XLA Modules:
  0.0 149.1 jit_solution(6132593284459114703)
XLA Ops:
  0.0 0.7 fusion.12.s_ref
  0.7 4.7 %fusion.6.term_ref = f32[1024,1024]{1,0:T(8,128)S(1)} fusion(bf16[1024,4096]{1,0:T(8,128)(2,1)} %param.5, s32[]{:T(128)S(6)} %select_n.25, bf16[1,1024,1024]{2,1,0:T(8,128)(2,1)} %param.6), kind=kOutput, calls=%fused_computation.6 | convolution fusion | flops 2147483648 | bytes 8388612 | tf_op jit(solution)/shard_map/dot_general | solution.py:150
  5.4 1.0 shard_map.55
  6.4 0.9 copy-done
  7.3 1.5 %collective-permute-start = (s16[528,1024]{1,0:T(8,128)(2,1)S(1)}, s16[528,1024]{1,0:T(8,128)(2,1)S(1)}, u32[]{:S(2)}, u32[]{:S(2)}) collective-permute-start(s16[528,1024]{1,0:T(8,128)(2,1)S(1)} %shard_map.55), channel_id=1, source_target_pairs={{0,1},{1,0},{2,3},{3,2},{4,5},{5,4},{6,7},{7,6},{8,9},{9,8},{10,11... | collective-permute-start | bytes 3244040 | tf_op jit(solution)/shard_map/ppermute | solution.py:54
  8.8 4.7 %fusion.2.term_ref = f32[1024,1024]{1,0:T(8,128)S(1)} fusion(bf16[1024,1024]{1,0:T(8,128)(2,1)} %bitcast.27, bf16[1024,4096]{1,0:T(8,128)(2,1)} %param.5, s32[]{:T(128)S(6)} %select_n.26), kind=kOutput, calls=%fused_computation.2 | convolution fusion | flops 2147483648 | bytes 8388612 | tf_op jit(solution)/shard_map/dot_general | solution.py:150
  13.5 1.0 shard_map.57
  14.5 3.1 %collective-permute-start.6 = (s16[528,1024]{1,0:T(8,128)(2,1)S(1)}, s16[528,1024]{1,0:T(8,128)(2,1)S(1)}, u32[]{:S(2)}, u32[]{:S(2)}) collective-permute-start(s16[528,1024]{1,0:T(8,128)(2,1)S(1)} %shard_map.57), channel_id=1, source_target_pairs={{0,12},{1,13},{2,14},{3,15},{4,8},{5,9},{6,10},{7,11},{8,4},{9,5},... | collective-permute-start | bytes 3244040 | tf_op jit(solution)/shard_map/ppermute | solution.py:54
  17.6 4.7 %fusion.4.term_ref = f32[1024,1024]{1,0:T(8,128)S(1)} fusion(bf16[1024,1024]{1,0:T(8,128)(2,1)} %collective-permute-done.1, bf16[1024,4096]{1,0:T(8,128)(2,1)} %param.5, s32[]{:T(128)S(6)} %select_n.25), kind=kOutput, calls=%fused_computation.4 | convolution fusion | flops 2147483648 | bytes 8388612 | tf_op jit(solution)/shard_map/dot_general | solution.py:150
  22.3 1.0 shard_map.58
  23.4 0.6 collective-permute-start.2
  24.0 4.7 %fusion.term_ref = f32[1024,1024]{1,0:T(8,128)S(1)} fusion(bf16[1024,1024]{1,0:T(8,128)(2,1)} %collective-permute-done.1, bf16[1024,4096]{1,0:T(8,128)(2,1)} %param.5, s32[]{:T(128)S(6)} %select_n.26), kind=kOutput, calls=%fused_computation | convolution fusion | flops 2147483648 | bytes 8388612 | tf_op jit(solution)/shard_map/dot_general | solution.py:150
  28.7 1.0 shard_map.63
  29.7 0.5 collective-permute-start.7
  30.2 0.6 copy-done.1
  30.8 1.2 shard_map.56
  32.1 2.5 %collective-permute-start.3 = (s16[272,1024]{1,0:T(8,128)(2,1)S(1)}, s16[272,1024]{1,0:T(8,128)(2,1)S(1)}, u32[]{:S(2)}, u32[]{:S(2)}) collective-permute-start(s16[272,1024]{1,0:T(8,128)(2,1)S(1)} %get-tuple-element.34), channel_id=1, source_target_pairs={{0,12},{1,13},{2,14},{3,15},{4,8},{5,9},{6,10},{7,11},{8,4},{9,5},... | collective-permute-start | bytes 1671176 | tf_op jit(solution)/shard_map/ppermute | solution.py:54
  34.6 4.0 %collective-permute-done.2.keep_in.give_in.codes_ref = s16[528,1024]{1,0:T(8,128)(2,1)S(1)} collective-permute-done((s16[528,1024]{1,0:T(8,128)(2,1)S(1)}, s16[528,1024]{1,0:T(8,128)(2,1)S(1)}, u32[]{:S(2)}, u32[]{:S(2)}) %collective-permute-start.2) | collective-permute-done | bytes 1081376 | tf_op jit(solution)/shard_map/ppermute | solution.py:54
  38.6 1.2 shard_map.59
  39.8 0.3 collective-permute-start.4
  40.1 1.2 shard_map.62
  41.4 0.6 collective-permute-start.8
  42.0 4.3 %collective-permute-done.7.keep_in.give_in.codes_ref = s16[528,1024]{1,0:T(8,128)(2,1)S(1)} collective-permute-done((s16[528,1024]{1,0:T(8,128)(2,1)S(1)}, s16[528,1024]{1,0:T(8,128)(2,1)S(1)}, u32[]{:S(2)}, u32[]{:S(2)}) %collective-permute-start.7) | collective-permute-done | bytes 1081376 | tf_op jit(solution)/shard_map/ppermute | solution.py:54
  46.4 1.2 shard_map.64
  47.6 1.6 %collective-permute-start.9 = (s16[272,1024]{1,0:T(8,128)(2,1)S(1)}, s16[272,1024]{1,0:T(8,128)(2,1)S(1)}, u32[]{:S(2)}, u32[]{:S(2)}) collective-permute-start(s16[272,1024]{1,0:T(8,128)(2,1)S(1)} %get-tuple-element.44), channel_id=1, source_target_pairs={{0,1},{1,0},{2,3},{3,2},{4,5},{5,4},{6,7},{7,6},{8,9},{9,8},{10,11... | collective-permute-start | bytes 1671176 | tf_op jit(solution)/shard_map/ppermute | solution.py:54
  49.2 3.1 %collective-permute-done.3.in_a = s16[272,1024]{1,0:T(8,128)(2,1)S(1)} collective-permute-done((s16[272,1024]{1,0:T(8,128)(2,1)S(1)}, s16[272,1024]{1,0:T(8,128)(2,1)S(1)}, u32[]{:S(2)}, u32[]{:S(2)}) %collective-permute-start.3) | collective-permute-done | bytes 557088 | tf_op jit(solution)/shard_map/ppermute | solution.py:54
  52.3 6.0 %collective-permute-done.4.in_b = s16[272,1024]{1,0:T(8,128)(2,1)S(1)} collective-permute-done((s16[272,1024]{1,0:T(8,128)(2,1)S(1)}, s16[272,1024]{1,0:T(8,128)(2,1)S(1)}, u32[]{:S(2)}, u32[]{:S(2)}) %collective-permute-start.4) | collective-permute-done | bytes 557088 | tf_op jit(solution)/shard_map/ppermute | solution.py:54
  58.3 1.2 shard_map.60
  59.5 2.8 %collective-permute-start.5 = (s16[272,1024]{1,0:T(8,128)(2,1)S(1)}, s16[272,1024]{1,0:T(8,128)(2,1)S(1)}, u32[]{:S(2)}, u32[]{:S(2)}) collective-permute-start(s16[272,1024]{1,0:T(8,128)(2,1)S(1)} %get-tuple-element.37), channel_id=1, source_target_pairs={{0,3},{1,2},{2,1},{3,0},{4,7},{5,6},{6,5},{7,4},{8,11},{9,10},{10,... | collective-permute-start | bytes 1671176 | tf_op jit(solution)/shard_map/ppermute | solution.py:54
  62.3 1.2 shard_map.65
  63.6 0.1 collective-permute-start.10
  63.7 6.7 %collective-permute-done.5.keep_in.give_in.codes_ref = s16[272,1024]{1,0:T(8,128)(2,1)S(1)} collective-permute-done((s16[272,1024]{1,0:T(8,128)(2,1)S(1)}, s16[272,1024]{1,0:T(8,128)(2,1)S(1)}, u32[]{:S(2)}, u32[]{:S(2)}) %collective-permute-start.5) | collective-permute-done | bytes 557088 | tf_op jit(solution)/shard_map/ppermute | solution.py:54
  70.3 0.9 shard_map.61
  71.3 0.1 collective-permute-start.11
  71.4 1.8 %collective-permute-done.10.keep_in.give_in.codes_ref = s16[272,1024]{1,0:T(8,128)(2,1)S(1)} collective-permute-done((s16[272,1024]{1,0:T(8,128)(2,1)S(1)}, s16[272,1024]{1,0:T(8,128)(2,1)S(1)}, u32[]{:S(2)}, u32[]{:S(2)}) %collective-permute-start.10) | collective-permute-done | bytes 557088 | tf_op jit(solution)/shard_map/ppermute | solution.py:54
  73.2 0.9 shard_map.66
  74.1 1.1 collective-permute-start.12
  75.2 2.9 %collective-permute-done.11.in_a = s16[144,1024]{1,0:T(8,128)(2,1)S(1)} collective-permute-done((s16[144,1024]{1,0:T(8,128)(2,1)S(1)}, s16[144,1024]{1,0:T(8,128)(2,1)S(1)}, u32[]{:S(2)}, u32[]{:S(2)}) %collective-permute-start.11) | collective-permute-done | bytes 294944 | tf_op jit(solution)/shard_map/ppermute | solution.py:54
  78.1 4.1 %collective-permute-done.12.in_b = s16[144,1024]{1,0:T(8,128)(2,1)S(1)} collective-permute-done((s16[144,1024]{1,0:T(8,128)(2,1)S(1)}, s16[144,1024]{1,0:T(8,128)(2,1)S(1)}, u32[]{:S(2)}, u32[]{:S(2)}) %collective-permute-start.12) | collective-permute-done | bytes 294944 | tf_op jit(solution)/shard_map/ppermute | solution.py:54
  82.1 0.4 shard_map.67
  82.6 20.9 %all_to_all.21.in_ref = s16[8,144,256]{2,1,0:T(8,128)(2,1)S(1)} all-to-all(s16[8,144,256]{2,1,0:T(8,128)(2,1)S(1)} %shard_map.67), channel_id=1, replica_groups=mesh['zh'=4,'core'=2,'zl'=2,'y'=4,'x'=4] {'zh','zl'}, dimensions={0} | all-to-all | bytes 1179648 | tf_op jit(solution)/shard_map/all_to_all | solution.py:450
  103.4 1.0 shard_map.68
  104.5 18.7 %all_to_all.22 = f32[256,1,128]{2,1,0:T(1,128)S(1)} all-to-all(f32[256,1,128]{2,1,0:T(1,128)S(1)} %bitcast.25), channel_id=1, replica_groups=mesh['zh'=4,'core'=2,'zl'=2,'y'=4,'x'=4] {'zh','core','zl','y','x'}, dimensions={0} | all-to-all | bytes 262144 | tf_op jit(solution)/shard_map/all_to_all | solution.py:452
  123.2 1.5 shard_map.69
  124.8 1.2 collective-permute-done.13
  125.9 0.2 broadcast_in_dim.19
  126.2 21.3 %all_to_all.23.in_ref = bf16[32,128,128]{2,1,0:T(8,128)(2,1)S(1)} all-to-all(bf16[32,128,128]{2,1,0:T(8,128)(2,1)S(1)} %broadcast_in_dim.19), channel_id=1, replica_groups=mesh['zh'=4,'core'=2,'zl'=2,'y'=4,'x'=4] {'zl','y','x'}, dimensions={0} | all-to-all | bytes 2097152 | tf_op jit(solution)/shard_map/all_to_all | solution.py:459
  147.5 1.5 %shard_map.70 = bf16[4096,128]{1,0:T(8,128)(2,1)} custom-call(bf16[32,128,128]{2,1,0:T(8,128)(2,1)S(1)} %all_to_all.23.in_ref), custom_call_target="tpu_custom_call" | custom-call | bytes 2097152 | tf_op jit(solution)/shard_map/pallas_call | solution.py:402
  (15 shorter events, 0.1 us)
Async XLA Ops:
  0.0 17.6 %collective-permute-start.1 = (bf16[1024,1024]{1,0:T(8,128)(2,1)}, bf16[1024,1024]{1,0:T(8,128)(2,1)}, u32[]{:S(2)}, u32[]{:S(2)}) collective-permute-start(bf16[1024,1024]{1,0:T(8,128)(2,1)} %bitcast.26), channel_id=1, source_target_pairs={{0,32},{32,0},{1,33},{33,1},{2,34},{34,2},{3,35},{35,3},{4,36},{36... | collective-permute-start | bytes 6291464 | tf_op jit(solution)/shard_map/ppermute | solution.py:417
  5.4 1.9 %copy-start = (f32[1024,1024]{1,0:T(8,128)}, f32[1024,1024]{1,0:T(8,128)S(1)}, u32[]{:S(2)}) copy-start(f32[1024,1024]{1,0:T(8,128)S(1)} %fusion.6.term_ref) | copy-start | bytes 12582916
  7.3 22.9 %collective-permute-start = (s16[528,1024]{1,0:T(8,128)(2,1)S(1)}, s16[528,1024]{1,0:T(8,128)(2,1)S(1)}, u32[]{:S(2)}, u32[]{:S(2)}) collective-permute-start(s16[528,1024]{1,0:T(8,128)(2,1)S(1)} %shard_map.55), channel_id=1, source_target_pairs={{0,1},{1,0},{2,3},{3,2},{4,5},{5,4},{6,7},{7,6},{8,9},{9,8},{10,11... | collective-permute-start | bytes 3244040 | tf_op jit(solution)/shard_map/ppermute | solution.py:54
  14.5 25.6 %collective-permute-start.6 = (s16[528,1024]{1,0:T(8,128)(2,1)S(1)}, s16[528,1024]{1,0:T(8,128)(2,1)S(1)}, u32[]{:S(2)}, u32[]{:S(2)}) collective-permute-start(s16[528,1024]{1,0:T(8,128)(2,1)S(1)} %shard_map.57), channel_id=1, source_target_pairs={{0,12},{1,13},{2,14},{3,15},{4,8},{5,9},{6,10},{7,11},{8,4},{9,5},... | collective-permute-start | bytes 3244040 | tf_op jit(solution)/shard_map/ppermute | solution.py:54
  23.4 15.2 %collective-permute-start.2 = (s16[528,1024]{1,0:T(8,128)(2,1)S(1)}, s16[528,1024]{1,0:T(8,128)(2,1)S(1)}, u32[]{:S(2)}, u32[]{:S(2)}) collective-permute-start(s16[528,1024]{1,0:T(8,128)(2,1)S(1)} %shard_map.58), channel_id=1, source_target_pairs={{0,1},{1,0},{2,3},{3,2},{4,5},{5,4},{6,7},{7,6},{8,9},{9,8},{10,11... | collective-permute-start | bytes 3244040 | tf_op jit(solution)/shard_map/ppermute | solution.py:54
  28.7 2.2 %copy-start.1 = (f32[1024,1024]{1,0:T(8,128)S(1)}, f32[1024,1024]{1,0:T(8,128)}, u32[]{:S(2)}) copy-start(f32[1024,1024]{1,0:T(8,128)} %copy-done) | copy-start | bytes 12582916
  29.7 16.6 %collective-permute-start.7 = (s16[528,1024]{1,0:T(8,128)(2,1)S(1)}, s16[528,1024]{1,0:T(8,128)(2,1)S(1)}, u32[]{:S(2)}, u32[]{:S(2)}) collective-permute-start(s16[528,1024]{1,0:T(8,128)(2,1)S(1)} %shard_map.63), channel_id=1, source_target_pairs={{0,12},{1,13},{2,14},{3,15},{4,8},{5,9},{6,10},{7,11},{8,4},{9,5},... | collective-permute-start | bytes 3244040 | tf_op jit(solution)/shard_map/ppermute | solution.py:54
  32.1 20.2 %collective-permute-start.3 = (s16[272,1024]{1,0:T(8,128)(2,1)S(1)}, s16[272,1024]{1,0:T(8,128)(2,1)S(1)}, u32[]{:S(2)}, u32[]{:S(2)}) collective-permute-start(s16[272,1024]{1,0:T(8,128)(2,1)S(1)} %get-tuple-element.34), channel_id=1, source_target_pairs={{0,12},{1,13},{2,14},{3,15},{4,8},{5,9},{6,10},{7,11},{8,4},{9,5},... | collective-permute-start | bytes 1671176 | tf_op jit(solution)/shard_map/ppermute | solution.py:54
  39.8 18.5 %collective-permute-start.4 = (s16[272,1024]{1,0:T(8,128)(2,1)S(1)}, s16[272,1024]{1,0:T(8,128)(2,1)S(1)}, u32[]{:S(2)}, u32[]{:S(2)}) collective-permute-start(s16[272,1024]{1,0:T(8,128)(2,1)S(1)} %get-tuple-element.35), channel_id=1, source_target_pairs={{0,12},{1,13},{2,14},{3,15},{4,8},{5,9},{6,10},{7,11},{8,4},{9,5},... | collective-permute-start | bytes 1671176 | tf_op jit(solution)/shard_map/ppermute | solution.py:54
  41.4 21.0 %collective-permute-start.8 = (s16[272,1024]{1,0:T(8,128)(2,1)S(1)}, s16[272,1024]{1,0:T(8,128)(2,1)S(1)}, u32[]{:S(2)}, u32[]{:S(2)}) collective-permute-start(s16[272,1024]{1,0:T(8,128)(2,1)S(1)} %get-tuple-element.43), channel_id=1, source_target_pairs={{0,1},{1,0},{2,3},{3,2},{4,5},{5,4},{6,7},{7,6},{8,9},{9,8},{10,11... | collective-permute-start | bytes 1671176 | tf_op jit(solution)/shard_map/ppermute | solution.py:54
  47.6 14.7 %collective-permute-start.9 = (s16[272,1024]{1,0:T(8,128)(2,1)S(1)}, s16[272,1024]{1,0:T(8,128)(2,1)S(1)}, u32[]{:S(2)}, u32[]{:S(2)}) collective-permute-start(s16[272,1024]{1,0:T(8,128)(2,1)S(1)} %get-tuple-element.44), channel_id=1, source_target_pairs={{0,1},{1,0},{2,3},{3,2},{4,5},{5,4},{6,7},{7,6},{8,9},{9,8},{10,11... | collective-permute-start | bytes 1671176 | tf_op jit(solution)/shard_map/ppermute | solution.py:54
  59.5 10.8 %collective-permute-start.5 = (s16[272,1024]{1,0:T(8,128)(2,1)S(1)}, s16[272,1024]{1,0:T(8,128)(2,1)S(1)}, u32[]{:S(2)}, u32[]{:S(2)}) collective-permute-start(s16[272,1024]{1,0:T(8,128)(2,1)S(1)} %get-tuple-element.37), channel_id=1, source_target_pairs={{0,3},{1,2},{2,1},{3,0},{4,7},{5,6},{6,5},{7,4},{8,11},{9,10},{10,... | collective-permute-start | bytes 1671176 | tf_op jit(solution)/shard_map/ppermute | solution.py:54
  63.6 9.6 %collective-permute-start.10 = (s16[272,1024]{1,0:T(8,128)(2,1)S(1)}, s16[272,1024]{1,0:T(8,128)(2,1)S(1)}, u32[]{:S(2)}, u32[]{:S(2)}) collective-permute-start(s16[272,1024]{1,0:T(8,128)(2,1)S(1)} %get-tuple-element.48), channel_id=1, source_target_pairs={{0,4},{1,5},{2,6},{3,7},{4,0},{5,1},{6,2},{7,3},{8,12},{9,13},{10,... | collective-permute-start | bytes 1671176 | tf_op jit(solution)/shard_map/ppermute | solution.py:54
  71.3 6.8 %collective-permute-start.11 = (s16[144,1024]{1,0:T(8,128)(2,1)S(1)}, s16[144,1024]{1,0:T(8,128)(2,1)S(1)}, u32[]{:S(2)}, u32[]{:S(2)}) collective-permute-start(s16[144,1024]{1,0:T(8,128)(2,1)S(1)} %get-tuple-element.46), channel_id=1, source_target_pairs={{0,4},{1,5},{2,6},{3,7},{4,0},{5,1},{6,2},{7,3},{8,12},{9,13},{10,... | collective-permute-start | bytes 884744 | tf_op jit(solution)/shard_map/ppermute | solution.py:54
  74.1 8.0 %collective-permute-start.12 = (s16[144,1024]{1,0:T(8,128)(2,1)S(1)}, s16[144,1024]{1,0:T(8,128)(2,1)S(1)}, u32[]{:S(2)}, u32[]{:S(2)}) collective-permute-start(s16[144,1024]{1,0:T(8,128)(2,1)S(1)} %get-tuple-element.50), channel_id=1, source_target_pairs={{0,3},{1,2},{2,1},{3,0},{4,7},{5,6},{6,5},{7,4},{8,11},{9,10},{10,... | collective-permute-start | bytes 884744 | tf_op jit(solution)/shard_map/ppermute | solution.py:54
  82.1 41.0 %copy-start.2 = (s32[8,8]{1,0:T(8,128)S(1)}, s32[8,8]{1,0:T(8,128)}, u32[]{:S(2)}) copy-start(s32[8,8]{1,0:T(8,128)} %flags_ref.1) | copy-start | bytes 772
  82.1 41.0 %copy-start.3 = (s32[8]{0:T(128)S(1)}, s32[8]{0:T(128)}, u32[]{:S(2)}) copy-start(s32[8]{0:T(128)} %order_ref.1) | copy-start | bytes 100
  124.7 1.3 collective-permute-start.13

commit v6 on v3

--- a/solution.py
+++ b/solution.py
@@ -340,21 +340,21 @@
         matrix = jnp.where((sub == s) & (lane < 8), row, matrix)
     flags = flags_ref[...].astype(F32)
     small = lanes((8, 8), 1)
-    coefficients = jnp.where(lane == sub, 1.0, 0.0)
+    turned = jnp.where(lane == sub, 1.0, 0.0)
     for k in range(8):
         target = order_ref[k]
-        row = jnp.sum(jnp.where(sub == target, matrix, 0.0), axis=0, keepdims=True)
-        dots = jnp.sum(coefficients * row, axis=1, keepdims=True)
-        square = jnp.sum(jnp.where(lane[:1] == target, row, 0.0), axis=1, keepdims=True)
+        column = jnp.sum(jnp.where(lane == target, matrix, 0.0), axis=1, keepdims=True)
+        square = jnp.sum(jnp.where(sub[:, :1] == target, column, 0.0), axis=0, keepdims=True)
         active = jnp.sum(jnp.where(small == target, flags, 0.0), axis=1, keepdims=True)
         active = jnp.where(sub[:, :1] == target, 0.0, active)
+        active = jnp.sum(jnp.where(lane == sub, active, 0.0), axis=0, keepdims=True)
+        dots = jnp.sum(turned * column, axis=0, keepdims=True)
         removed = jnp.minimum(dots, 0.0) / square * active
-        coefficients = coefficients - jnp.where(lane == target, removed, 0.0)
-    weights = jnp.sum(coefficients, axis=0, keepdims=True)
+        turned = turned - jnp.where(sub == target, removed, 0.0)
+    weights = jnp.sum(jnp.where(lane < 8, turned, 0.0), axis=1, keepdims=True)
     total = None
     for t in range(8):
-        weight = jnp.sum(jnp.where(lane[:1] == t, weights, 0.0), axis=1, keepdims=True)
-        term = weight * grads_ref[t]
+        term = weights[t : t + 1] * grads_ref[t]
         total = term if total is None else total + term
     left, right = total[:, :128].astype(BF16), total[:, 128:].astype(BF16)
 
@@ -425,14 +425,17 @@
         arrived[task, chunk] = swap_along(coded, dims[chunk][0])
     for at in keys:
         chunk = at[1]
-        kept[at], coded = level(table, slots[chunk] + 1, terms[at][None], arrived[at], slots[chunk])
+        term = terms[at][None]
+        if at != keys[0]:
+            term = after(term, coded)
+        kept[at], coded = level(table, slots[chunk] + 1, term, arrived[at], slots[chunk])
         arrived[at] = swap_along(coded, dims[chunk][1])
     joined, taken = {}, {}
+    coded = arrived[keys[0]]
     for chunk in (1, 0):
         pair = [(task, chunk) for task in range(2)]
         sums = [kept[at] for at in pair]
-        if chunk == 0:
-            sums[0] = after(sums[0], coded)
+        sums[0] = after(sums[0], coded)
         joined[chunk], coded = join_tasks(table, slots[chunk] + 2, sums, [arrived[at] for at in pair])
         taken[chunk] = swap_along(coded, dims[chunk][2])
     for chunk in (1, 0):

time: 161 us -> 149 us (0.925)
  waiting for transfers between devices: 38.4 us -> 29.6 us
    ppermute x12, waiting for transfers between devices: 37.3 us -> 28.5 us  [swap_along(): return lax.ppermute(value, AXES, pairs)]
  transfers between devices with their start and end apart: 14 -> 14, of which waited for: 9 -> 10; matrix products, arithmetic and copies ran while one was open for 12% -> 13% of each run, Pallas kernels for 8% -> 8%
where the time goes in v6:
time: 149 us
  blocking collectives  61.9 us (42%)
  waiting for transfers between devices  29.6 us (20%)
  starting transfers between devices  18.7 us (13%)
  matrix products  18.7 us (13%)
  Pallas kernels  17.4 us (12%)
  local copies, waits for them, and re-layouts  2.45 us (2%)
    ppermute x12, waiting for transfers between devices, swap_along(): return lax.ppermute(value, AXES, pairs)  28.5 us
    all_to_all x1, blocking collectives, on_device(): lax.all_to_all(copies, DP, split_axis=0, concat_axis=0, tiled=True)  21.3 us
    all_to_all x1, blocking collectives, on_device(): lax.all_to_all(blocks, ('zh', 'zl'), split_axis=0, concat_axis=0, tiled=T...  21.1 us
    all_to_all x1, blocking collectives, on_device(): grams = lax.all_to_all(grams, AXES, split_axis=0, concat_axis=0, tiled=True)  19.5 us
    dot_general x4, matrix products, term_of(): lax.dot_general(part, cot, (((0,), (0,)), ((), ())), preferred_element_ty...  18.7 us
    ppermute x12, starting transfers between devices, swap_along(): return lax.ppermute(value, AXES, pairs)  18.6 us
    pallas_call x14, Pallas kernels, call(): pl.pallas_call(kernel, out_shape=out_shape, grid_spec=pltpu.PrefetchScala...  15.9 us
  transfers between devices with their start and end apart: 14, of which 10 were waited for; matrix products, arithmetic and copies ran while one was open for 13% of the time, Pallas kernels for 8%

profile of v6, /device:TPU:32, one launch (start us, length us, event | category | flops | bytes accessed | tf_op | source)
XLA Modules:
  0.0 149.0 jit_solution(17331100423786842071)
XLA Ops:
  0.0 0.7 fusion.12.s_ref
  0.7 4.7 %fusion.6.term_ref = f32[1024,1024]{1,0:T(8,128)S(1)} fusion(bf16[1024,4096]{1,0:T(8,128)(2,1)} %param.5, s32[]{:T(128)S(6)} %select_n.25, bf16[1,1024,1024]{2,1,0:T(8,128)(2,1)} %param.6), kind=kOutput, calls=%fused_computation.6 | convolution fusion | flops 2147483648 | bytes 8388612 | tf_op jit(solution)/shard_map/dot_general | solution.py:150
  5.4 1.0 shard_map.55
  6.4 0.9 copy-done
  7.3 1.5 %collective-permute-start = (s16[528,1024]{1,0:T(8,128)(2,1)S(1)}, s16[528,1024]{1,0:T(8,128)(2,1)S(1)}, u32[]{:S(2)}, u32[]{:S(2)}) collective-permute-start(s16[528,1024]{1,0:T(8,128)(2,1)S(1)} %shard_map.55), channel_id=1, source_target_pairs={{0,1},{1,0},{2,3},{3,2},{4,5},{5,4},{6,7},{7,6},{8,9},{9,8},{10,11... | collective-permute-start | bytes 3244040 | tf_op jit(solution)/shard_map/ppermute | solution.py:54
  8.8 4.7 %fusion.2.term_ref = f32[1024,1024]{1,0:T(8,128)S(1)} fusion(bf16[1024,1024]{1,0:T(8,128)(2,1)} %bitcast.27, bf16[1024,4096]{1,0:T(8,128)(2,1)} %param.5, s32[]{:T(128)S(6)} %select_n.26), kind=kOutput, calls=%fused_computation.2 | convolution fusion | flops 2147483648 | bytes 8388612 | tf_op jit(solution)/shard_map/dot_general | solution.py:150
  13.5 1.0 shard_map.57
  14.5 3.1 %collective-permute-start.1 = (s16[528,1024]{1,0:T(8,128)(2,1)S(1)}, s16[528,1024]{1,0:T(8,128)(2,1)S(1)}, u32[]{:S(2)}, u32[]{:S(2)}) collective-permute-start(s16[528,1024]{1,0:T(8,128)(2,1)S(1)} %shard_map.57), channel_id=1, source_target_pairs={{0,12},{1,13},{2,14},{3,15},{4,8},{5,9},{6,10},{7,11},{8,4},{9,5},... | collective-permute-start | bytes 3244040 | tf_op jit(solution)/shard_map/ppermute | solution.py:54
  17.6 4.7 %fusion.4.term_ref = f32[1024,1024]{1,0:T(8,128)S(1)} fusion(bf16[1024,1024]{1,0:T(8,128)(2,1)} %collective-permute-done.3, bf16[1024,4096]{1,0:T(8,128)(2,1)} %param.5, s32[]{:T(128)S(6)} %select_n.25), kind=kOutput, calls=%fused_computation.4 | convolution fusion | flops 2147483648 | bytes 8388612 | tf_op jit(solution)/shard_map/dot_general | solution.py:150
  22.3 1.0 shard_map.59
  23.4 0.6 collective-permute-start.4
  24.0 4.7 %fusion.term_ref = f32[1024,1024]{1,0:T(8,128)S(1)} fusion(bf16[1024,1024]{1,0:T(8,128)(2,1)} %collective-permute-done.3, bf16[1024,4096]{1,0:T(8,128)(2,1)} %param.5, s32[]{:T(128)S(6)} %select_n.26), kind=kOutput, calls=%fused_computation | convolution fusion | flops 2147483648 | bytes 8388612 | tf_op jit(solution)/shard_map/dot_general | solution.py:150
  28.7 1.0 shard_map.61
  29.7 0.5 collective-permute-start.5
  30.2 0.6 copy-done.1
  30.8 1.2 shard_map.56
  32.1 2.5 %collective-permute-start.2 = (s16[272,1024]{1,0:T(8,128)(2,1)S(1)}, s16[272,1024]{1,0:T(8,128)(2,1)S(1)}, u32[]{:S(2)}, u32[]{:S(2)}) collective-permute-start(s16[272,1024]{1,0:T(8,128)(2,1)S(1)} %get-tuple-element.36), channel_id=1, source_target_pairs={{0,12},{1,13},{2,14},{3,15},{4,8},{5,9},{6,10},{7,11},{8,4},{9,5},... | collective-permute-start | bytes 1671176 | tf_op jit(solution)/shard_map/ppermute | solution.py:54
  34.6 1.2 shard_map.58
  35.8 1.6 %collective-permute-start.6 = (s16[272,1024]{1,0:T(8,128)(2,1)S(1)}, s16[272,1024]{1,0:T(8,128)(2,1)S(1)}, u32[]{:S(2)}, u32[]{:S(2)}) collective-permute-start(s16[272,1024]{1,0:T(8,128)(2,1)S(1)} %get-tuple-element.42), channel_id=1, source_target_pairs={{0,1},{1,0},{2,3},{3,2},{4,5},{5,4},{6,7},{7,6},{8,9},{9,8},{10,11... | collective-permute-start | bytes 1671176 | tf_op jit(solution)/shard_map/ppermute | solution.py:54
  37.4 1.2 collective-permute-done.4.keep_in.give_in.codes_ref
  38.6 1.2 shard_map.60
  39.8 6.5 %collective-permute-done.5.keep_in.give_in.codes_ref = s16[528,1024]{1,0:T(8,128)(2,1)S(1)} collective-permute-done((s16[528,1024]{1,0:T(8,128)(2,1)S(1)}, s16[528,1024]{1,0:T(8,128)(2,1)S(1)}, u32[]{:S(2)}, u32[]{:S(2)}) %collective-permute-start.5) | collective-permute-done | bytes 1081376 | tf_op jit(solution)/shard_map/ppermute | solution.py:54
  46.3 1.2 shard_map.62
  47.6 1.6 %collective-permute-start.7 = (s16[272,1024]{1,0:T(8,128)(2,1)S(1)}, s16[272,1024]{1,0:T(8,128)(2,1)S(1)}, u32[]{:S(2)}, u32[]{:S(2)}) collective-permute-start(s16[272,1024]{1,0:T(8,128)(2,1)S(1)} %get-tuple-element.47), channel_id=1, source_target_pairs={{0,1},{1,0},{2,3},{3,2},{4,5},{5,4},{6,7},{7,6},{8,9},{9,8},{10,11... | collective-permute-start | bytes 1671176 | tf_op jit(solution)/shard_map/ppermute | solution.py:54
  49.2 0.2 collective-permute-start.8
  49.4 2.9 %collective-permute-done.2.in_a = s16[272,1024]{1,0:T(8,128)(2,1)S(1)} collective-permute-done((s16[272,1024]{1,0:T(8,128)(2,1)S(1)}, s16[272,1024]{1,0:T(8,128)(2,1)S(1)}, u32[]{:S(2)}, u32[]{:S(2)}) %collective-permute-start.2) | collective-permute-done | bytes 557088 | tf_op jit(solution)/shard_map/ppermute | solution.py:54
  52.3 4.9 %collective-permute-done.7.in_b = s16[272,1024]{1,0:T(8,128)(2,1)S(1)} collective-permute-done((s16[272,1024]{1,0:T(8,128)(2,1)S(1)}, s16[272,1024]{1,0:T(8,128)(2,1)S(1)}, u32[]{:S(2)}, u32[]{:S(2)}) %collective-permute-start.7) | collective-permute-done | bytes 557088 | tf_op jit(solution)/shard_map/ppermute | solution.py:54
  57.2 1.2 shard_map.63
  58.5 1.4 collective-permute-done.8.in_b
  59.9 1.2 shard_map.64
  61.1 3.6 %collective-permute-start.10 = (s16[272,1024]{1,0:T(8,128)(2,1)S(1)}, s16[272,1024]{1,0:T(8,128)(2,1)S(1)}, u32[]{:S(2)}, u32[]{:S(2)}) collective-permute-start(s16[272,1024]{1,0:T(8,128)(2,1)S(1)} %get-tuple-element.55), channel_id=1, source_target_pairs={{0,3},{1,2},{2,1},{3,0},{4,7},{5,6},{6,5},{7,4},{8,11},{9,10},{10,... | collective-permute-start | bytes 1671176 | tf_op jit(solution)/shard_map/ppermute | solution.py:54
  64.7 3.4 %collective-permute-done.9.keep_in.give_in.codes_ref = s16[272,1024]{1,0:T(8,128)(2,1)S(1)} collective-permute-done((s16[272,1024]{1,0:T(8,128)(2,1)S(1)}, s16[272,1024]{1,0:T(8,128)(2,1)S(1)}, u32[]{:S(2)}, u32[]{:S(2)}) %collective-permute-start.9) | collective-permute-done | bytes 557088 | tf_op jit(solution)/shard_map/ppermute | solution.py:54
  68.0 0.9 shard_map.65
  69.0 3.2 %collective-permute-done.10.keep_in.give_in.codes_ref = s16[272,1024]{1,0:T(8,128)(2,1)S(1)} collective-permute-done((s16[272,1024]{1,0:T(8,128)(2,1)S(1)}, s16[272,1024]{1,0:T(8,128)(2,1)S(1)}, u32[]{:S(2)}, u32[]{:S(2)}) %collective-permute-start.10) | collective-permute-done | bytes 557088 | tf_op jit(solution)/shard_map/ppermute | solution.py:54
  72.2 0.9 shard_map.66
  73.1 0.5 collective-permute-start.11
  73.6 3.0 %collective-permute-start.12 = (s16[144,1024]{1,0:T(8,128)(2,1)S(1)}, s16[144,1024]{1,0:T(8,128)(2,1)S(1)}, u32[]{:S(2)}, u32[]{:S(2)}) collective-permute-start(s16[144,1024]{1,0:T(8,128)(2,1)S(1)} %get-tuple-element.53), channel_id=1, source_target_pairs={{0,3},{1,2},{2,1},{3,0},{4,7},{5,6},{6,5},{7,4},{8,11},{9,10},{10,... | collective-permute-start | bytes 884744 | tf_op jit(solution)/shard_map/ppermute | solution.py:54
  76.6 3.4 %collective-permute-done.11.in_a = s16[144,1024]{1,0:T(8,128)(2,1)S(1)} collective-permute-done((s16[144,1024]{1,0:T(8,128)(2,1)S(1)}, s16[144,1024]{1,0:T(8,128)(2,1)S(1)}, u32[]{:S(2)}, u32[]{:S(2)}) %collective-permute-start.11) | collective-permute-done | bytes 294944 | tf_op jit(solution)/shard_map/ppermute | solution.py:54
  80.0 1.6 %collective-permute-done.12.in_b = s16[144,1024]{1,0:T(8,128)(2,1)S(1)} collective-permute-done((s16[144,1024]{1,0:T(8,128)(2,1)S(1)}, s16[144,1024]{1,0:T(8,128)(2,1)S(1)}, u32[]{:S(2)}, u32[]{:S(2)}) %collective-permute-start.12) | collective-permute-done | bytes 294944 | tf_op jit(solution)/shard_map/ppermute | solution.py:54
  81.5 0.4 shard_map.67
  82.0 21.1 %all_to_all.21.in_ref = s16[8,144,256]{2,1,0:T(8,128)(2,1)S(1)} all-to-all(s16[8,144,256]{2,1,0:T(8,128)(2,1)S(1)} %shard_map.67), channel_id=1, replica_groups=mesh['zh'=4,'core'=2,'zl'=2,'y'=4,'x'=4] {'zh','zl'}, dimensions={0} | all-to-all | bytes 1179648 | tf_op jit(solution)/shard_map/all_to_all | solution.py:447
  103.1 1.0 shard_map.68
  104.1 19.5 %all_to_all.22 = f32[256,1,128]{2,1,0:T(1,128)S(1)} all-to-all(f32[256,1,128]{2,1,0:T(1,128)S(1)} %bitcast.25), channel_id=1, replica_groups=mesh['zh'=4,'core'=2,'zl'=2,'y'=4,'x'=4] {'zh','core','zl','y','x'}, dimensions={0} | all-to-all | bytes 262144 | tf_op jit(solution)/shard_map/all_to_all | solution.py:449
  123.6 1.5 shard_map.69
  125.2 1.2 collective-permute-done.13
  126.4 0.2 broadcast_in_dim.19
  126.6 21.3 %all_to_all.23.in_ref = bf16[32,128,128]{2,1,0:T(8,128)(2,1)S(1)} all-to-all(bf16[32,128,128]{2,1,0:T(8,128)(2,1)S(1)} %broadcast_in_dim.19), channel_id=1, replica_groups=mesh['zh'=4,'core'=2,'zl'=2,'y'=4,'x'=4] {'zl','y','x'}, dimensions={0} | all-to-all | bytes 2097152 | tf_op jit(solution)/shard_map/all_to_all | solution.py:456
  148.0 1.0 shard_map.70
  (15 shorter events, 0.2 us)
Async XLA Ops:
  0.0 17.6 %collective-permute-start.3 = (bf16[1024,1024]{1,0:T(8,128)(2,1)}, bf16[1024,1024]{1,0:T(8,128)(2,1)}, u32[]{:S(2)}, u32[]{:S(2)}) collective-permute-start(bf16[1024,1024]{1,0:T(8,128)(2,1)} %bitcast.26), channel_id=1, source_target_pairs={{0,32},{32,0},{1,33},{33,1},{2,34},{34,2},{3,35},{35,3},{4,36},{36... | collective-permute-start | bytes 6291464 | tf_op jit(solution)/shard_map/ppermute | solution.py:412
  5.4 1.9 %copy-start = (f32[1024,1024]{1,0:T(8,128)}, f32[1024,1024]{1,0:T(8,128)S(1)}, u32[]{:S(2)}) copy-start(f32[1024,1024]{1,0:T(8,128)S(1)} %fusion.6.term_ref) | copy-start | bytes 12582916
  7.3 22.9 %collective-permute-start = (s16[528,1024]{1,0:T(8,128)(2,1)S(1)}, s16[528,1024]{1,0:T(8,128)(2,1)S(1)}, u32[]{:S(2)}, u32[]{:S(2)}) collective-permute-start(s16[528,1024]{1,0:T(8,128)(2,1)S(1)} %shard_map.55), channel_id=1, source_target_pairs={{0,1},{1,0},{2,3},{3,2},{4,5},{5,4},{6,7},{7,6},{8,9},{9,8},{10,11... | collective-permute-start | bytes 3244040 | tf_op jit(solution)/shard_map/ppermute | solution.py:54
  14.5 20.0 %collective-permute-start.1 = (s16[528,1024]{1,0:T(8,128)(2,1)S(1)}, s16[528,1024]{1,0:T(8,128)(2,1)S(1)}, u32[]{:S(2)}, u32[]{:S(2)}) collective-permute-start(s16[528,1024]{1,0:T(8,128)(2,1)S(1)} %shard_map.57), channel_id=1, source_target_pairs={{0,12},{1,13},{2,14},{3,15},{4,8},{5,9},{6,10},{7,11},{8,4},{9,5},... | collective-permute-start | bytes 3244040 | tf_op jit(solution)/shard_map/ppermute | solution.py:54
  23.4 15.2 %collective-permute-start.4 = (s16[528,1024]{1,0:T(8,128)(2,1)S(1)}, s16[528,1024]{1,0:T(8,128)(2,1)S(1)}, u32[]{:S(2)}, u32[]{:S(2)}) collective-permute-start(s16[528,1024]{1,0:T(8,128)(2,1)S(1)} %shard_map.59), channel_id=1, source_target_pairs={{0,1},{1,0},{2,3},{3,2},{4,5},{5,4},{6,7},{7,6},{8,9},{9,8},{10,11... | collective-permute-start | bytes 3244040 | tf_op jit(solution)/shard_map/ppermute | solution.py:54
  28.7 2.2 %copy-start.1 = (f32[1024,1024]{1,0:T(8,128)S(1)}, f32[1024,1024]{1,0:T(8,128)}, u32[]{:S(2)}) copy-start(f32[1024,1024]{1,0:T(8,128)} %copy-done) | copy-start | bytes 12582916
  29.7 16.6 %collective-permute-start.5 = (s16[528,1024]{1,0:T(8,128)(2,1)S(1)}, s16[528,1024]{1,0:T(8,128)(2,1)S(1)}, u32[]{:S(2)}, u32[]{:S(2)}) collective-permute-start(s16[528,1024]{1,0:T(8,128)(2,1)S(1)} %shard_map.61), channel_id=1, source_target_pairs={{0,12},{1,13},{2,14},{3,15},{4,8},{5,9},{6,10},{7,11},{8,4},{9,5},... | collective-permute-start | bytes 3244040 | tf_op jit(solution)/shard_map/ppermute | solution.py:54
  32.1 20.2 %collective-permute-start.2 = (s16[272,1024]{1,0:T(8,128)(2,1)S(1)}, s16[272,1024]{1,0:T(8,128)(2,1)S(1)}, u32[]{:S(2)}, u32[]{:S(2)}) collective-permute-start(s16[272,1024]{1,0:T(8,128)(2,1)S(1)} %get-tuple-element.36), channel_id=1, source_target_pairs={{0,12},{1,13},{2,14},{3,15},{4,8},{5,9},{6,10},{7,11},{8,4},{9,5},... | collective-permute-start | bytes 1671176 | tf_op jit(solution)/shard_map/ppermute | solution.py:54
  35.8 16.5 %collective-permute-start.6 = (s16[272,1024]{1,0:T(8,128)(2,1)S(1)}, s16[272,1024]{1,0:T(8,128)(2,1)S(1)}, u32[]{:S(2)}, u32[]{:S(2)}) collective-permute-start(s16[272,1024]{1,0:T(8,128)(2,1)S(1)} %get-tuple-element.42), channel_id=1, source_target_pairs={{0,1},{1,0},{2,3},{3,2},{4,5},{5,4},{6,7},{7,6},{8,9},{9,8},{10,11... | collective-permute-start | bytes 1671176 | tf_op jit(solution)/shard_map/ppermute | solution.py:54
  47.6 9.6 %collective-permute-start.7 = (s16[272,1024]{1,0:T(8,128)(2,1)S(1)}, s16[272,1024]{1,0:T(8,128)(2,1)S(1)}, u32[]{:S(2)}, u32[]{:S(2)}) collective-permute-start(s16[272,1024]{1,0:T(8,128)(2,1)S(1)} %get-tuple-element.47), channel_id=1, source_target_pairs={{0,1},{1,0},{2,3},{3,2},{4,5},{5,4},{6,7},{7,6},{8,9},{9,8},{10,11... | collective-permute-start | bytes 1671176 | tf_op jit(solution)/shard_map/ppermute | solution.py:54
  49.2 10.7 %collective-permute-start.8 = (s16[272,1024]{1,0:T(8,128)(2,1)S(1)}, s16[272,1024]{1,0:T(8,128)(2,1)S(1)}, u32[]{:S(2)}, u32[]{:S(2)}) collective-permute-start(s16[272,1024]{1,0:T(8,128)(2,1)S(1)} %get-tuple-element.44), channel_id=1, source_target_pairs={{0,12},{1,13},{2,14},{3,15},{4,8},{5,9},{6,10},{7,11},{8,4},{9,5},... | collective-permute-start | bytes 1671176 | tf_op jit(solution)/shard_map/ppermute | solution.py:54
  58.4 9.6 %collective-permute-start.9 = (s16[272,1024]{1,0:T(8,128)(2,1)S(1)}, s16[272,1024]{1,0:T(8,128)(2,1)S(1)}, u32[]{:S(2)}, u32[]{:S(2)}) collective-permute-start(s16[272,1024]{1,0:T(8,128)(2,1)S(1)} %get-tuple-element.48), channel_id=1, source_target_pairs={{0,4},{1,5},{2,6},{3,7},{4,0},{5,1},{6,2},{7,3},{8,12},{9,13},{10,... | collective-permute-start | bytes 1671176 | tf_op jit(solution)/shard_map/ppermute | solution.py:54
  61.1 11.1 %collective-permute-start.10 = (s16[272,1024]{1,0:T(8,128)(2,1)S(1)}, s16[272,1024]{1,0:T(8,128)(2,1)S(1)}, u32[]{:S(2)}, u32[]{:S(2)}) collective-permute-start(s16[272,1024]{1,0:T(8,128)(2,1)S(1)} %get-tuple-element.55), channel_id=1, source_target_pairs={{0,3},{1,2},{2,1},{3,0},{4,7},{5,6},{6,5},{7,4},{8,11},{9,10},{10,... | collective-permute-start | bytes 1671176 | tf_op jit(solution)/shard_map/ppermute | solution.py:54
  73.1 6.8 %collective-permute-start.11 = (s16[144,1024]{1,0:T(8,128)(2,1)S(1)}, s16[144,1024]{1,0:T(8,128)(2,1)S(1)}, u32[]{:S(2)}, u32[]{:S(2)}) collective-permute-start(s16[144,1024]{1,0:T(8,128)(2,1)S(1)} %get-tuple-element.58), channel_id=1, source_target_pairs={{0,4},{1,5},{2,6},{3,7},{4,0},{5,1},{6,2},{7,3},{8,12},{9,13},{10,... | collective-permute-start | bytes 884744 | tf_op jit(solution)/shard_map/ppermute | solution.py:54
  73.6 7.9 %collective-permute-start.12 = (s16[144,1024]{1,0:T(8,128)(2,1)S(1)}, s16[144,1024]{1,0:T(8,128)(2,1)S(1)}, u32[]{:S(2)}, u32[]{:S(2)}) collective-permute-start(s16[144,1024]{1,0:T(8,128)(2,1)S(1)} %get-tuple-element.53), channel_id=1, source_target_pairs={{0,3},{1,2},{2,1},{3,0},{4,7},{5,6},{6,5},{7,4},{8,11},{9,10},{10,... | collective-permute-start | bytes 884744 | tf_op jit(solution)/shard_map/ppermute | solution.py:54
  81.5 42.1 %copy-start.2 = (s32[8,8]{1,0:T(8,128)S(1)}, s32[8,8]{1,0:T(8,128)}, u32[]{:S(2)}) copy-start(s32[8,8]{1,0:T(8,128)} %flags_ref.1) | copy-start | bytes 772
  81.5 42.1 %copy-start.3 = (s32[8]{0:T(128)S(1)}, s32[8]{0:T(128)}, u32[]{:S(2)}) copy-start(s32[8]{0:T(128)} %order_ref.1) | copy-start | bytes 100
  125.1 1.3 collective-permute-start.13
